TPU v7x, 512 devices: a whole 4x4x16 slice. The times are simulated.
512 devices in a mesh: seq: 32 (over x, z_lo, core), head: 16 (over y, z_hi).
Axes of the slice: x: 4, y: 4, z: 16 (z_hi: 4, z_lo: 4; z = z_hi * 4 + z_lo), core: 2. Of those that a mesh axis runs over, the one named last changes fastest.
Arguments:
- features: bfloat16 [65536, 4096], P(('seq', 'head')), may hold values from -6 to 6
- dt_raw: bfloat16 [65536, 64], P(('seq', 'head')), may hold values from -3 to 3
- b_proj: bfloat16 [65536, 512], P(('seq', 'head')), may hold values from -2 to 2
- c_proj: bfloat16 [65536, 512], P(('seq', 'head')), may hold values from -2 to 2
- cotangent: bfloat16 [65536, 4096], P(('seq', 'head')), may hold values from -6 to 6
- starts: int32 [65536], P('seq'), may hold values from 0 to 1, as said below
- a_log: float32 [64], P('head'), may hold values from -14 to 0
- dt_bias: float32 [64], P('head'), may hold values from -6 to -1
- d_skip: float32 [64], P('head'), may hold values from 0.5 to 1.5
Outputs:
- mixed_out: bfloat16 [65536, 4096], P(('seq', 'head'))
- grad_features: bfloat16 [65536, 4096], P(('seq', 'head'))
- grad_dt: bfloat16 [65536, 64], P(('seq', 'head'))
- grad_b: bfloat16 [65536, 512], P(('seq', 'head'))
- grad_c: bfloat16 [65536, 512], P(('seq', 'head'))
Inputs may be any that keep to these rules, and one draw needn't show every extreme that they name: `starts`: 1 marks the first token of a document, 0 any other token; the window's first token is always 1.
All inputs are finite; a program needn't handle non-finite values.
Results may differ from a plain program's by a relative error of at most 0.0022.
Values may be sent and summed in bfloat16 or wider, within the bound.
No kernel may reach another device: no remote copies, remote signals or barrier semaphores. Data moves between devices by JAX's collectives and lax.ppermute only.
A program may use at most 128 MiB of HBM per device.

v0:
```python
import jax
import jax.numpy as jnp
from jax import lax
from jax.sharding import PartitionSpec as P

GROUPS = 4
HEADDIM = 64
STATE = 128
SPAN = 256


PRECISE = lax.Precision.HIGHEST


def carried_in(array, axis, combine, identity, reverse):
    devices, mine = (lax.axis_size(axis), lax.axis_index(axis))
    everything = jax.tree.map(lambda part: lax.all_gather(part, axis), array)
    start = jax.tree.map(
        lambda part, zero: jnp.broadcast_to(jnp.asarray(zero, part.dtype), part.shape),
        array,
        identity,
    )

    def hop(k, before):
        at = devices - 1 - k if reverse else k
        reached = at > mine if reverse else at < mine
        new = combine(before, jax.tree.map(lambda part: part[at], everything))
        return jax.tree.map(lambda a, b: jnp.where(reached, a, b), new, before)

    return lax.fori_loop(0, devices, hop, start)


def span_step(state, pieces):
    scaled, running, b_vals, c_vals, doc_count = pieces
    length = doc_count.shape[0]
    places = jnp.arange(length)
    same_doc = (doc_count[:, None] == doc_count[None, :]) & (places[:, None] >= places[None, :])
    scores = jnp.einsum("tgn,sgn->gts", c_vals, b_vals, precision=PRECISE)
    run_heads = jnp.transpose(running, (1, 2, 0))
    spread = run_heads[:, :, :, None] - run_heads[:, :, None, :]
    decay = jnp.exp(jnp.where(same_doc[None, None], spread, -1e30))
    weights = scores[:, None] * decay
    inner = jnp.einsum("gkts,sgkp->tgkp", weights, scaled, precision=PRECISE)
    reach = jnp.exp(running) * (doc_count == 0)[:, None, None]
    carried = jnp.einsum("tgn,gkpn->tgkp", c_vals, state, precision=PRECISE) * reach[..., None]
    last_doc = doc_count[-1]
    tail = jnp.exp(running[-1][None] - running) * (doc_count == last_doc)[:, None, None]
    keep = jnp.exp(running[-1]) * (last_doc == 0)
    added = jnp.einsum("sgkp,sgn->gkpn", scaled * tail[..., None], b_vals, precision=PRECISE)
    return (keep[..., None, None] * state + added, inner + carried)


def compose(earlier, later):
    return (earlier[0] * later[0], later[0][..., None, None] * earlier[1] + later[1])


def per_device(features, dt_raw, b_proj, c_proj, cotangent, starts, a_log, dt_bias, d_skip):
    parts = lax.axis_size("head")
    tok_rows = features.shape[0]
    heads = dt_raw.shape[1]
    per_dev = heads // parts
    repeat = parts // GROUPS
    feat_three = features.reshape(tok_rows, parts, per_dev * HEADDIM)
    rate_three = dt_raw.reshape(tok_rows, parts, per_dev)
    b_three = jnp.repeat(b_proj.reshape(tok_rows, GROUPS, STATE), repeat, axis=1)
    c_three = jnp.repeat(c_proj.reshape(tok_rows, GROUPS, STATE), repeat, axis=1)
    cot_three = cotangent.reshape(tok_rows, parts, per_dev * HEADDIM)
    feat_seg, rate_seg, b_seg, c_seg, cot_seg = (
        lax.all_to_all(feat_three, "head", split_axis=1, concat_axis=0, tiled=True),
        lax.all_to_all(rate_three, "head", split_axis=1, concat_axis=0, tiled=True),
        lax.all_to_all(b_three, "head", split_axis=1, concat_axis=0, tiled=True),
        lax.all_to_all(c_three, "head", split_axis=1, concat_axis=0, tiled=True),
        lax.all_to_all(cot_three, "head", split_axis=1, concat_axis=0, tiled=True),
    )
    seg_len = feat_seg.shape[0]
    blocks = seg_len // SPAN
    doc_count = jnp.cumsum(starts.reshape(blocks, SPAN), axis=1)
    open_rows = jnp.cumsum(starts) == 0
    no_start = jnp.sum(starts) == 0
    decay_head = -jnp.exp(a_log)

    def local_part(feat, rates, b_vals, c_vals):
        sizes = jax.nn.softplus(rates + dt_bias)
        log_rate = sizes * decay_head
        scaled = feat * sizes[..., None]
        running = jnp.cumsum(log_rate.reshape(blocks, SPAN, 1, per_dev), axis=1)
        start_state = jnp.zeros((1, per_dev, HEADDIM, STATE), jnp.float32)
        pieces = (
            scaled.reshape(blocks, SPAN, 1, per_dev, HEADDIM),
            running,
            b_vals.reshape(blocks, SPAN, 1, STATE),
            c_vals.reshape(blocks, SPAN, 1, STATE),
            doc_count,
        )
        end_state, outputs = lax.scan(jax.checkpoint(span_step), start_state, pieces)
        through = jnp.exp(jnp.sum(log_rate, axis=0)) * no_start
        return (outputs.reshape(seg_len, 1, per_dev, HEADDIM), through, end_state)

    def entry_part(feat, rates, c_vals, entering):
        sizes = jax.nn.softplus(rates + dt_bias)
        log_rate = sizes * decay_head
        reach = jnp.exp(jnp.cumsum(log_rate, axis=0)) * open_rows[:, None, None]
        carried = jnp.einsum("tgn,gkpn->tgkp", c_vals, entering, precision=PRECISE)
        return carried * reach[..., None] + feat * d_skip[:, None]

    feat_full = feat_seg.astype(jnp.float32).reshape(seg_len, 1, per_dev, HEADDIM)
    rate_full = rate_seg.astype(jnp.float32)
    b_full = b_seg.astype(jnp.float32)
    c_full = c_seg.astype(jnp.float32)
    (inner, through, final_state), pull_local = jax.vjp(
        local_part, feat_full, rate_full, b_full, c_full
    )
    forward_pair = carried_in(
        (through, final_state),
        "seq",
        compose,
        (jnp.ones_like(through), jnp.zeros_like(final_state)),
        False,
    )
    entering = forward_pair[1]
    outer, pull_entry = jax.vjp(entry_part, feat_full, rate_full, c_full, entering)
    mixed = (inner + outer).astype(jnp.bfloat16).reshape(seg_len, 1, per_dev * HEADDIM)
    cot_full = cot_seg.astype(jnp.float32).reshape(seg_len, 1, per_dev, HEADDIM)
    feat_two, rate_two, c_two, grad_here = pull_entry(cot_full)
    backward_pair = carried_in(
        (through, grad_here),
        "seq",
        compose,
        (jnp.ones_like(through), jnp.zeros_like(grad_here)),
        True,
    )
    grad_next = backward_pair[1]
    grad_through = jnp.sum(grad_next * entering, axis=(2, 3))
    feat_one, rate_one, b_one, c_one = pull_local((cot_full, grad_through, grad_next))
    grad_feat = (feat_one + feat_two).astype(jnp.bfloat16).reshape(seg_len, 1, per_dev * HEADDIM)
    grad_rate = (rate_one + rate_two).astype(jnp.bfloat16)
    mixed_tok, feat_tok, rate_tok = (
        lax.all_to_all(mixed, "head", split_axis=0, concat_axis=1, tiled=True),
        lax.all_to_all(grad_feat, "head", split_axis=0, concat_axis=1, tiled=True),
        lax.all_to_all(grad_rate, "head", split_axis=0, concat_axis=1, tiled=True),
    )
    b_tok, c_tok = (
        lax.all_to_all(b_one, "head", split_axis=0, concat_axis=1, tiled=True),
        lax.all_to_all(c_one + c_two, "head", split_axis=0, concat_axis=1, tiled=True),
    )
    grad_b = (
        b_tok.reshape(tok_rows, GROUPS, repeat, STATE).sum(axis=2).reshape(tok_rows, GROUPS * STATE)
    )
    grad_c = (
        c_tok.reshape(tok_rows, GROUPS, repeat, STATE).sum(axis=2).reshape(tok_rows, GROUPS * STATE)
    )
    return (
        mixed_tok.reshape(tok_rows, heads * HEADDIM),
        feat_tok.reshape(tok_rows, heads * HEADDIM),
        rate_tok.reshape(tok_rows, heads),
        grad_b.astype(jnp.bfloat16),
        grad_c.astype(jnp.bfloat16),
    )


def solution(mesh):
    in_specs = (
        P(("seq", "head"), None),
        P(("seq", "head"), None),
        P(("seq", "head"), None),
        P(("seq", "head"), None),
        P(("seq", "head"), None),
        P("seq"),
        P("head"),
        P("head"),
        P("head"),
    )
    out_specs = (
        P(("seq", "head"), None),
        P(("seq", "head"), None),
        P(("seq", "head"), None),
        P(("seq", "head"), None),
        P(("seq", "head"), None),
    )
    return jax.shard_map(
        per_device, mesh=mesh, in_specs=in_specs, out_specs=out_specs, check_vma=False
    )
```

profile of v0, /device:TPU:98, one launch (start us, length us, event | category | flops | bytes accessed | tf_op | source)
XLA Modules:
  0.0 1102.1 jit_solution(6593680507735033292)
XLA Ops:
  7.2 15.3 %all-to-all-start = ((bf16[128,16,4]{0,2,1:T(4,128)(2,1)}), bf16[128,16,4]{0,2,1:T(4,128)(2,1)S(1)}, u32[]{:S(2)}, u32[]{:S(2)}) async-start(bf16[128,16,4]{0,2,1:T(4,128)(2,1)} %bitcast.684), calls=%async_computation | async-start | bytes 32768 | tf_op jit(solution)/shard_map/all_to_all | solution.py:70
  22.5 14.8 %all-to-all-done = bf16[128,16,4]{0,2,1:T(4,128)(2,1)S(1)} async-done(((bf16[128,16,4]{0,2,1:T(4,128)(2,1)}), bf16[128,16,4]{0,2,1:T(4,128)(2,1)S(1)}, u32[]{:S(2)}, u32[]{:S(2)}) %all-to-all-start) | async-done | bytes 16416 | tf_op jit(solution)/shard_map/all_to_all | solution.py:70
  38.2 3.6 all-to-all-start.2
  42.7 32.1 %all-to-all-done.2 = bf16[128,16,128]{2,0,1:T(8,128)(2,1)S(1)} async-done(((bf16[128,16,128]{2,0,1:T(8,128)(2,1)}), bf16[128,16,128]{2,0,1:T(8,128)(2,1)S(1)}, u32[]{:S(2)}, u32[]{:S(2)}) %all-to-all-start.2) | async-done | bytes 524320 | tf_op jit(solution)/shard_map/all_to_all | solution.py:71
  75.7 4.2 all-to-all-start.3
  81.3 23.1 %all-to-all-done.3 = bf16[128,16,128]{2,0,1:T(8,128)(2,1)S(1)} async-done(((bf16[128,16,128]{2,0,1:T(8,128)(2,1)}), bf16[128,16,128]{2,0,1:T(8,128)(2,1)S(1)}, u32[]{:S(2)}, u32[]{:S(2)}) %all-to-all-start.3) | async-done | bytes 524320 | tf_op jit(solution)/shard_map/all_to_all | solution.py:72
  104.3 11.2 %all-to-all-start.1 = ((bf16[128,16,256]{0,2,1:T(8,128)(2,1)}), bf16[128,16,256]{0,2,1:T(8,128)(2,1)S(1)}, u32[]{:S(2)}, u32[]{:S(2)}) async-start(bf16[128,16,256]{0,2,1:T(8,128)(2,1)} %bitcast.62), calls=%async_computation.1 | async-start | bytes 2097152 | tf_op jit(solution)/shard_map/all_to_all | solution.py:69
  123.0 20.2 %all-to-all-done.1 = bf16[128,16,256]{0,2,1:T(8,128)(2,1)S(1)} async-done(((bf16[128,16,256]{0,2,1:T(8,128)(2,1)}), bf16[128,16,256]{0,2,1:T(8,128)(2,1)S(1)}, u32[]{:S(2)}, u32[]{:S(2)}) %all-to-all-start.1) | async-done | bytes 1048608 | tf_op jit(solution)/shard_map/all_to_all | solution.py:69
  152.7 159.3 %while.69 = (s32[]{:T(128)}, f32[1,4,64,128]{3,2,1,0:T(8,128)S(1)}, f32[8,256,1,4,64]{1,0,4,3,2:T(8,128)}, f32[8,1,4,64,128]{4,3,2,1,0:T(8,128)}, f32[8,256,1,4]...) while((s32[]{:T(128)}, f32[1,4,64,128]{3,2,1,0:T(8,128)S(1)}, ...), condition=%wide.region_5.7_spmd.clone, body=%wide.region_4.6_spmd.clone.sunk | while | flops 504664064 | bytes 4242234 | solution.py:95
  165.6 7.0 dynamic_update_slice.67
  185.6 7.0 dynamic_update_slice.67
  205.5 7.0 dynamic_update_slice.67
  225.4 7.0 dynamic_update_slice.67
  245.3 7.0 dynamic_update_slice.67
  265.2 7.0 dynamic_update_slice.67
  285.1 7.0 dynamic_update_slice.67
  305.0 7.0 dynamic_update_slice.67
  315.1 26.5 %all-to-all-start.5 = ((bf16[128,16,256]{0,2,1:T(8,128)(2,1)}), bf16[128,16,256]{0,2,1:T(8,128)(2,1)}, u32[]{:S(2)}, u32[]{:S(2)}) async-start(bf16[128,16,256]{0,2,1:T(8,128)(2,1)} %bitcast.648), calls=%async_computation.5 | async-start | bytes 2097152 | tf_op jit(solution)/shard_map/all_to_all | solution.py:73
  347.8 78.2 %all-reduce.2 = f32[128]{0:T(128)S(1)} all-reduce(f32[128]{0:T(128)S(1)} %multiply_dynamic-update-slice_fusion), channel_id=2, replica_groups=mesh['seq'=32,'head'=16] {'seq'}, use_global_device_ids=true, to_apply=%add.2 | all-reduce | flops 128 | bytes 1024
  427.7 2.9 convert_bitcast_fusion.1
  434.9 2.9 reshape.1395
  442.3 33.1 %while.70 = (s32[]{:T(128)}, f32[1,4,64,128]{3,2,1,0:T(8,128)S(1)}, s32[]{:T(128)}, f32[32,1,4]{2,1,0:T(1,128)S(1)}, f32[32,1,4,64,128]{4,3,2,1,0:T(8,128)}, /*index=5*/s32[]{:T(128)}, s32[]{:T(128)}) while((s32[]{:T(128)}, f32[1,4,64,128]{3,2,1,0:T(8,128)S(1)}, s32[]{:T(128)}, f32[32,1,4]{2,1,0:T(1,128)S(1)}, ...), condition=%wide.region_9.11_spmd.clone, body=%wide.region_8.10_spmd.clone.sunk | while | flops 131076 | bytes 393377 | solution.py:30
  475.4 4.6 multiply_reduce_fusion.3
  480.1 5.0 reduce-window.59
  486.4 43.3 %all-gather.8.cloned.1.call-done = f32[128,64,128]{2,1,0:T(8,128)} async-done(((f32[4,64,128]{2,1,0:T(8,128)}), f32[128,64,128]{2,1,0:T(8,128)}) %all-gather.8.cloned.1.call-update) | async-done | bytes 4194320 | tf_op jit(solution)/shard_map/all_gather | solution.py:17
  529.7 33.4 %while.71 = (s32[]{:T(128)}, f32[1,4,64,128]{3,2,1,0:T(8,128)S(1)}, s32[]{:T(128)}, f32[32,1,4]{2,1,0:T(1,128)S(1)}, f32[32,1,4,64,128]{4,3,2,1,0:T(8,128)}, /*index=5*/s32[]{:T(128)}, s32[]{:T(128)}, s32[]{:T(128)}, s32[]{:T(128)}) while((s32[]{:T(128)}, f32[1,4,64,128]{3,2,1,0:T(8,128)S(1)}, s32[]{:T(128)}, ...), condition=%wide.region_15.17_spmd.clone, body=%wide.region_14.16_spmd.clone.sunk | while | flops 131080 | bytes 393439 | solution.py:30
  567.4 242.0 %while.68 = (s32[]{:T(128)}, f32[1,4,64,128]{3,2,1,0:T(8,128)S(1)}, f32[8,256,1,4,64]{1,0,4,3,2:T(8,128)}, f32[8,256,1,4]{1,3,2,0:T(4,128)}, f32[8,256,1,128]{3,...) while((s32[]{:T(128)}, f32[1,4,64,128]{3,2,1,0:T(8,128)S(1)}, ...), condition=%wide.region_24.26_spmd, body=%wide.region_16.25_spmd.sunk | while | flops 1212038144 | bytes 12756147 | solution.py:95
  586.2 7.0 dynamic_update_slice.65
  616.4 7.0 dynamic_update_slice.65
  646.6 7.0 dynamic_update_slice.65
  676.8 7.0 dynamic_update_slice.65
  707.0 7.0 dynamic_update_slice.65
  737.2 7.0 dynamic_update_slice.65
  767.4 7.0 dynamic_update_slice.65
  797.6 7.0 dynamic_update_slice.65
  810.1 9.9 reduce-window.55
  831.1 13.3 %all-to-all-start.7 = ((bf16[16,2,256]{2,1,0:T(2,128)(2,1)}), bf16[16,2,256]{2,1,0:T(2,128)(2,1)S(1)}, u32[]{:S(2)}, u32[]{:S(2)}) async-start(bf16[16,2,256]{2,1,0:T(2,128)(2,1)} %reshape.1436), calls=%async_computation.7 | async-start | bytes 32768 | tf_op jit(solution)/shard_map/all_to_all | solution.py:140
  849.2 10.1 all-to-all-done.7
  859.3 4.5 all-to-all-start.4
  868.2 2.9 fusion.98
  871.1 3.3 reduce.74
  878.9 34.7 %all-to-all-done.4 = bf16[16,2,16384]{2,1,0:T(2,128)(2,1)S(1)} async-done(((bf16[16,2,16384]{2,1,0:T(2,128)(2,1)}), bf16[16,2,16384]{2,1,0:T(2,128)(2,1)S(1)}, u32[]{:S(2)}, u32[]{:S(2)}) %all-to-all-start.4) | async-done | bytes 1048608 | tf_op jit(solution)/shard_map/all_to_all | solution.py:138
  913.7 68.5 %all_to_all.126 = bf16[16,2,16384]{2,1,0:T(2,128)(2,1)} all-to-all(bf16[16,2,16384]{2,1,0:T(2,128)(2,1)} %reshape.1434), channel_id=1, replica_groups=mesh['seq'=32,'head'=16] {'head'}, dimensions={0} | all-to-all | bytes 2097152 | tf_op jit(solution)/shard_map/all_to_all | solution.py:139
  982.2 11.1 %all-to-all-start.8 = ((f32[2048,1,128]{2,1,0:T(1,128)}), f32[2048,1,128]{2,1,0:T(1,128)}, u32[]{:S(2)}, u32[]{:S(2)}) async-start(f32[2048,1,128]{2,1,0:T(1,128)} %bitcast.649), calls=%async_computation.8 | async-start | bytes 2097152 | tf_op jit(solution)/shard_map/all_to_all | solution.py:143
  993.3 5.7 fusion.96
  999.0 40.1 %all-to-all-done.8 = f32[2048,1,128]{2,1,0:T(1,128)} async-done(((f32[2048,1,128]{2,1,0:T(1,128)}), f32[2048,1,128]{2,1,0:T(1,128)}, u32[]{:S(2)}, u32[]{:S(2)}) %all-to-all-start.8) | async-done | bytes 1048608 | tf_op jit(solution)/shard_map/all_to_all | solution.py:143
  1039.1 5.2 all-to-all-start.9
  1057.6 35.2 %all-to-all-done.9 = f32[2048,1,128]{2,1,0:T(1,128)} async-done(((f32[2048,1,128]{2,1,0:T(1,128)}), f32[2048,1,128]{2,1,0:T(1,128)}, u32[]{:S(2)}, u32[]{:S(2)}) %all-to-all-start.9) | async-done | bytes 1048608 | tf_op jit(solution)/shard_map/all_to_all | solution.py:144
  (730 shorter events, 427.7 us)
Async XLA Ops:
  7.2 15.3 %copy-start = (bf16[128,512]{1,0:T(8,128)(2,1)S(1)}, bf16[128,512]{1,0:T(8,128)(2,1)}, u32[]{:S(2)}) copy-start(bf16[128,512]{1,0:T(8,128)(2,1)} %param.20) | copy-start | bytes 393220
  7.2 72.7 %copy-start.13 = (bf16[128,4096]{1,0:T(8,128)(2,1)S(1)}, bf16[128,4096]{1,0:T(8,128)(2,1)}, u32[]{:S(2)}) copy-start(bf16[128,4096]{1,0:T(8,128)(2,1)} %param.18) | copy-start | bytes 3145732
  7.2 30.1 %all-to-all-start = ((bf16[128,16,4]{0,2,1:T(4,128)(2,1)}), bf16[128,16,4]{0,2,1:T(4,128)(2,1)S(1)}, u32[]{:S(2)}, u32[]{:S(2)}) async-start(bf16[128,16,4]{0,2,1:T(4,128)(2,1)} %bitcast.684), calls=%async_computation | async-start | bytes 32768 | tf_op jit(solution)/shard_map/all_to_all | solution.py:70
  37.3 79.9 %copy-start.19 = (bf16[128,16,4]{0,2,1:T(4,128)(2,1)}, bf16[128,16,4]{0,2,1:T(4,128)(2,1)S(1)}, u32[]{:S(2)}) copy-start(bf16[128,16,4]{0,2,1:T(4,128)(2,1)S(1)} %all-to-all-done) | copy-start | bytes 49156
  38.2 36.6 %all-to-all-start.2 = ((bf16[128,16,128]{2,0,1:T(8,128)(2,1)}), bf16[128,16,128]{2,0,1:T(8,128)(2,1)S(1)}, u32[]{:S(2)}, u32[]{:S(2)}) async-start(bf16[128,16,128]{2,0,1:T(8,128)(2,1)} %bitcast.65), calls=%async_computation.2 | async-start | bytes 1048576 | tf_op jit(solution)/shard_map/all_to_all | solution.py:71
  75.7 28.6 %all-to-all-start.3 = ((bf16[128,16,128]{2,0,1:T(8,128)(2,1)}), bf16[128,16,128]{2,0,1:T(8,128)(2,1)S(1)}, u32[]{:S(2)}, u32[]{:S(2)}) async-start(bf16[128,16,128]{2,0,1:T(8,128)(2,1)} %bitcast.69), calls=%async_computation.3 | async-start | bytes 1048576 | tf_op jit(solution)/shard_map/all_to_all | solution.py:72
  79.9 35.7 %copy-start.23 = (s32[2048]{0:T(1024)S(1)}, s32[2048]{0:T(1024)}, u32[]{:S(2)}) copy-start(s32[2048]{0:T(1024)} %param.23) | copy-start | bytes 24580
  79.9 36.5 %copy-start.32 = (f32[4]{0:T(128)S(1)}, f32[4]{0:T(128)}, u32[]{:S(2)}) copy-start(f32[4]{0:T(128)} %param.24) | copy-start | bytes 52
  79.9 37.2 %copy-start.28 = (f32[4]{0:T(128)S(1)}, f32[4]{0:T(128)}, u32[]{:S(2)}) copy-start(f32[4]{0:T(128)} %param.25) | copy-start | bytes 52
  104.3 38.9 %all-to-all-start.1 = ((bf16[128,16,256]{0,2,1:T(8,128)(2,1)}), bf16[128,16,256]{0,2,1:T(8,128)(2,1)S(1)}, u32[]{:S(2)}, u32[]{:S(2)}) async-start(bf16[128,16,256]{0,2,1:T(8,128)(2,1)} %bitcast.62), calls=%async_computation.1 | async-start | bytes 2097152 | tf_op jit(solution)/shard_map/all_to_all | solution.py:69
  115.5 326.7 %all-gather.6.cloned.1.call-start = ((), (), s32[]{:S(2)}) async-start(), calls=%async_computation.10 | async-start | bytes 4325376 | tf_op jit(solution)/shard_map/all_gather | solution.py:17
  117.4 26.0 %copy-start.16 = (f32[2048,1,4]{0,2,1:T(4,128)}, f32[2048,1,4]{0,2,1:T(4,128)S(1)}, u32[]{:S(2)}) copy-start(f32[2048,1,4]{0,2,1:T(4,128)S(1)} %get-tuple-element.939) | copy-start | bytes 98308
  117.4 230.3 %copy-start.26 = (f32[4]{0:T(128)}, f32[4]{0:T(128)S(1)}, u32[]{:S(2)}) copy-start(f32[4]{0:T(128)S(1)} %get-tuple-element.937) | copy-start | bytes 52
  312.7 113.5 %copy-start.4 = (f32[16,128,1,256]{1,0,3,2:T(8,128)S(1)}, f32[16,128,1,256]{1,0,3,2:T(8,128)}, u32[]{:S(2)}) copy-start(f32[16,128,1,256]{1,0,3,2:T(8,128)} %copy.217) | copy-start | bytes 6291460
  315.1 112.6 %all-to-all-start.5 = ((bf16[128,16,256]{0,2,1:T(8,128)(2,1)}), bf16[128,16,256]{0,2,1:T(8,128)(2,1)}, u32[]{:S(2)}, u32[]{:S(2)}) async-start(bf16[128,16,256]{0,2,1:T(8,128)(2,1)} %bitcast.648), calls=%async_computation.5 | async-start | bytes 2097152 | tf_op jit(solution)/shard_map/all_to_all | solution.py:73
  341.7 188.0 %all-gather.8.cloned.1.call-start = ((), (), s32[]{:S(2)}) async-start(), calls=%async_computation.11 | async-start | bytes 4325376 | tf_op jit(solution)/shard_map/all_gather | solution.py:17
  426.2 49.2 %copy-start.14 = (f32[2048,4]{0,1:T(4,128)}, f32[2048,4]{0,1:T(4,128)S(1)}, u32[]{:S(2)}) copy-start(f32[2048,4]{0,1:T(4,128)S(1)} %fusion.120) | copy-start | bytes 98308
  440.4 35.0 %copy-start.30 = (f32[4]{0:T(128)S(1)}, f32[4]{0:T(128)}, u32[]{:S(2)}) copy-start(f32[4]{0:T(128)} %param.26) | copy-start | bytes 52
  475.4 4.7 copy-start.5
  563.0 4.3 copy-start.9
  574.3 4.4 copy-start.8
  574.4 4.3 copy-start.12
  604.5 4.4 copy-start.8
  604.6 4.3 copy-start.12
  634.7 4.4 copy-start.8
  634.8 4.3 copy-start.12
  664.9 4.4 copy-start.8
  665.0 4.3 copy-start.12
  695.1 4.4 copy-start.8
  695.2 4.3 copy-start.12
  725.2 4.4 copy-start.8
  725.4 4.3 copy-start.12
  755.4 4.4 copy-start.8
  755.6 4.3 copy-start.12
  785.6 4.4 copy-start.8
  785.7 4.3 copy-start.12
  823.4 3.0 copy-start.17
  823.4 3.0 copy-start.20
  823.4 21.1 %copy-start.10 = (bf16[2048,1,4,64]{0,3,2,1:T(8,128)(2,1)S(1)}, bf16[2048,1,4,64]{0,3,2,1:T(8,128)(2,1)}, u32[]{:S(2)}) copy-start(bf16[2048,1,4,64]{0,3,2,1:T(8,128)(2,1)} %get-tuple-element.958) | copy-start | bytes 3145732
  831.1 28.1 %all-to-all-start.7 = ((bf16[16,2,256]{2,1,0:T(2,128)(2,1)}), bf16[16,2,256]{2,1,0:T(2,128)(2,1)S(1)}, u32[]{:S(2)}, u32[]{:S(2)}) async-start(bf16[16,2,256]{2,1,0:T(2,128)(2,1)} %reshape.1436), calls=%async_computation.7 | async-start | bytes 32768 | tf_op jit(solution)/shard_map/all_to_all | solution.py:140
  848.1 15.7 %copy-start.31 = (f32[4]{0:T(128)S(1)}, f32[4]{0:T(128)}, u32[]{:S(2)}) copy-start(f32[4]{0:T(128)} %param.26) | copy-start | bytes 52
  859.3 54.4 %all-to-all-start.4 = ((bf16[16,2,16384]{2,1,0:T(2,128)(2,1)}), bf16[16,2,16384]{2,1,0:T(2,128)(2,1)S(1)}, u32[]{:S(2)}, u32[]{:S(2)}) async-start(bf16[16,2,16384]{2,1,0:T(2,128)(2,1)} %reshape.1432), calls=%async_computation.4 | async-start | bytes 2097152 | tf_op jit(solution)/shard_map/all_to_all | solution.py:138
  878.9 114.4 %copy-start.6 = (f32[1,4,64,128]{3,2,1,0:T(8,128)S(1)}, f32[1,4,64,128]{3,2,1,0:T(8,128)}, u32[]{:S(2)}) copy-start(f32[1,4,64,128]{3,2,1,0:T(8,128)} %copy-done.5) | copy-start | bytes 393220
  878.9 114.4 %copy-start.15 = (f32[2048,4]{0,1:T(4,128)S(1)}, f32[2048,4]{0,1:T(4,128)}, u32[]{:S(2)}) copy-start(f32[2048,4]{0,1:T(4,128)} %copy-done.14) | copy-start | bytes 98308
  982.2 56.9 %all-to-all-start.8 = ((f32[2048,1,128]{2,1,0:T(1,128)}), f32[2048,1,128]{2,1,0:T(1,128)}, u32[]{:S(2)}, u32[]{:S(2)}) async-start(f32[2048,1,128]{2,1,0:T(1,128)} %bitcast.649), calls=%async_computation.8 | async-start | bytes 2097152 | tf_op jit(solution)/shard_map/all_to_all | solution.py:143
  1039.1 53.7 %all-to-all-start.9 = ((f32[2048,1,128]{2,1,0:T(1,128)}), f32[2048,1,128]{2,1,0:T(1,128)}, u32[]{:S(2)}, u32[]{:S(2)}) async-start(f32[2048,1,128]{2,1,0:T(1,128)} %bitcast.652), calls=%async_computation.9 | async-start | bytes 2097152 | tf_op jit(solution)/shard_map/all_to_all | solution.py:144
  1049.2 3.0 copy-start.11
  1054.1 40.9 %copy-start.1 = (bf16[128,512]{1,0:T(8,128)(2,1)S(1)}, bf16[128,512]{1,0:T(8,128)(2,1)}, u32[]{:S(2)}) copy-start(bf16[128,512]{1,0:T(8,128)(2,1)} %param.20) | copy-start | bytes 393220
  (24 other events, 53.9 us)
Sparse Core Ops, SparseCore 0:
  312.8 109.1 all-gather.5
  442.4 87.2 all-gather.7
where the time goes:
time: 1120 us; the launch traced here: 1100 us
  local copies, waits for them, and re-layouts  276 us (25%)
  waiting for transfers between devices  254 us (23%)
  other arithmetic  154 us (14%)
  blocking collectives  147 us (13%)
  matrix products  146 us (13%)
  starting transfers between devices  95.1 us (8%)
  between operations  16.4 us (1%)
  loops' own time  14.2 us (1%)
    dynamic_update_slice x48, local copies, waits for them, and re-layouts, local_part(): lax.scan(jax.checkpoint(span_step), start_state, pieces)  122 us
    unnamed x1, blocking collectives  78.2 us
    all_to_all x1, blocking collectives, per_device(): lax.all_to_all(grad_feat, 'head', split_axis=0, concat_axis=1, tiled=True)  68.5 us
    select_n x64, other arithmetic, hop(): return jax.tree.map(lambda a, b: jnp.where(reached, a, b), new, before)  63.6 us
    dot_general x24, matrix products, span_step(): inner = jnp.einsum('gkts,sgkp->tgkp', weights, scaled, precision=PRECISE)  51.8 us
    all_gather x2, waiting for transfers between devices, carried_in(): everything = jax.tree.map(lambda part: lax.all_gather(part, axis), array)  43.3 us
    all_to_all x1, waiting for transfers between devices, per_device(): lax.all_to_all(b_one, 'head', split_axis=0, concat_axis=1, tiled=True)  40.1 us
    all_to_all x1, waiting for transfers between devices, per_device(): lax.all_to_all(c_one + c_two, 'head', split_axis=0, concat_axis=1, tiled=...  35.2 us
  transfers between devices with their start and end apart: 11, of which 9 were waited for; matrix products, arithmetic and copies ran while one was open for 10% of the time, Pallas kernels for 0%

commit v1 on v0

v1 whole, which is shorter than its diff:
```python
import functools

import jax
import jax.numpy as jnp
from jax import lax
from jax.experimental import pallas as pl
from jax.experimental.pallas import tpu as pltpu
from jax.sharding import PartitionSpec as P

GROUPS = 4
HEADDIM = 64
STATE = 128
ROWS = STATE + 8
TOP = 13.0
CUT = -65000.0
F32 = jnp.float32
BF16 = jnp.bfloat16
PRECISE = lax.Precision.HIGHEST
PARAMS = pltpu.CompilerParams(vmem_limit_bytes=40 * 1024 * 1024)


def iota(shape, axis):
    return lax.broadcasted_iota(jnp.int32, shape, axis)


def split(value):
    high = value.astype(BF16)
    return high, (value - high.astype(F32)).astype(BF16)


def dot(a, b, dims=((1,), (0,)), precision=None):
    return lax.dot_general(a, b, (dims, ((), ())), precision=precision, preferred_element_type=F32)


def spread_map(heads, dtype):
    shape = (heads, heads * HEADDIM)
    return (iota(shape, 0) == iota(shape, 1) // HEADDIM).astype(dtype)


def widen(value):
    both = jnp.concatenate(split(value), axis=1)
    spread = spread_map(value.shape[1], BF16)
    return dot(both, jnp.concatenate([spread, spread], axis=0))


def head_sums(value):
    heads = value.shape[1] // HEADDIM
    shape = (heads * HEADDIM, heads)
    fold = (iota(shape, 0) // HEADDIM == iota(shape, 1)).astype(BF16)
    high, low = split(value)
    return dot(high, fold) + dot(low, fold)


def exponent_of(block):
    top = jnp.max(jnp.max(jnp.abs(block), axis=0, keepdims=True), axis=1, keepdims=True)
    return jnp.clip(jnp.floor(jnp.log(jnp.maximum(top, 1e-30)) * 1.4426950408889634), -90.0, 40.0)


def prep_kernel(dt_ref, par_ref, st_ref, size_ref, sig_ref, run_ref, runt_ref, reach_ref, tail_ref, bias_ref, edge_ref):
    tokens, heads = dt_ref.shape
    per = heads // GROUPS
    par = par_ref[...]
    a_log, dt_bias = par[0:1], par[1:2]
    decay = -jnp.exp(a_log)
    value = dt_ref[...].astype(F32) + dt_bias
    sizes = jnp.maximum(value, 0.0) + jnp.log1p(jnp.exp(-jnp.abs(value)))
    sigmoid = 1.0 / (1.0 + jnp.exp(-value))
    shape = (tokens, tokens)
    lower = (iota(shape, 0) >= iota(shape, 1)).astype(F32)
    upper = (iota(shape, 0) <= iota(shape, 1)).astype(F32)
    running = dot(lower, sizes * decay, precision=PRECISE)
    marks = st_ref[...]
    doc_row = dot(marks, upper)[0:1]
    doc_col = dot(lower, marks, ((1,), (1,)))[:, 0:1]
    doc_last = doc_row[:, tokens - 1 :]
    last = running[tokens - 1 :]
    reach = jnp.where(doc_col == 0.0, jnp.exp(running), 0.0)
    tail = jnp.where(doc_col == doc_last, jnp.exp(last - running), 0.0) * sizes
    linked = (doc_col == doc_row) & (iota(shape, 0) >= iota(shape, 1))
    bias_ref[...] = jnp.where(linked, 0.0, -1e30)
    turned = (running - jnp.log(sizes)).T
    through = jnp.where(doc_last == 0.0, last * 128.0, CUT)
    high = through.astype(BF16).astype(F32)
    mid = (through - high).astype(BF16).astype(F32)
    low = (through - high - mid).astype(BF16).astype(F32)
    keep = jnp.exp((high + mid + low) * (1.0 / 128.0))
    edge = jnp.concatenate([high, mid, low, jnp.zeros_like(keep), keep, decay, decay, decay], axis=0)
    for g in range(GROUPS):
        mine = slice(g * per, (g + 1) * per)
        size_ref[g] = sizes[:, mine]
        sig_ref[g] = sigmoid[:, mine]
        run_ref[g] = running[:, mine]
        runt_ref[g] = turned[mine]
        reach_ref[g] = reach[:, mine]
        tail_ref[g] = tail[:, mine]
        edge_ref[g] = edge[:, mine]


def prep(dt_raw, params, marks):
    tokens, heads = dt_raw.shape
    per = heads // GROUPS
    token_head = jax.ShapeDtypeStruct((GROUPS, tokens, per), F32)
    return pl.pallas_call(
        prep_kernel,
        out_shape=[
            token_head,
            token_head,
            token_head,
            jax.ShapeDtypeStruct((GROUPS, per, tokens), F32),
            token_head,
            token_head,
            jax.ShapeDtypeStruct((tokens, tokens), F32),
            jax.ShapeDtypeStruct((GROUPS, 8, per), F32),
        ],
        compiler_params=PARAMS,
        name="prep",
    )(dt_raw, params, marks)


def state_kernel(val_ref, proj_ref, scale_ref, edge_ref, out_ref):
    wide = widen(scale_ref[0])
    high, low = split(val_ref[...].astype(F32) * wide)
    proj = proj_ref[...]
    state = dot(jnp.concatenate([proj, proj], axis=0), jnp.concatenate([high, low], axis=0), ((0,), (0,)))
    pieces = dot(edge_ref[0].astype(BF16), spread_map(scale_ref.shape[2], BF16))
    chunks, _, width = out_ref.shape
    row = iota((8, width), 0)
    for j in range(chunks):
        mine = slice(j * width, (j + 1) * width)
        block = state[:, mine]
        power = exponent_of(block)
        out_ref[j, 0:STATE] = block * jnp.exp2(TOP - power)
        aux = jnp.where(row == 3, jnp.broadcast_to(power, row.shape), pieces[:, mine])
        out_ref[j, STATE:ROWS] = jnp.where(row < 4, aux, 0.0)


def states(values, proj, scale, edge, parts):
    tokens, channels = values.shape
    chunks = parts // GROUPS
    wide = channels // GROUPS
    per = scale.shape[2]
    return pl.pallas_call(
        state_kernel,
        grid=(GROUPS,),
        in_specs=[
            pl.BlockSpec((tokens, wide), lambda g: (0, g)),
            pl.BlockSpec((tokens, STATE), lambda g: (0, g)),
            pl.BlockSpec((1, tokens, per), lambda g: (g, 0, 0)),
            pl.BlockSpec((1, 8, per), lambda g: (g, 0, 0)),
        ],
        out_specs=pl.BlockSpec((chunks, ROWS, wide // chunks), lambda g: (g, 0, 0)),
        out_shape=jax.ShapeDtypeStruct((parts, ROWS, channels // parts), F32),
        compiler_params=PARAMS,
        cost_estimate=pl.CostEstimate(flops=2 * 2 * tokens * STATE * channels, bytes_accessed=3500000, transcendentals=0),
        name="states",
    )(values, proj, scale, edge)


def keep_row(block):
    return jnp.exp((block[STATE : STATE + 1] + block[STATE + 1 : STATE + 2] + block[STATE + 2 : STATE + 3]) * (1.0 / 128.0))


def unscaled(block):
    return block[0:STATE] * jnp.exp2(block[STATE + 3 : STATE + 4] - TOP)


def total_kernel(reverse, pay_ref, out_ref):
    parts, _, width = pay_ref.shape
    total = jnp.zeros((STATE, width), F32)
    through = jnp.ones((1, width), F32)
    for i in reversed(range(parts)) if reverse else range(parts):
        block = pay_ref[i]
        keep = keep_row(block)
        total = keep * total + unscaled(block)
        through = through * keep
    out_ref[0:STATE] = total
    out_ref[STATE:ROWS] = jnp.broadcast_to(through, (8, width))


def totals(pay, reverse):
    _, _, width = pay.shape
    return pl.pallas_call(
        functools.partial(total_kernel, reverse),
        out_shape=jax.ShapeDtypeStruct((ROWS, width), F32),
        compiler_params=PARAMS,
        cost_estimate=pl.CostEstimate(flops=2 * pay.size, bytes_accessed=4 * pay.size, transcendentals=0),
        name="totals",
    )(pay)


def enter_kernel(reverse, pay_ref, carry_ref, out_ref):
    parts, _, width = pay_ref.shape
    state = carry_ref[0:STATE]
    row = iota((8, width), 0)
    for i in reversed(range(parts)) if reverse else range(parts):
        power = exponent_of(state)
        out_ref[i, 0:STATE] = state * jnp.exp2(TOP - power)
        out_ref[i, STATE:ROWS] = jnp.where(row == 3, jnp.broadcast_to(power, row.shape), 0.0)
        block = pay_ref[i]
        state = keep_row(block) * state + unscaled(block)


def entering(pay, carry, reverse):
    return pl.pallas_call(
        functools.partial(enter_kernel, reverse),
        out_shape=jax.ShapeDtypeStruct(pay.shape, F32),
        compiler_params=PARAMS,
        cost_estimate=pl.CostEstimate(flops=4 * pay.size, bytes_accessed=8 * pay.size, transcendentals=0),
        name="entering",
    )(pay, carry)


def carried_in(total, reverse):
    count = lax.axis_size("far")

    def moved(value, by):
        if reverse:
            pairs = [(s, s - by) for s in range(by, count)]
        else:
            pairs = [(s, s + by) for s in range(count - by)]
        return lax.ppermute(value, "far", pairs)

    def joined(near, far):
        state = near[0:STATE] + near[STATE : STATE + 1] * far[0:STATE]
        return jnp.concatenate([state, near[STATE:] * far[STATE:]], axis=0)

    near = functools.reduce(joined, [moved(total, by) for by in (1, 2, 3, 4)])
    reach = 4
    while reach < count:
        steps = [by for by in (reach, 2 * reach, 3 * reach) if by < count]
        near = functools.reduce(joined, [near] + [moved(near, by) for by in steps])
        reach *= 4
    return near


def inner_kernel(x_ref, w_ref, b_ref, c_ref, run_ref, runt_ref, bias_ref, skip_ref, y_ref, gx_ref, gb_ref, gc_ref, col_ref, diff_ref):
    tokens, wide = x_ref.shape
    heads = wide // HEADDIM
    pair = 2 * HEADDIM
    b_vals, c_vals = b_ref[...], c_ref[...]
    scores = dot(c_vals, b_vals, ((1,), (1,)))
    bias = bias_ref[...]
    run, runt = run_ref[0], runt_ref[0]
    first = iota((tokens, pair), 1) < HEADDIM
    grad_scores = jnp.zeros((tokens, tokens), F32)
    y_all, u_all = [], []
    for k in range(0, heads, 2):
        mine = slice(k * HEADDIM, (k + 2) * HEADDIM)
        x_pair, w_pair = x_ref[:, mine], w_ref[:, mine]
        x_two = jnp.concatenate([x_pair, x_pair], axis=0)
        w_two = jnp.concatenate([w_pair, w_pair], axis=0)
        ys, us = [], []
        for which in range(2):
            h = k + which
            keep = first if which == 0 else ~first
            weight = jnp.exp(run[:, h : h + 1] - runt[h : h + 1, :] + bias)
            cross = dot(jnp.where(keep, w_pair, jnp.zeros_like(w_pair)), x_pair, ((1,), (1,)))
            grad_scores = grad_scores + weight * cross
            high, low = split(weight * scores)
            ys.append(dot(jnp.concatenate([high, low], axis=1), x_two))
            us.append(dot(jnp.concatenate([high, low], axis=0), w_two, ((0,), (0,))))
        y_all.append(jnp.where(first, ys[0], ys[1]))
        u_all.append(jnp.where(first, us[0], us[1]))
    y_in = jnp.concatenate(y_all, axis=1)
    u_in = jnp.concatenate(u_all, axis=1)
    x_vals, w_vals = x_ref[...].astype(F32), w_ref[...].astype(F32)
    skip = skip_ref[0:1]
    y_ref[...] = y_in + skip * x_vals
    gx_ref[...] = u_in + skip * w_vals
    high, low = split(grad_scores)
    gc_ref[...] = dot(jnp.concatenate([high, low], axis=1), jnp.concatenate([b_vals, b_vals], axis=0))
    gb_ref[...] = dot(jnp.concatenate([high, low], axis=0), jnp.concatenate([c_vals, c_vals], axis=0), ((0,), (0,)))
    col = head_sums(x_vals * u_in)
    col_ref[0] = col
    diff_ref[0] = head_sums(w_vals * y_in) - col


def inner(x, w, b, c, run, runt, bias, skip):
    tokens, channels = x.shape
    wide = channels // GROUPS
    per = run.shape[2]
    values = pl.BlockSpec((tokens, wide), lambda g: (0, g))
    proj = pl.BlockSpec((tokens, STATE), lambda g: (0, g))
    small = pl.BlockSpec((1, tokens, per), lambda g: (g, 0, 0))
    return pl.pallas_call(
        inner_kernel,
        grid=(GROUPS,),
        in_specs=[
            values,
            values,
            proj,
            proj,
            small,
            pl.BlockSpec((1, per, tokens), lambda g: (g, 0, 0)),
            pl.BlockSpec((tokens, tokens), lambda g: (0, 0)),
            pl.BlockSpec((8, wide), lambda g: (0, g)),
        ],
        out_specs=[values, values, proj, proj, small, small],
        out_shape=[
            jax.ShapeDtypeStruct((tokens, channels), F32),
            jax.ShapeDtypeStruct((tokens, channels), F32),
            jax.ShapeDtypeStruct((tokens, GROUPS * STATE), F32),
            jax.ShapeDtypeStruct((tokens, GROUPS * STATE), F32),
            jax.ShapeDtypeStruct((GROUPS, tokens, per), F32),
            jax.ShapeDtypeStruct((GROUPS, tokens, per), F32),
        ],
        compiler_params=PARAMS,
        cost_estimate=pl.CostEstimate(flops=20_000_000_000, bytes_accessed=8_000_000, transcendentals=tokens * tokens * 64),
        name="inner",
    )(x, w, b, c, run, runt, bias, skip)


def carried_terms(pay_ref, val_ref, other_ref, scale_ref, proj_ref):
    chunks = pay_ref.shape[0]
    wide = widen(scale_ref[0])
    proj = proj_ref[...]
    blocks = [pay_ref[j] for j in range(chunks)]
    state = jnp.concatenate([block[0:STATE] for block in blocks], axis=1)
    factor = jnp.exp2(jnp.concatenate([block[STATE + 3 : STATE + 4] for block in blocks], axis=1) - TOP)
    high, low = split(state)
    wide = wide * factor
    terms = dot(jnp.concatenate([proj, proj], axis=1), jnp.concatenate([high, low], axis=0)) * wide
    left_high, left_low = split(val_ref[...].astype(F32) * wide)
    last = ((1,), (1,))
    grad = dot(left_high, high, last) + (dot(left_high, low, last) + dot(left_low, high, last))
    return terms, grad, head_sums(terms * other_ref[...].astype(F32))


def forward_kernel(pay_ref, w_ref, c_ref, reach_ref, y_ref, gc_ref, mixed_ref, grad_ref, row_ref):
    terms, grad, rows = carried_terms(pay_ref, w_ref, w_ref, reach_ref, c_ref)
    mixed_ref[...] = (y_ref[...] + terms).astype(BF16)
    grad_ref[...] = (gc_ref[...] + grad).astype(BF16)
    row_ref[0] = rows


def forward(pay, w, c, reach, y, gc):
    tokens, channels = w.shape
    parts, _, width = pay.shape
    wide = channels // GROUPS
    per = reach.shape[2]
    values = pl.BlockSpec((tokens, wide), lambda g: (0, g))
    proj = pl.BlockSpec((tokens, STATE), lambda g: (0, g))
    small = pl.BlockSpec((1, tokens, per), lambda g: (g, 0, 0))
    return pl.pallas_call(
        forward_kernel,
        grid=(GROUPS,),
        in_specs=[
            pl.BlockSpec((parts // GROUPS, ROWS, width), lambda g: (g, 0, 0)),
            values,
            proj,
            small,
            values,
            proj,
        ],
        out_specs=[values, proj, small],
        out_shape=[
            jax.ShapeDtypeStruct((tokens, channels), BF16),
            jax.ShapeDtypeStruct((tokens, GROUPS * STATE), BF16),
            jax.ShapeDtypeStruct((GROUPS, tokens, per), F32),
        ],
        compiler_params=PARAMS,
        cost_estimate=pl.CostEstimate(flops=5 * 2 * tokens * STATE * channels, bytes_accessed=7_000_000, transcendentals=0),
        name="forward",
    )(pay, w, c, reach, y, gc)


def backward_kernel(
    pay_ref, enter_ref, x_ref, b_ref, tail_ref, gx_ref, gb_ref, col_ref, diff_ref, row_ref, size_ref, sig_ref, edge_ref,
    gradx_ref, grad_ref, dt_ref, all_ref,
):
    g = pl.program_id(0)
    tokens, _ = x_ref.shape
    chunks, _, width = pay_ref.shape
    per = tail_ref.shape[2]
    terms, grad, cols = carried_terms(pay_ref, x_ref, x_ref, tail_ref, b_ref)
    gradx_ref[...] = (gx_ref[...] + terms).astype(BF16)
    grad_ref[...] = (gb_ref[...] + grad).astype(BF16)
    met = []
    for j in range(chunks):
        leave, enter = pay_ref[j], enter_ref[j]
        factor = jnp.exp2(leave[STATE + 3 : STATE + 4] - TOP) * jnp.exp2(enter[STATE + 3 : STATE + 4] - TOP)
        met.append(jnp.sum(leave[0:STATE] * enter[0:STATE], axis=0, keepdims=True) * factor)
    met = head_sums(jnp.broadcast_to(jnp.concatenate(met, axis=1), (8, chunks * width)))[0:1]
    edge = edge_ref[0]
    keep, decay = edge[4:5], edge[5:6]
    shape = (tokens, tokens)
    from_here = (iota(shape, 0) <= iota(shape, 1)).astype(F32)
    before = (iota(shape, 0) > iota(shape, 1)).astype(F32)
    grad_rate = (
        dot(from_here, diff_ref[0] + row_ref[0], precision=PRECISE)
        + dot(before, cols, precision=PRECISE)
        + keep * met
    )
    grad_size = (col_ref[0] + cols) / size_ref[0] + decay * grad_rate
    place = (iota((per, GROUPS * per), 0) + g * per == iota((per, GROUPS * per), 1)).astype(F32)
    placed = dot(grad_size * sig_ref[0], place, precision=PRECISE)

    @pl.when(g == 0)
    def _():
        all_ref[...] = placed

    @pl.when(g > 0)
    def _():
        all_ref[...] += placed

    dt_ref[...] = all_ref[...].astype(BF16)


def backward(pay, enter, x, b, tail, gx, gb, col, diff, row, size, sig, edge):
    tokens, channels = x.shape
    parts, _, width = pay.shape
    wide = channels // GROUPS
    per = tail.shape[2]
    chunk = pl.BlockSpec((parts // GROUPS, ROWS, width), lambda g: (g, 0, 0))
    values = pl.BlockSpec((tokens, wide), lambda g: (0, g))
    proj = pl.BlockSpec((tokens, STATE), lambda g: (0, g))
    small = pl.BlockSpec((1, tokens, per), lambda g: (g, 0, 0))
    return pl.pallas_call(
        backward_kernel,
        grid=(GROUPS,),
        in_specs=[
            chunk, chunk, values, proj, small, values, proj, small, small, small, small, small,
            pl.BlockSpec((1, 8, per), lambda g: (g, 0, 0)),
        ],
        out_specs=[values, proj, pl.BlockSpec((tokens, GROUPS * per), lambda g: (0, 0))],
        out_shape=[
            jax.ShapeDtypeStruct((tokens, channels), BF16),
            jax.ShapeDtypeStruct((tokens, GROUPS * STATE), BF16),
            jax.ShapeDtypeStruct((tokens, GROUPS * per), BF16),
        ],
        scratch_shapes=[pltpu.VMEM((tokens, GROUPS * per), F32)],
        compiler_params=PARAMS,
        cost_estimate=pl.CostEstimate(flops=5 * 2 * tokens * STATE * channels, bytes_accessed=9_000_000, transcendentals=0),
        name="backward",
    )(pay, enter, x, b, tail, gx, gb, col, diff, row, size, sig, edge)


GROUP = ("near", "head")


def exchanged(*values):
    sent = jnp.concatenate([value.astype(jnp.float16) for value in values], axis=1)
    sent = lax.all_to_all(sent, GROUP, split_axis=0, concat_axis=0, tiled=True)
    return [sent[:, k * ROWS : (k + 1) * ROWS].astype(F32) for k in range(len(values))]


def gathered(own, heads):
    parts = lax.axis_size("head")
    per_dev = own.shape[1]
    mine = lax.axis_index("head")
    whole = jnp.where(iota((8, 128), 1) // per_dev == mine, jnp.tile(own, (1, 128 // per_dev)), 0.0)
    whole = jnp.broadcast_to(whole[None], (parts, 8, 128))
    return lax.all_to_all(whole, "head", split_axis=0, concat_axis=0, tiled=True).sum(axis=0)[:, :heads]


def per_device(features, dt_raw, b_proj, c_proj, cotangent, starts, a_log, dt_bias, d_skip):
    parts = lax.axis_size(GROUP)
    tokens, heads = dt_raw.shape
    params = gathered(jnp.stack([a_log, dt_bias, d_skip] + [d_skip] * 5), heads)
    marks = lax.dynamic_slice(starts, (lax.axis_index("head") * tokens,), (tokens,)).astype(F32)
    marks = jnp.broadcast_to(marks[None], (8, tokens))
    skip = jnp.broadcast_to(jnp.repeat(params[2], HEADDIM)[None], (8, heads * HEADDIM))
    size, sig, run, runt, reach, tail, bias, edge = prep(dt_raw, params, marks)
    leave, back = exchanged(
        states(features, b_proj, tail, edge, parts), states(cotangent, c_proj, reach, edge, parts)
    )
    y, gx, gb, gc, col, diff = inner(features, cotangent, b_proj, c_proj, run, runt, bias, skip)
    enter, after = exchanged(
        entering(leave, carried_in(totals(leave, False), False), False),
        entering(back, carried_in(totals(back, True), True), True),
    )
    mixed, grad_c, row = forward(enter, cotangent, c_proj, reach, y, gc)
    grad_x, grad_b, grad_dt = backward(
        after, enter, features, b_proj, tail, gx, gb, col, diff, row, size, sig, edge
    )
    return mixed, grad_x, grad_dt, grad_b, grad_c


def solution(mesh):
    devices = mesh.devices
    seq, parts = devices.shape
    fine = jax.sharding.Mesh(devices.reshape(seq // 2, 2, parts), ("far",) + GROUP)
    token = P(("far",) + GROUP, None)
    return jax.shard_map(
        per_device,
        mesh=fine,
        in_specs=(token, token, token, token, token, P(("far", "near")), P("head"), P("head"), P("head")),
        out_specs=(token, token, token, token, token),
        check_vma=False,
    )
```

time: 1120 us -> 331 us (0.30)
  the two profiles are of different devices: /device:TPU:98 before, /device:TPU:35 now
where the time goes in v1:
time: 331 us; the launch traced here: 330 us
  blocking collectives  113 us (34%)
  waiting for transfers between devices  105 us (32%)
  starting transfers between devices  63.6 us (19%)
  Pallas kernels  26.2 us (8%)
  local copies, waits for them, and re-layouts  15.4 us (5%)
  other arithmetic  6.57 us (2%)
    all_to_all x1, blocking collectives, exchanged(): sent = lax.all_to_all(sent, GROUP, split_axis=0, concat_axis=0, tiled=True)  113 us
    all_to_all x1, waiting for transfers between devices, exchanged(): sent = lax.all_to_all(sent, GROUP, split_axis=0, concat_axis=0, tiled=True)  90.1 us
    ppermute x14, starting transfers between devices, moved(): return lax.ppermute(value, 'far', pairs)  36.7 us
    all_to_all x1, starting transfers between devices, gathered(): lax.all_to_all(whole, 'head', split_axis=0, concat_axis=0, tiled=True)  16.6 us
    all_to_all x1, waiting for transfers between devices, gathered(): lax.all_to_all(whole, 'head', split_axis=0, concat_axis=0, tiled=True)  12.4 us
    unnamed x42, local copies, waits for them, and re-layouts  12.2 us
    all_to_all x1, starting transfers between devices, exchanged(): sent = lax.all_to_all(sent, GROUP, split_axis=0, concat_axis=0, tiled=True)  10.2 us
    pallas_call x1, Pallas kernels, inner(): pl.pallas_call(inner_kernel, grid=(GROUPS,), in_specs=[values, values, pr...  8.04 us
  transfers between devices with their start and end apart: 16, of which 3 were waited for; matrix products, arithmetic and copies ran while one was open for 1% of the time, Pallas kernels for 3%

profile of v1, /device:TPU:35, one launch (start us, length us, event | category | flops | bytes accessed | tf_op | source)
XLA Modules:
  0.0 330.5 jit_solution(8711086638762677864)
XLA Ops:
  0.7 0.9 stack.20
  1.8 0.7 broadcast_in_dim.27
  2.5 16.6 %all-to-all-start = ((f32[16,8,128]{2,1,0:T(8,128)}), f32[16,8,128]{2,1,0:T(8,128)S(1)}, u32[]{:S(2)}, u32[]{:S(2)}) async-start(f32[16,8,128]{2,1,0:T(8,128)} %broadcast_in_dim.27), calls=%async_computation | async-start | bytes 131072 | tf_op jit(solution)/shard_map/all_to_all | solution.py:453
  19.1 0.8 copy.22.dt_ref
  20.0 0.8 dynamic-slice_convert_fusion
  20.8 12.4 %all-to-all-done = f32[16,8,128]{2,1,0:T(8,128)S(1)} async-done(((f32[16,8,128]{2,1,0:T(8,128)}), f32[16,8,128]{2,1,0:T(8,128)S(1)}, u32[]{:S(2)}, u32[]{:S(2)}) %all-to-all-start) | async-done | bytes 65568 | tf_op jit(solution)/shard_map/all_to_all | solution.py:453
  33.2 0.6 prep.1
  33.8 0.7 copy-done.18
  34.5 1.2 copy-done
  35.7 0.9 copy-done.7
  36.6 2.5 states.2
  39.3 1.0 copy-done.2
  40.3 2.5 states.3
  43.0 0.6 pad_maximum_fusion
  43.6 112.6 %all_to_all.15 = f16[32,272,128]{2,1,0:T(8,128)(2,1)S(1)} all-to-all(f16[32,272,128]{2,1,0:T(8,128)(2,1)S(1)} %pad_maximum_fusion), channel_id=1, replica_groups=mesh['far'=16,'near'=2,'head'=16] {'near','head'}, dimensions={0} | all-to-all | bytes 4456448 | tf_op jit(solution)/shard_map/all_to_all | solution.py:443
  156.9 2.2 collective-permute-start.10
  159.1 1.9 collective-permute-start.9
  161.0 1.9 collective-permute-start.8
  162.9 2.5 collective-permute-start.7
  165.7 4.4 %collective-permute-start.3 = (f32[136,128]{1,0:T(8,128)S(1)}, f32[136,128]{1,0:T(8,128)S(1)}, u32[]{:S(2)}, u32[]{:S(2)}) collective-permute-start(f32[136,128]{1,0:T(8,128)S(1)} %totals.2), channel_id=1, source_target_pairs={{0,128},{32,160},{64,192},{96,224},{128,256},{160,288},{192,320},{... | collective-permute-start | bytes 208904 | tf_op jit(solution)/shard_map/ppermute | solution.py:221
  170.2 5.2 %collective-permute-start.2 = (f32[136,128]{1,0:T(8,128)S(1)}, f32[136,128]{1,0:T(8,128)S(1)}, u32[]{:S(2)}, u32[]{:S(2)}) collective-permute-start(f32[136,128]{1,0:T(8,128)S(1)} %totals.2), channel_id=1, source_target_pairs={{0,96},{32,128},{64,160},{96,192},{128,224},{160,256},{192,288},{2... | collective-permute-start | bytes 208904 | tf_op jit(solution)/shard_map/ppermute | solution.py:221
  175.4 1.9 collective-permute-start.1
  177.3 3.8 %collective-permute-start = (f32[136,128]{1,0:T(8,128)S(1)}, f32[136,128]{1,0:T(8,128)S(1)}, u32[]{:S(2)}, u32[]{:S(2)}) collective-permute-start(f32[136,128]{1,0:T(8,128)S(1)} %totals.2), channel_id=1, source_target_pairs={{0,32},{32,64},{64,96},{96,128},{128,160},{160,192},{192,224},{224... | collective-permute-start | bytes 208904 | tf_op jit(solution)/shard_map/ppermute | solution.py:221
  181.3 0.7 collective-permute-start.13
  181.9 1.3 collective-permute-start.12
  183.3 2.8 collective-permute-start.11
  186.2 0.7 collective-permute-start.6
  186.9 5.5 %collective-permute-start.5 = (f32[136,128]{1,0:T(8,128)S(1)}, f32[136,128]{1,0:T(8,128)S(1)}, u32[]{:S(2)}, u32[]{:S(2)}) collective-permute-start(f32[136,128]{1,0:T(8,128)S(1)} %pad_maximum_fusion.2), channel_id=1, source_target_pairs={{0,256},{32,288},{64,320},{96,352},{128,384},{160,416},{192,448},{... | collective-permute-start | bytes 208904 | tf_op jit(solution)/shard_map/ppermute | solution.py:221
  192.4 1.9 collective-permute-start.4
  195.1 2.3 collective-permute-done.4
  197.5 0.5 entering.2
  198.2 2.0 pad_maximum_fusion.1
  200.2 10.2 %all-to-all-start.2 = ((f16[32,272,128]{2,1,0:T(8,128)(2,1)}), f16[32,272,128]{2,1,0:T(8,128)(2,1)}, u32[]{:S(2)}, u32[]{:S(2)}) async-start(f16[32,272,128]{2,1,0:T(8,128)(2,1)} %pad_maximum_fusion.1), calls=%async_computation.2 | async-start | bytes 4456448 | tf_op jit(solution)/shard_map/all_to_all | solution.py:443
  210.4 0.7 broadcast_in_dim.29
  211.1 0.8 broadcast_in_dim.30
  212.0 0.9 copy-done.19
  212.9 8.0 %inner.1 = (f32[128,4096]{1,0:T(8,128)S(1)}, f32[128,4096]{1,0:T(8,128)S(1)}, f32[128,512]{1,0:T(8,128)S(1)}, f32[128,512]{1,0:T(8,128)S(1)}, f32[4,128,16]{2,1,0:T(8,128)S(1)}, /*index=5*/f32[4,128,16]{2,1,0:T(8,128)S(1)}) custom-call(bf16[128,4096]{1,0:T(8,128)(2,1)S(1)} %copy-done.1, bf16[128,4096]{1,0:T(8,128)(2,1)S(1)} %copy-done.2, ...), custom_call_target="tpu_custom_call" | custom-call | flops 20000000000 | bytes 8000000 | tf_op jit(solution)/shard_map/inner/pallas_call | solution.py:285
  221.0 1.4 copy-done.3
  222.3 1.4 copy-done.5
  223.7 0.7 copy-done.10
  224.4 0.7 copy-done.12
  225.1 0.7 copy-done.14
  225.8 0.7 copy-done.16
  226.5 90.1 %all-to-all-done.2 = f16[32,272,128]{2,1,0:T(8,128)(2,1)} async-done(((f16[32,272,128]{2,1,0:T(8,128)(2,1)}), f16[32,272,128]{2,1,0:T(8,128)(2,1)}, u32[]{:S(2)}, u32[]{:S(2)}) %all-to-all-start.2) | async-done | bytes 2228256 | tf_op jit(solution)/shard_map/all_to_all | solution.py:443
  316.6 2.0 slice_convert_fusion
  318.9 4.2 %forward.1 = (bf16[128,4096]{1,0:T(8,128)(2,1)}, bf16[128,512]{1,0:T(8,128)(2,1)}, f32[4,128,16]{2,1,0:T(8,128)S(1)}) custom-call(f32[32,136,128]{2,1,0:T(8,128)S(1)} %get-tuple-element.73.pay_ref.enter_ref, bf16[128,4096]{1,0:T(8,128)(2,1)S(1)} %copy-done.2, bf16[128,512]{1,0:T(8,128)(2,1)S(1)} %copy-done.9, ...), custom_call_target="tpu_custom_call" | custom-call | flops 671088640 | bytes 7000000 | tf_op jit(solution)/shard_map/forward/pallas_call | solution.py:344
  323.1 6.7 %backward.1 = (bf16[128,4096]{1,0:T(8,128)(2,1)}, bf16[128,512]{1,0:T(8,128)(2,1)}, bf16[128,64]{1,0:T(8,128)(2,1)S(1)}) custom-call(f32[32,136,128]{2,1,0:T(8,128)S(1)} %get-tuple-element.72.pay_ref, f32[32,136,128]{2,1,0:T(8,128)S(1)} %get-tuple-element.73.pay_ref.enter_ref, bf16[128,4096]{1,0:T(8,128)(2,1)S(1)} %copy-done.1, ...), custom_call_target="tpu_custom_call" | custom-call | flops 671088640 | bytes 9000000 | tf_op jit(solution)/shard_map/backward/pallas_call | solution.py:418
  329.8 0.7 copy.23
  (84 shorter events, 2.9 us)
Async XLA Ops:
  2.5 30.7 %all-to-all-start = ((f32[16,8,128]{2,1,0:T(8,128)}), f32[16,8,128]{2,1,0:T(8,128)S(1)}, u32[]{:S(2)}, u32[]{:S(2)}) async-start(f32[16,8,128]{2,1,0:T(8,128)} %broadcast_in_dim.27), calls=%async_computation | async-start | bytes 131072 | tf_op jit(solution)/shard_map/all_to_all | solution.py:453
  33.8 0.7 copy-start.18
  34.5 1.2 copy-start
  35.7 0.9 copy-start.7
  39.1 1.2 copy-start.2
  39.1 1.2 copy-start.9
  156.9 13.3 %collective-permute-start.10 = (f32[136,128]{1,0:T(8,128)S(1)}, f32[136,128]{1,0:T(8,128)S(1)}, u32[]{:S(2)}, u32[]{:S(2)}) collective-permute-start(f32[136,128]{1,0:T(8,128)S(1)} %totals.3), channel_id=1, source_target_pairs={{128,0},{160,32},{192,64},{224,96},{256,128},{288,160},{320,192},{... | collective-permute-start | bytes 208904 | tf_op jit(solution)/shard_map/ppermute | solution.py:221
  159.1 16.3 %collective-permute-start.9 = (f32[136,128]{1,0:T(8,128)S(1)}, f32[136,128]{1,0:T(8,128)S(1)}, u32[]{:S(2)}, u32[]{:S(2)}) collective-permute-start(f32[136,128]{1,0:T(8,128)S(1)} %totals.3), channel_id=1, source_target_pairs={{96,0},{128,32},{160,64},{192,96},{224,128},{256,160},{288,192},{3... | collective-permute-start | bytes 208904 | tf_op jit(solution)/shard_map/ppermute | solution.py:221
  161.0 16.3 %collective-permute-start.8 = (f32[136,128]{1,0:T(8,128)S(1)}, f32[136,128]{1,0:T(8,128)S(1)}, u32[]{:S(2)}, u32[]{:S(2)}) collective-permute-start(f32[136,128]{1,0:T(8,128)S(1)} %totals.3), channel_id=1, source_target_pairs={{64,0},{96,32},{128,64},{160,96},{192,128},{224,160},{256,192},{28... | collective-permute-start | bytes 208904 | tf_op jit(solution)/shard_map/ppermute | solution.py:221
  162.9 18.2 %collective-permute-start.7 = (f32[136,128]{1,0:T(8,128)S(1)}, f32[136,128]{1,0:T(8,128)S(1)}, u32[]{:S(2)}, u32[]{:S(2)}) collective-permute-start(f32[136,128]{1,0:T(8,128)S(1)} %totals.3), channel_id=1, source_target_pairs={{32,0},{64,32},{96,64},{128,96},{160,128},{192,160},{224,192},{256... | collective-permute-start | bytes 208904 | tf_op jit(solution)/shard_map/ppermute | solution.py:221
  165.7 16.2 %collective-permute-start.3 = (f32[136,128]{1,0:T(8,128)S(1)}, f32[136,128]{1,0:T(8,128)S(1)}, u32[]{:S(2)}, u32[]{:S(2)}) collective-permute-start(f32[136,128]{1,0:T(8,128)S(1)} %totals.2), channel_id=1, source_target_pairs={{0,128},{32,160},{64,192},{96,224},{128,256},{160,288},{192,320},{... | collective-permute-start | bytes 208904 | tf_op jit(solution)/shard_map/ppermute | solution.py:221
  170.2 13.1 %collective-permute-start.2 = (f32[136,128]{1,0:T(8,128)S(1)}, f32[136,128]{1,0:T(8,128)S(1)}, u32[]{:S(2)}, u32[]{:S(2)}) collective-permute-start(f32[136,128]{1,0:T(8,128)S(1)} %totals.2), channel_id=1, source_target_pairs={{0,96},{32,128},{64,160},{96,192},{128,224},{160,256},{192,288},{2... | collective-permute-start | bytes 208904 | tf_op jit(solution)/shard_map/ppermute | solution.py:221
  175.4 10.7 %collective-permute-start.1 = (f32[136,128]{1,0:T(8,128)S(1)}, f32[136,128]{1,0:T(8,128)S(1)}, u32[]{:S(2)}, u32[]{:S(2)}) collective-permute-start(f32[136,128]{1,0:T(8,128)S(1)} %totals.2), channel_id=1, source_target_pairs={{0,64},{32,96},{64,128},{96,160},{128,192},{160,224},{192,256},{22... | collective-permute-start | bytes 208904 | tf_op jit(solution)/shard_map/ppermute | solution.py:221
  177.3 8.8 %collective-permute-start = (f32[136,128]{1,0:T(8,128)S(1)}, f32[136,128]{1,0:T(8,128)S(1)}, u32[]{:S(2)}, u32[]{:S(2)}) collective-permute-start(f32[136,128]{1,0:T(8,128)S(1)} %totals.2), channel_id=1, source_target_pairs={{0,32},{32,64},{64,96},{96,128},{128,160},{160,192},{192,224},{224... | collective-permute-start | bytes 208904 | tf_op jit(solution)/shard_map/ppermute | solution.py:221
  181.3 11.1 %collective-permute-start.13 = (f32[136,128]{1,0:T(8,128)S(1)}, f32[136,128]{1,0:T(8,128)S(1)}, u32[]{:S(2)}, u32[]{:S(2)}) collective-permute-start(f32[136,128]{1,0:T(8,128)S(1)} %pad_maximum_fusion.4), channel_id=1, source_target_pairs={{384,0},{416,32},{448,64},{480,96},{385,1},{417,33},{449,65},{481,... | collective-permute-start | bytes 208904 | tf_op jit(solution)/shard_map/ppermute | solution.py:221
  181.9 12.4 %collective-permute-start.12 = (f32[136,128]{1,0:T(8,128)S(1)}, f32[136,128]{1,0:T(8,128)S(1)}, u32[]{:S(2)}, u32[]{:S(2)}) collective-permute-start(f32[136,128]{1,0:T(8,128)S(1)} %pad_maximum_fusion.4), channel_id=1, source_target_pairs={{256,0},{288,32},{320,64},{352,96},{384,128},{416,160},{448,192},{... | collective-permute-start | bytes 208904 | tf_op jit(solution)/shard_map/ppermute | solution.py:221
  183.3 11.1 %collective-permute-start.11 = (f32[136,128]{1,0:T(8,128)S(1)}, f32[136,128]{1,0:T(8,128)S(1)}, u32[]{:S(2)}, u32[]{:S(2)}) collective-permute-start(f32[136,128]{1,0:T(8,128)S(1)} %pad_maximum_fusion.4), channel_id=1, source_target_pairs={{128,0},{160,32},{192,64},{224,96},{256,128},{288,160},{320,192},{... | collective-permute-start | bytes 208904 | tf_op jit(solution)/shard_map/ppermute | solution.py:221
  186.2 8.9 %collective-permute-start.6 = (f32[136,128]{1,0:T(8,128)S(1)}, f32[136,128]{1,0:T(8,128)S(1)}, u32[]{:S(2)}, u32[]{:S(2)}) collective-permute-start(f32[136,128]{1,0:T(8,128)S(1)} %pad_maximum_fusion.2), channel_id=1, source_target_pairs={{0,384},{32,416},{64,448},{96,480},{1,385},{33,417},{65,449},{97,4... | collective-permute-start | bytes 208904 | tf_op jit(solution)/shard_map/ppermute | solution.py:221
  186.9 8.2 %collective-permute-start.5 = (f32[136,128]{1,0:T(8,128)S(1)}, f32[136,128]{1,0:T(8,128)S(1)}, u32[]{:S(2)}, u32[]{:S(2)}) collective-permute-start(f32[136,128]{1,0:T(8,128)S(1)} %pad_maximum_fusion.2), channel_id=1, source_target_pairs={{0,256},{32,288},{64,320},{96,352},{128,384},{160,416},{192,448},{... | collective-permute-start | bytes 208904 | tf_op jit(solution)/shard_map/ppermute | solution.py:221
  192.4 5.1 %collective-permute-start.4 = (f32[136,128]{1,0:T(8,128)S(1)}, f32[136,128]{1,0:T(8,128)S(1)}, u32[]{:S(2)}, u32[]{:S(2)}) collective-permute-start(f32[136,128]{1,0:T(8,128)S(1)} %pad_maximum_fusion.2), channel_id=1, source_target_pairs={{0,128},{32,160},{64,192},{96,224},{128,256},{160,288},{192,320},{... | collective-permute-start | bytes 208904 | tf_op jit(solution)/shard_map/ppermute | solution.py:221
  200.2 11.8 %copy-start.1 = (bf16[128,4096]{1,0:T(8,128)(2,1)S(1)}, bf16[128,4096]{1,0:T(8,128)(2,1)}, u32[]{:S(2)}) copy-start(bf16[128,4096]{1,0:T(8,128)(2,1)} %x_ref.3) | copy-start | bytes 3145732
  200.2 11.8 %copy-start.8 = (bf16[128,512]{1,0:T(8,128)(2,1)S(1)}, bf16[128,512]{1,0:T(8,128)(2,1)}, u32[]{:S(2)}) copy-start(bf16[128,512]{1,0:T(8,128)(2,1)} %b_ref.3) | copy-start | bytes 393220
  200.2 116.5 %all-to-all-start.2 = ((f16[32,272,128]{2,1,0:T(8,128)(2,1)}), f16[32,272,128]{2,1,0:T(8,128)(2,1)}, u32[]{:S(2)}, u32[]{:S(2)}) async-start(f16[32,272,128]{2,1,0:T(8,128)(2,1)} %pad_maximum_fusion.1), calls=%async_computation.2 | async-start | bytes 4456448 | tf_op jit(solution)/shard_map/all_to_all | solution.py:443
  212.0 1.0 copy-start.19
  221.0 1.4 copy-start.3
  222.3 1.4 copy-start.5
  223.7 0.7 copy-start.10
  224.4 0.7 copy-start.12
  225.1 0.7 copy-start.14
  225.8 0.7 copy-start.16
  316.6 2.3 copy-start.4
  316.6 2.3 copy-start.17
  318.9 4.2 %copy-start.6 = (f32[128,4096]{1,0:T(8,128)S(1)}, f32[128,4096]{1,0:T(8,128)}, u32[]{:S(2)}) copy-start(f32[128,4096]{1,0:T(8,128)} %copy-done.5) | copy-start | bytes 6291460
  318.9 4.2 %copy-start.11 = (f32[128,512]{1,0:T(8,128)S(1)}, f32[128,512]{1,0:T(8,128)}, u32[]{:S(2)}) copy-start(f32[128,512]{1,0:T(8,128)} %copy-done.10) | copy-start | bytes 786436
  318.9 4.2 %copy-start.13 = (f32[4,128,16]{2,1,0:T(8,128)S(1)}, f32[4,128,16]{2,1,0:T(8,128)}, u32[]{:S(2)}) copy-start(f32[4,128,16]{2,1,0:T(8,128)} %copy-done.12) | copy-start | bytes 98308
  318.9 4.2 %copy-start.15 = (f32[4,128,16]{2,1,0:T(8,128)S(1)}, f32[4,128,16]{2,1,0:T(8,128)}, u32[]{:S(2)}) copy-start(f32[4,128,16]{2,1,0:T(8,128)} %copy-done.14) | copy-start | bytes 98308

commit v2 on v1

v2 whole, which is shorter than its diff:
```python
import functools

import jax
import jax.numpy as jnp
from jax import lax
from jax.experimental import pallas as pl
from jax.experimental.pallas import tpu as pltpu
from jax.sharding import PartitionSpec as P

GROUPS = 4
HEADDIM = 64
STATE = 128
LANES = 128
TOP = 13.0
CUT = -65000.0
F32 = jnp.float32
BF16 = jnp.bfloat16
PRECISE = lax.Precision.HIGHEST
PARAMS = pltpu.CompilerParams(vmem_limit_bytes=40 * 1024 * 1024)


def iota(shape, axis):
    return lax.broadcasted_iota(jnp.int32, shape, axis)


def split(value):
    high = value.astype(BF16)
    return high, (value - high.astype(F32)).astype(BF16)


def dot(a, b, dims=((1,), (0,)), precision=None):
    return lax.dot_general(a, b, (dims, ((), ())), precision=precision, preferred_element_type=F32)


def spread_map(heads, dtype):
    shape = (heads, heads * HEADDIM)
    return (iota(shape, 0) == iota(shape, 1) // HEADDIM).astype(dtype)


def widen(value):
    both = jnp.concatenate(split(value), axis=1)
    spread = spread_map(value.shape[1], BF16)
    return dot(both, jnp.concatenate([spread, spread], axis=0))


def head_sums(value):
    heads = value.shape[1] // HEADDIM
    shape = (heads * HEADDIM, heads)
    fold = (iota(shape, 0) // HEADDIM == iota(shape, 1)).astype(BF16)
    high, low = split(value)
    return dot(high, fold) + dot(low, fold)


def exponent_of(block):
    top = jnp.max(jnp.abs(block), axis=0, keepdims=True)
    return jnp.clip(jnp.floor(jnp.log(jnp.maximum(top, 1e-30)) * 1.4426950408889634), -90.0, 40.0)


def prep_kernel(dt_ref, par_ref, st_ref, size_ref, sig_ref, run_ref, runt_ref, reach_ref, tail_ref, bias_ref, edge_ref):
    tokens, heads = dt_ref.shape
    per = heads // GROUPS
    par = par_ref[...]
    a_log, dt_bias = par[0:1], par[1:2]
    decay = -jnp.exp(a_log)
    value = dt_ref[...].astype(F32) + dt_bias
    sizes = jnp.maximum(value, 0.0) + jnp.log1p(jnp.exp(-jnp.abs(value)))
    sigmoid = 1.0 / (1.0 + jnp.exp(-value))
    shape = (tokens, tokens)
    lower = (iota(shape, 0) >= iota(shape, 1)).astype(F32)
    upper = (iota(shape, 0) <= iota(shape, 1)).astype(F32)
    running = dot(lower, sizes * decay, precision=PRECISE)
    marks = st_ref[...]
    doc_row = dot(marks, upper)[0:1]
    doc_col = dot(lower, marks, ((1,), (1,)))[:, 0:1]
    doc_last = doc_row[:, tokens - 1 :]
    last = running[tokens - 1 :]
    reach = jnp.where(doc_col == 0.0, jnp.exp(running), 0.0)
    tail = jnp.where(doc_col == doc_last, jnp.exp(last - running), 0.0) * sizes
    linked = (doc_col == doc_row) & (iota(shape, 0) >= iota(shape, 1))
    bias_ref[...] = jnp.where(linked, 0.0, -1e30)
    turned = (running - jnp.log(sizes)).T
    through = jnp.where(doc_last == 0.0, last * 128.0, CUT)
    high = through.astype(BF16).astype(F32)
    mid = (through - high).astype(BF16).astype(F32)
    low = (through - high - mid).astype(BF16).astype(F32)
    keep = jnp.exp((high + mid + low) * (1.0 / 128.0))
    edge = jnp.concatenate([high, mid, low, jnp.zeros_like(keep), keep, decay, decay, decay], axis=0)
    for g in range(GROUPS):
        mine = slice(g * per, (g + 1) * per)
        size_ref[g] = sizes[:, mine]
        sig_ref[g] = sigmoid[:, mine]
        run_ref[g] = running[:, mine]
        runt_ref[g] = turned[mine]
        reach_ref[g] = reach[:, mine]
        tail_ref[g] = tail[:, mine]
        edge_ref[g] = edge[:, mine]


def prep(dt_raw, params, marks):
    tokens, heads = dt_raw.shape
    per = heads // GROUPS
    token_head = jax.ShapeDtypeStruct((GROUPS, tokens, per), F32)
    return pl.pallas_call(
        prep_kernel,
        out_shape=[
            token_head,
            token_head,
            token_head,
            jax.ShapeDtypeStruct((GROUPS, per, tokens), F32),
            token_head,
            token_head,
            jax.ShapeDtypeStruct((tokens, tokens), F32),
            jax.ShapeDtypeStruct((GROUPS, 8, per), F32),
        ],
        compiler_params=PARAMS,
        name="prep",
    )(dt_raw, params, marks)


def state_of(val_ref, proj_ref, scale_ref):
    high, low = split(val_ref[...].astype(F32) * widen(scale_ref[0]))
    proj = proj_ref[...]
    return dot(jnp.concatenate([proj, proj], axis=0), jnp.concatenate([high, low], axis=0), ((0,), (0,)))


def state_kernel(x_ref, w_ref, b_ref, c_ref, tail_ref, reach_ref, edge_ref, out_ref):
    forth = state_of(x_ref, b_ref, tail_ref)
    back = state_of(w_ref, c_ref, reach_ref)
    pieces = dot(edge_ref[0].astype(BF16), spread_map(tail_ref.shape[2], BF16))
    messages, rows, _ = out_ref.shape
    part = (rows - 8) // 2
    fold = STATE // part
    row = iota((8, LANES), 0)
    for k in range(messages):
        lanes = slice(k // fold * LANES, (k // fold + 1) * LANES)
        here = slice(k % fold * part, (k % fold + 1) * part)
        aux = jnp.where(row < 3, pieces[:, lanes], 0.0)
        for which, state in enumerate((forth, back)):
            block = state[here, lanes]
            power = exponent_of(block)
            out_ref[k, which * part : (which + 1) * part] = block * jnp.exp2(TOP - power)
            aux = jnp.where(row == 3 + which, power, aux)
        out_ref[k, 2 * part :] = aux


def states(x, w, b, c, tail, reach, edge, parts):
    tokens, channels = x.shape
    wide = channels // GROUPS
    per = tail.shape[2]
    rows = 2 * STATE * channels // (parts * LANES) + 8
    values = pl.BlockSpec((tokens, wide), lambda g: (0, g))
    proj = pl.BlockSpec((tokens, STATE), lambda g: (0, g))
    small = pl.BlockSpec((1, tokens, per), lambda g: (g, 0, 0))
    return pl.pallas_call(
        state_kernel,
        grid=(GROUPS,),
        in_specs=[values, values, proj, proj, small, small, pl.BlockSpec((1, 8, per), lambda g: (g, 0, 0))],
        out_specs=pl.BlockSpec((parts // GROUPS, rows, LANES), lambda g: (g, 0, 0)),
        out_shape=jax.ShapeDtypeStruct((parts, rows, LANES), F32),
        compiler_params=PARAMS,
        cost_estimate=pl.CostEstimate(flops=8 * tokens * STATE * channels, bytes_accessed=7000000, transcendentals=0),
        name="states",
    )(x, w, b, c, tail, reach, edge)


def keep_row(pay_ref, i, part):
    side = pay_ref[i, 2 * part :]
    return jnp.exp((side[0:1] + side[1:2] + side[2:3]) * (1.0 / 128.0))


def unscaled(pay_ref, i, part, which):
    power = pay_ref[i, 2 * part :][3 + which : 4 + which]
    return pay_ref[i, which * part : (which + 1) * part] * jnp.exp2(power - TOP)


def total_kernel(pay_ref, out_ref):
    blocks, rows, _ = pay_ref.shape
    part = (rows - 8) // 2

    def step(k, carry):
        forth, back, through = carry
        forth = keep_row(pay_ref, k, part) * forth + unscaled(pay_ref, k, part, 0)
        late = blocks - 1 - k
        keep = keep_row(pay_ref, late, part)
        return forth, unscaled(pay_ref, late, part, 1) + keep * back, through * keep

    zero = jnp.zeros((part, LANES), F32)
    forth, back, through = lax.fori_loop(0, blocks, step, (zero, zero, jnp.ones((1, LANES), F32)), unroll=8)
    for which, state in enumerate((forth, back)):
        out_ref[which, 0:part] = state
        out_ref[which, part:] = jnp.broadcast_to(through, (8, LANES))


def totals(pay):
    _, rows, _ = pay.shape
    part = (rows - 8) // 2
    return pl.pallas_call(
        total_kernel,
        out_shape=jax.ShapeDtypeStruct((2, part + 8, LANES), F32),
        compiler_params=PARAMS,
        cost_estimate=pl.CostEstimate(flops=2 * pay.size, bytes_accessed=4 * pay.size, transcendentals=0),
        name="totals",
    )(pay)


def enter_kernel(pay_ref, forth_ref, back_ref, out_ref):
    blocks, rows, _ = pay_ref.shape
    part = (rows - 8) // 2
    row = iota((8, LANES), 0)

    def put(i, which, state):
        power = exponent_of(state)
        out_ref[i, which * part : (which + 1) * part] = state * jnp.exp2(TOP - power)
        return power

    def step(k, carry):
        forth, back = carry
        late = blocks - 1 - k
        out_ref[k, 2 * part :] = jnp.where(row == 3, put(k, 0, forth), out_ref[k, 2 * part :])
        out_ref[late, 2 * part :] = jnp.where(row == 4, put(late, 1, back), out_ref[late, 2 * part :])
        forth = keep_row(pay_ref, k, part) * forth + unscaled(pay_ref, k, part, 0)
        back = keep_row(pay_ref, late, part) * back + unscaled(pay_ref, late, part, 1)
        return forth, back

    out_ref[:, 2 * part :, :] = jnp.zeros((blocks, 8, LANES), F32)
    lax.fori_loop(0, blocks, step, (forth_ref[0:part], back_ref[0:part]), unroll=8)


def entering(pay, forth, back):
    return pl.pallas_call(
        enter_kernel,
        out_shape=jax.ShapeDtypeStruct(pay.shape, F32),
        compiler_params=PARAMS,
        cost_estimate=pl.CostEstimate(flops=4 * pay.size, bytes_accessed=8 * pay.size, transcendentals=0),
        name="entering",
    )(pay, forth, back)


def carried_in(total, reverse):
    count = lax.axis_size("far")

    def moved(by):
        if reverse:
            pairs = [(s, s - by) for s in range(by, count)]
        else:
            pairs = [(s, s + by) for s in range(count - by)]
        return lax.ppermute(total, "far", pairs)

    def joined(near, far):
        through = near[-8:]
        state = near[:-8] + through[0:1] * far[:-8]
        return jnp.concatenate([state, through * far[-8:]], axis=0)

    return functools.reduce(joined, [moved(by) for by in range(1, count)])


def inner_kernel(x_ref, w_ref, b_ref, c_ref, run_ref, runt_ref, bias_ref, skip_ref, y_ref, gx_ref, gb_ref, gc_ref, col_ref, diff_ref):
    tokens, wide = x_ref.shape
    heads = wide // HEADDIM
    pair = 2 * HEADDIM
    b_vals, c_vals = b_ref[...], c_ref[...]
    scores = dot(c_vals, b_vals, ((1,), (1,)))
    bias = bias_ref[...]
    run, runt = run_ref[0], runt_ref[0]
    first = iota((tokens, pair), 1) < HEADDIM
    grad_scores = jnp.zeros((tokens, tokens), F32)
    y_all, u_all = [], []
    for k in range(0, heads, 2):
        mine = slice(k * HEADDIM, (k + 2) * HEADDIM)
        x_pair, w_pair = x_ref[:, mine], w_ref[:, mine]
        x_two = jnp.concatenate([x_pair, x_pair], axis=0)
        w_two = jnp.concatenate([w_pair, w_pair], axis=0)
        ys, us = [], []
        for which in range(2):
            h = k + which
            keep = first if which == 0 else ~first
            weight = jnp.exp(run[:, h : h + 1] - runt[h : h + 1, :] + bias)
            cross = dot(jnp.where(keep, w_pair, jnp.zeros_like(w_pair)), x_pair, ((1,), (1,)))
            grad_scores = grad_scores + weight * cross
            high, low = split(weight * scores)
            ys.append(dot(jnp.concatenate([high, low], axis=1), x_two))
            us.append(dot(jnp.concatenate([high, low], axis=0), w_two, ((0,), (0,))))
        y_all.append(jnp.where(first, ys[0], ys[1]))
        u_all.append(jnp.where(first, us[0], us[1]))
    y_in = jnp.concatenate(y_all, axis=1)
    u_in = jnp.concatenate(u_all, axis=1)
    x_vals, w_vals = x_ref[...].astype(F32), w_ref[...].astype(F32)
    skip = skip_ref[0:1]
    y_ref[...] = y_in + skip * x_vals
    gx_ref[...] = u_in + skip * w_vals
    high, low = split(grad_scores)
    gc_ref[...] = dot(jnp.concatenate([high, low], axis=1), jnp.concatenate([b_vals, b_vals], axis=0))
    gb_ref[...] = dot(jnp.concatenate([high, low], axis=0), jnp.concatenate([c_vals, c_vals], axis=0), ((0,), (0,)))
    col = head_sums(x_vals * u_in)
    col_ref[0] = col
    diff_ref[0] = head_sums(w_vals * y_in) - col


def inner(x, w, b, c, run, runt, bias, skip):
    tokens, channels = x.shape
    wide = channels // GROUPS
    per = run.shape[2]
    values = pl.BlockSpec((tokens, wide), lambda g: (0, g))
    proj = pl.BlockSpec((tokens, STATE), lambda g: (0, g))
    small = pl.BlockSpec((1, tokens, per), lambda g: (g, 0, 0))
    return pl.pallas_call(
        inner_kernel,
        grid=(GROUPS,),
        in_specs=[
            values,
            values,
            proj,
            proj,
            small,
            pl.BlockSpec((1, per, tokens), lambda g: (g, 0, 0)),
            pl.BlockSpec((tokens, tokens), lambda g: (0, 0)),
            pl.BlockSpec((8, wide), lambda g: (0, g)),
        ],
        out_specs=[values, values, proj, proj, small, small],
        out_shape=[
            jax.ShapeDtypeStruct((tokens, channels), F32),
            jax.ShapeDtypeStruct((tokens, channels), F32),
            jax.ShapeDtypeStruct((tokens, GROUPS * STATE), F32),
            jax.ShapeDtypeStruct((tokens, GROUPS * STATE), F32),
            jax.ShapeDtypeStruct((GROUPS, tokens, per), F32),
            jax.ShapeDtypeStruct((GROUPS, tokens, per), F32),
        ],
        compiler_params=PARAMS,
        cost_estimate=pl.CostEstimate(flops=20_000_000_000, bytes_accessed=8_000_000, transcendentals=tokens * tokens * 64),
        name="inner",
    )(x, w, b, c, run, runt, bias, skip)


def state_from(pay_ref, which):
    messages, rows, _ = pay_ref.shape
    part = (rows - 8) // 2
    fold = STATE // part
    columns = []
    for first in range(0, messages, fold):
        columns.append(jnp.concatenate([unscaled(pay_ref, first + k, part, which) for k in range(fold)], axis=0))
    return jnp.concatenate(columns, axis=1)


def carried_terms(state, values, scale_ref, proj_ref):
    wide = widen(scale_ref[0])
    proj = proj_ref[...]
    high, low = split(state)
    terms = dot(jnp.concatenate([proj, proj], axis=1), jnp.concatenate([high, low], axis=0)) * wide
    left_high, left_low = split(values * wide)
    last = ((1,), (1,))
    grad = dot(left_high, high, last) + (dot(left_high, low, last) + dot(left_low, high, last))
    return terms, grad, head_sums(terms * values)


def finish_kernel(
    pay_ref, x_ref, w_ref, b_ref, c_ref, tail_ref, reach_ref, y_ref, gx_ref, gb_ref, gc_ref, col_ref, diff_ref, size_ref, sig_ref, edge_ref,
    mixed_ref, gradx_ref, dt_ref, gradb_ref, gradc_ref, all_ref,
):
    g = pl.program_id(0)
    tokens, _ = x_ref.shape
    per = tail_ref.shape[2]
    enter, leave = state_from(pay_ref, 0), state_from(pay_ref, 1)
    terms, grad, rows = carried_terms(enter, w_ref[...].astype(F32), reach_ref, c_ref)
    mixed_ref[...] = (y_ref[...] + terms).astype(BF16)
    gradc_ref[...] = (gc_ref[...] + grad).astype(BF16)
    terms, grad, cols = carried_terms(leave, x_ref[...].astype(F32), tail_ref, b_ref)
    gradx_ref[...] = (gx_ref[...] + terms).astype(BF16)
    gradb_ref[...] = (gb_ref[...] + grad).astype(BF16)
    met = jnp.sum(enter * leave, axis=0, keepdims=True)
    met = head_sums(jnp.broadcast_to(met, (8, met.shape[1])))[0:1]
    edge = edge_ref[0]
    keep, decay = edge[4:5], edge[5:6]
    shape = (tokens, tokens)
    from_here = (iota(shape, 0) <= iota(shape, 1)).astype(F32)
    before = (iota(shape, 0) > iota(shape, 1)).astype(F32)
    grad_rate = dot(from_here, diff_ref[0] + rows, precision=PRECISE) + dot(before, cols, precision=PRECISE) + keep * met
    grad_size = (col_ref[0] + cols) / size_ref[0] + decay * grad_rate
    place = (iota((per, GROUPS * per), 0) + g * per == iota((per, GROUPS * per), 1)).astype(F32)
    placed = dot(grad_size * sig_ref[0], place, precision=PRECISE)

    @pl.when(g == 0)
    def _():
        all_ref[...] = placed

    @pl.when(g > 0)
    def _():
        all_ref[...] += placed

    dt_ref[...] = all_ref[...].astype(BF16)


def finish(pay, x, w, b, c, tail, reach, y, gx, gb, gc, col, diff, size, sig, edge):
    tokens, channels = x.shape
    parts, rows, _ = pay.shape
    wide = channels // GROUPS
    per = tail.shape[2]
    values = pl.BlockSpec((tokens, wide), lambda g: (0, g))
    proj = pl.BlockSpec((tokens, STATE), lambda g: (0, g))
    small = pl.BlockSpec((1, tokens, per), lambda g: (g, 0, 0))
    return pl.pallas_call(
        finish_kernel,
        grid=(GROUPS,),
        in_specs=[
            pl.BlockSpec((parts // GROUPS, rows, LANES), lambda g: (g, 0, 0)),
            values, values, proj, proj, small, small, values, values, proj, proj, small, small, small, small,
            pl.BlockSpec((1, 8, per), lambda g: (g, 0, 0)),
        ],
        out_specs=[values, values, pl.BlockSpec((tokens, GROUPS * per), lambda g: (0, 0)), proj, proj],
        out_shape=[
            jax.ShapeDtypeStruct((tokens, channels), BF16),
            jax.ShapeDtypeStruct((tokens, channels), BF16),
            jax.ShapeDtypeStruct((tokens, GROUPS * per), BF16),
            jax.ShapeDtypeStruct((tokens, GROUPS * STATE), BF16),
            jax.ShapeDtypeStruct((tokens, GROUPS * STATE), BF16),
        ],
        scratch_shapes=[pltpu.VMEM((tokens, GROUPS * per), F32)],
        compiler_params=PARAMS,
        cost_estimate=pl.CostEstimate(flops=20 * tokens * STATE * channels, bytes_accessed=14_000_000, transcendentals=0),
        name="finish",
    )(pay, x, w, b, c, tail, reach, y, gx, gb, gc, col, diff, size, sig, edge)


GROUP = ("near", "head")


def exchanged(messages):
    sent = lax.all_to_all(messages.astype(jnp.float16), GROUP, split_axis=0, concat_axis=0, tiled=True)
    return sent.astype(F32)


def gathered(own, heads):
    parts = lax.axis_size("head")
    per_dev = own.shape[1]
    mine = lax.axis_index("head")
    whole = jnp.where(iota((8, 128), 1) // per_dev == mine, jnp.tile(own, (1, 128 // per_dev)), 0.0)
    whole = jnp.broadcast_to(whole[None], (parts, 8, 128))
    return lax.all_to_all(whole, "head", split_axis=0, concat_axis=0, tiled=True).sum(axis=0)[:, :heads]


def per_device(features, dt_raw, b_proj, c_proj, cotangent, starts, a_log, dt_bias, d_skip):
    parts = lax.axis_size(GROUP)
    tokens, heads = dt_raw.shape
    params = gathered(jnp.stack([a_log, dt_bias, d_skip] + [d_skip] * 5), heads)
    marks = lax.dynamic_slice(starts, (lax.axis_index("head") * tokens,), (tokens,)).astype(F32)
    marks = jnp.broadcast_to(marks[None], (8, tokens))
    skip = jnp.broadcast_to(jnp.repeat(params[2], HEADDIM)[None], (8, heads * HEADDIM))
    size, sig, run, runt, reach, tail, bias, edge = prep(dt_raw, params, marks)
    came = exchanged(states(features, cotangent, b_proj, c_proj, tail, reach, edge, parts))
    y, gx, gb, gc, col, diff = inner(features, cotangent, b_proj, c_proj, run, runt, bias, skip)
    total = totals(came)
    back = exchanged(entering(came, carried_in(total[0], False), carried_in(total[1], True)))
    return finish(
        back, features, cotangent, b_proj, c_proj, tail, reach, y, gx, gb, gc, col, diff, size, sig, edge
    )


def solution(mesh):
    near = 8
    devices = mesh.devices
    seq, parts = devices.shape
    fine = jax.sharding.Mesh(devices.reshape(seq // near, near, parts), ("far",) + GROUP)
    token = P(("far",) + GROUP, None)
    return jax.shard_map(
        per_device,
        mesh=fine,
        in_specs=(token, token, token, token, token, P(("far", "near")), P("head"), P("head"), P("head")),
        out_specs=(token, token, token, token, token),
        check_vma=False,
    )
```

time: 331 us -> 319 us (0.964)
  the two profiles are of different devices: /device:TPU:35 before, /device:TPU:2 now
where the time goes in v2:
time: 319 us; the launch traced here: 318 us
  blocking collectives  118 us (37%)
  waiting for transfers between devices  113 us (35%)
  starting transfers between devices  38.9 us (12%)
  Pallas kernels  24.3 us (8%)
  local copies, waits for them, and re-layouts  17.2 us (5%)
  other arithmetic  5.43 us (2%)
    all_to_all x1, blocking collectives, exchanged(): lax.all_to_all(messages.astype(jnp.float16), GROUP, split_axis=0, concat_...  118 us
    all_to_all x1, waiting for transfers between devices, exchanged(): lax.all_to_all(messages.astype(jnp.float16), GROUP, split_axis=0, concat_...  95.7 us
    all_to_all x1, starting transfers between devices, gathered(): lax.all_to_all(whole, 'head', split_axis=0, concat_axis=0, tiled=True)  17.8 us
    ppermute x6, starting transfers between devices, moved(): return lax.ppermute(total, 'far', pairs)  13.7 us
    all_to_all x1, waiting for transfers between devices, gathered(): lax.all_to_all(whole, 'head', split_axis=0, concat_axis=0, tiled=True)  13.4 us
    unnamed x45, local copies, waits for them, and re-layouts  13.3 us
    pallas_call x1, Pallas kernels, finish(): pl.pallas_call(finish_kernel, grid=(GROUPS,), in_specs=[pl.BlockSpec((par...  9.22 us
    pallas_call x1, Pallas kernels, inner(): pl.pallas_call(inner_kernel, grid=(GROUPS,), in_specs=[values, values, pr...  8.03 us
  transfers between devices with their start and end apart: 8, of which 3 were waited for; matrix products, arithmetic and copies ran while one was open for 1% of the time, Pallas kernels for 3%

profile of v2, /device:TPU:2, one launch (start us, length us, event | category | flops | bytes accessed | tf_op | source)
XLA Modules:
  0.0 317.9 jit_solution(12487270056005103427)
XLA Ops:
  0.7 0.9 stack.20
  1.6 0.1 copy.20
  1.7 0.1 fusion
  1.8 0.7 broadcast_in_dim.27
  2.5 17.8 %all-to-all-start = ((f32[16,8,128]{2,1,0:T(8,128)}), f32[16,8,128]{2,1,0:T(8,128)S(1)}, u32[]{:S(2)}, u32[]{:S(2)}) async-start(f32[16,8,128]{2,1,0:T(8,128)} %broadcast_in_dim.27), calls=%async_computation | async-start | bytes 131072 | tf_op jit(solution)/shard_map/all_to_all | solution.py:437
  20.3 0.8 copy.22.dt_ref
  21.2 0.8 dynamic-slice_convert_fusion
  21.9 13.4 %all-to-all-done = f32[16,8,128]{2,1,0:T(8,128)S(1)} async-done(((f32[16,8,128]{2,1,0:T(8,128)}), f32[16,8,128]{2,1,0:T(8,128)S(1)}, u32[]{:S(2)}, u32[]{:S(2)}) %all-to-all-start) | async-done | bytes 65568 | tf_op jit(solution)/shard_map/all_to_all | solution.py:437
  35.3 0.6 prep.1
  35.9 0.7 copy-done.20
  36.6 1.2 copy-done
  37.8 1.2 copy-done.2
  39.1 0.9 copy-done.8
  40.0 0.9 copy-done.10
  40.9 3.6 %states.1 = f32[128,72,128]{2,1,0:T(8,128)S(1)} custom-call(bf16[128,4096]{1,0:T(8,128)(2,1)S(1)} %copy-done, bf16[128,4096]{1,0:T(8,128)(2,1)S(1)} %copy-done.2, bf16[128,512]{1,0:T(8,128)(2,1)S(1)} %copy-done.8, bf16[128,512]{1,0:T(8,128)(2,1)S(1)} %copy-done.10, f32[4,128,16]{2,1,0:T(8,128)S(1)} %get-tuple-element.19.tail_ref, ...), custom_call_target="tpu_custom_call" | custom-call | flops 536870912 | bytes 7000000 | tf_op jit(solution)/shard_map/states/pallas_call | solution.py:154
  44.5 0.3 convert_element_type.16
  44.8 118.2 %all_to_all.15 = f16[128,72,128]{2,1,0:T(8,128)(2,1)S(1)} all-to-all(f16[128,72,128]{2,1,0:T(8,128)(2,1)S(1)} %convert_element_type.16), channel_id=1, replica_groups=mesh['far'=4,'near'=8,'head'=16] {'near','head'}, dimensions={0} | all-to-all | bytes 4718592 | tf_op jit(solution)/shard_map/all_to_all | solution.py:427
  163.0 0.3 convert_element_type.17.pay_ref
  163.3 0.9 totals.1
  164.2 0.7 collective-permute-start.5
  164.9 1.3 collective-permute-start.4
  166.2 3.1 collective-permute-start.3
  169.3 0.7 collective-permute-start.2
  169.9 6.1 %collective-permute-start.1 = (f32[40,128]{1,0:T(8,128)S(1)}, f32[40,128]{1,0:T(8,128)S(1)}, u32[]{:S(2)}, u32[]{:S(2)}) collective-permute-start(f32[40,128]{1,0:T(8,128)S(1)} %get-tuple-element.53), channel_id=1, source_target_pairs={{0,256},{128,384},{1,257},{129,385},{2,258},{130,386},{3,259},{131... | collective-permute-start | bytes 61448 | tf_op jit(solution)/shard_map/ppermute | solution.py:247
  176.0 1.9 collective-permute-start
  178.0 3.7 %collective-permute-done = f32[40,128]{1,0:T(8,128)S(1)} collective-permute-done((f32[40,128]{1,0:T(8,128)S(1)}, f32[40,128]{1,0:T(8,128)S(1)}, u32[]{:S(2)}, u32[]{:S(2)}) %collective-permute-start) | collective-permute-done | bytes 20512 | tf_op jit(solution)/shard_map/ppermute | solution.py:247
  181.8 2.0 entering.1
  183.8 1.7 convert_element_type.18
  185.6 7.4 %all-to-all-start.2 = ((f16[128,72,128]{2,1,0:T(8,128)(2,1)}), f16[128,72,128]{2,1,0:T(8,128)(2,1)}, u32[]{:S(2)}, u32[]{:S(2)}) async-start(f16[128,72,128]{2,1,0:T(8,128)(2,1)} %convert_element_type.18), calls=%async_computation.2 | async-start | bytes 4718592 | tf_op jit(solution)/shard_map/all_to_all | solution.py:427
  193.0 0.7 broadcast_in_dim.29
  193.7 0.8 broadcast_in_dim.30
  194.6 0.9 copy-done.21
  195.5 8.0 %inner.1 = (f32[128,4096]{1,0:T(8,128)S(1)}, f32[128,4096]{1,0:T(8,128)S(1)}, f32[128,512]{1,0:T(8,128)S(1)}, f32[128,512]{1,0:T(8,128)S(1)}, f32[4,128,16]{2,1,0:T(8,128)S(1)}, /*index=5*/f32[4,128,16]{2,1,0:T(8,128)S(1)}) custom-call(bf16[128,4096]{1,0:T(8,128)(2,1)S(1)} %copy-done.1, bf16[128,4096]{1,0:T(8,128)(2,1)S(1)} %copy-done.3, ...), custom_call_target="tpu_custom_call" | custom-call | flops 20000000000 | bytes 8000000 | tf_op jit(solution)/shard_map/inner/pallas_call | solution.py:306
  203.6 1.4 copy-done.4
  205.0 1.4 copy-done.6
  206.3 0.7 copy-done.12
  207.0 0.7 copy-done.14
  207.7 0.7 copy-done.16
  208.4 0.7 copy-done.18
  209.1 95.7 %all-to-all-done.2 = f16[128,72,128]{2,1,0:T(8,128)(2,1)} async-done(((f16[128,72,128]{2,1,0:T(8,128)(2,1)}), f16[128,72,128]{2,1,0:T(8,128)(2,1)}, u32[]{:S(2)}, u32[]{:S(2)}) %all-to-all-start.2) | async-done | bytes 2359328 | tf_op jit(solution)/shard_map/all_to_all | solution.py:427
  304.8 2.1 convert_element_type.19.pay_ref
  307.0 0.1 copy-done.5
  307.1 0.6 copy-done.7
  307.7 0.1 copy-done.15
  307.8 0.1 copy-done.17
  307.9 0.1 copy-done.19
  308.0 9.2 %finish.1 = (bf16[128,4096]{1,0:T(8,128)(2,1)}, bf16[128,4096]{1,0:T(8,128)(2,1)}, bf16[128,64]{1,0:T(8,128)(2,1)S(1)}, bf16[128,512]{1,0:T(8,128)(2,1)}, bf16[128,512]{1,0:T(8,128)(2,1)}) custom-call(f32[128,72,128]{2,1,0:T(8,128)S(1)} %convert_element_type.19.pay_ref, bf16[128,4096]{1,0:T(8,128)(2,1)S(1)} %copy-done.1, bf16[128,4096]{1,0:T(8,128)(2,1)S(1)} %copy-done.3, ...), custom_call_target="tpu_custom_call" | custom-call | flops 1342177280 | bytes 14000000 | tf_op jit(solution)/shard_map/finish/pallas_call | solution.py:400
  317.2 0.7 copy.23
  (51 shorter events, 0.2 us)
Async XLA Ops:
  2.5 32.8 %all-to-all-start = ((f32[16,8,128]{2,1,0:T(8,128)}), f32[16,8,128]{2,1,0:T(8,128)S(1)}, u32[]{:S(2)}, u32[]{:S(2)}) async-start(f32[16,8,128]{2,1,0:T(8,128)} %broadcast_in_dim.27), calls=%async_computation | async-start | bytes 131072 | tf_op jit(solution)/shard_map/all_to_all | solution.py:437
  35.9 0.7 copy-start.20
  36.6 1.2 copy-start
  37.8 1.2 copy-start.2
  39.1 0.9 copy-start.8
  40.0 0.9 copy-start.10
  164.2 11.8 %collective-permute-start.5 = (f32[40,128]{1,0:T(8,128)S(1)}, f32[40,128]{1,0:T(8,128)S(1)}, u32[]{:S(2)}, u32[]{:S(2)}) collective-permute-start(f32[40,128]{1,0:T(8,128)S(1)} %get-tuple-element.52), channel_id=1, source_target_pairs={{384,0},{385,1},{386,2},{387,3},{388,4},{389,5},{390,6},{391,7},{3... | collective-permute-start | bytes 61448 | tf_op jit(solution)/shard_map/ppermute | solution.py:247
  164.9 13.1 %collective-permute-start.4 = (f32[40,128]{1,0:T(8,128)S(1)}, f32[40,128]{1,0:T(8,128)S(1)}, u32[]{:S(2)}, u32[]{:S(2)}) collective-permute-start(f32[40,128]{1,0:T(8,128)S(1)} %get-tuple-element.52), channel_id=1, source_target_pairs={{256,0},{384,128},{257,1},{385,129},{258,2},{386,130},{259,3},{387... | collective-permute-start | bytes 61448 | tf_op jit(solution)/shard_map/ppermute | solution.py:247
  166.2 11.8 %collective-permute-start.3 = (f32[40,128]{1,0:T(8,128)S(1)}, f32[40,128]{1,0:T(8,128)S(1)}, u32[]{:S(2)}, u32[]{:S(2)}) collective-permute-start(f32[40,128]{1,0:T(8,128)S(1)} %get-tuple-element.52), channel_id=1, source_target_pairs={{128,0},{256,128},{384,256},{129,1},{257,129},{385,257},{130,2},{2... | collective-permute-start | bytes 61448 | tf_op jit(solution)/shard_map/ppermute | solution.py:247
  169.3 8.7 %collective-permute-start.2 = (f32[40,128]{1,0:T(8,128)S(1)}, f32[40,128]{1,0:T(8,128)S(1)}, u32[]{:S(2)}, u32[]{:S(2)}) collective-permute-start(f32[40,128]{1,0:T(8,128)S(1)} %get-tuple-element.53), channel_id=1, source_target_pairs={{0,384},{1,385},{2,386},{3,387},{4,388},{5,389},{6,390},{7,391},{8... | collective-permute-start | bytes 61448 | tf_op jit(solution)/shard_map/ppermute | solution.py:247
  169.9 8.1 %collective-permute-start.1 = (f32[40,128]{1,0:T(8,128)S(1)}, f32[40,128]{1,0:T(8,128)S(1)}, u32[]{:S(2)}, u32[]{:S(2)}) collective-permute-start(f32[40,128]{1,0:T(8,128)S(1)} %get-tuple-element.53), channel_id=1, source_target_pairs={{0,256},{128,384},{1,257},{129,385},{2,258},{130,386},{3,259},{131... | collective-permute-start | bytes 61448 | tf_op jit(solution)/shard_map/ppermute | solution.py:247
  176.0 5.7 %collective-permute-start = (f32[40,128]{1,0:T(8,128)S(1)}, f32[40,128]{1,0:T(8,128)S(1)}, u32[]{:S(2)}, u32[]{:S(2)}) collective-permute-start(f32[40,128]{1,0:T(8,128)S(1)} %get-tuple-element.53), channel_id=1, source_target_pairs={{0,128},{128,256},{256,384},{1,129},{129,257},{257,385},{2,130},{1... | collective-permute-start | bytes 61448 | tf_op jit(solution)/shard_map/ppermute | solution.py:247
  185.6 9.0 %copy-start.1 = (bf16[128,4096]{1,0:T(8,128)(2,1)S(1)}, bf16[128,4096]{1,0:T(8,128)(2,1)}, u32[]{:S(2)}) copy-start(bf16[128,4096]{1,0:T(8,128)(2,1)} %x_ref.5) | copy-start | bytes 3145732
  185.6 9.0 %copy-start.3 = (bf16[128,4096]{1,0:T(8,128)(2,1)S(1)}, bf16[128,4096]{1,0:T(8,128)(2,1)}, u32[]{:S(2)}) copy-start(bf16[128,4096]{1,0:T(8,128)(2,1)} %w_ref.5) | copy-start | bytes 3145732
  185.6 9.0 %copy-start.9 = (bf16[128,512]{1,0:T(8,128)(2,1)S(1)}, bf16[128,512]{1,0:T(8,128)(2,1)}, u32[]{:S(2)}) copy-start(bf16[128,512]{1,0:T(8,128)(2,1)} %b_ref.5) | copy-start | bytes 393220
  185.6 9.0 %copy-start.11 = (bf16[128,512]{1,0:T(8,128)(2,1)S(1)}, bf16[128,512]{1,0:T(8,128)(2,1)}, u32[]{:S(2)}) copy-start(bf16[128,512]{1,0:T(8,128)(2,1)} %c_ref.5) | copy-start | bytes 393220
  185.6 119.2 %all-to-all-start.2 = ((f16[128,72,128]{2,1,0:T(8,128)(2,1)}), f16[128,72,128]{2,1,0:T(8,128)(2,1)}, u32[]{:S(2)}, u32[]{:S(2)}) async-start(f16[128,72,128]{2,1,0:T(8,128)(2,1)} %convert_element_type.18), calls=%async_computation.2 | async-start | bytes 4718592 | tf_op jit(solution)/shard_map/all_to_all | solution.py:427
  194.6 1.0 copy-start.21
  203.6 1.4 copy-start.4
  205.0 1.4 copy-start.6
  206.3 0.7 copy-start.12
  207.0 0.7 copy-start.14
  207.7 0.7 copy-start.16
  208.4 0.7 copy-start.18
  304.8 2.3 copy-start.5
  304.8 2.9 copy-start.7
  304.8 2.9 copy-start.13
  304.8 3.0 copy-start.15
  304.8 3.1 copy-start.17
  304.8 3.1 copy-start.19

commit v3 on v2

--- a/solution.py
+++ b/solution.py
@@ -11,8 +11,9 @@
 HEADDIM = 64
 STATE = 128
 LANES = 128
+BITS = 10.0
 TOP = 13.0
-CUT = -65000.0
+CUT = -1000.0
 F32 = jnp.float32
 BF16 = jnp.bfloat16
 PRECISE = lax.Precision.HIGHEST
@@ -52,7 +53,7 @@
 
 
 def exponent_of(block):
-    top = jnp.max(jnp.abs(block), axis=0, keepdims=True)
+    top = jnp.max(jnp.max(jnp.abs(block), axis=0, keepdims=True), axis=1, keepdims=True)
     return jnp.clip(jnp.floor(jnp.log(jnp.maximum(top, 1e-30)) * 1.4426950408889634), -90.0, 40.0)
 
 
@@ -79,12 +80,9 @@
     linked = (doc_col == doc_row) & (iota(shape, 0) >= iota(shape, 1))
     bias_ref[...] = jnp.where(linked, 0.0, -1e30)
     turned = (running - jnp.log(sizes)).T
-    through = jnp.where(doc_last == 0.0, last * 128.0, CUT)
-    high = through.astype(BF16).astype(F32)
-    mid = (through - high).astype(BF16).astype(F32)
-    low = (through - high - mid).astype(BF16).astype(F32)
-    keep = jnp.exp((high + mid + low) * (1.0 / 128.0))
-    edge = jnp.concatenate([high, mid, low, jnp.zeros_like(keep), keep, decay, decay, decay], axis=0)
+    through = jnp.where(doc_last == 0.0, last, CUT)
+    keep = jnp.exp(through)
+    edge = jnp.concatenate([through, keep, decay] + [decay] * 5, axis=0)
     for g in range(GROUPS):
         mine = slice(g * per, (g + 1) * per)
         size_ref[g] = sizes[:, mine]
@@ -123,135 +121,129 @@
     return dot(jnp.concatenate([proj, proj], axis=0), jnp.concatenate([high, low], axis=0), ((0,), (0,)))
 
 
-def state_kernel(x_ref, w_ref, b_ref, c_ref, tail_ref, reach_ref, edge_ref, out_ref):
-    forth = state_of(x_ref, b_ref, tail_ref)
-    back = state_of(w_ref, c_ref, reach_ref)
-    pieces = dot(edge_ref[0].astype(BF16), spread_map(tail_ref.shape[2], BF16))
+def state_kernel(x_ref, w_ref, b_ref, c_ref, tail_ref, reach_ref, out_ref, power_ref):
     messages, rows, _ = out_ref.shape
-    part = (rows - 8) // 2
+    part = rows // 2
     fold = STATE // part
     row = iota((8, LANES), 0)
-    for k in range(messages):
-        lanes = slice(k // fold * LANES, (k // fold + 1) * LANES)
-        here = slice(k % fold * part, (k % fold + 1) * part)
-        aux = jnp.where(row < 3, pieces[:, lanes], 0.0)
-        for which, state in enumerate((forth, back)):
-            block = state[here, lanes]
-            power = exponent_of(block)
-            out_ref[k, which * part : (which + 1) * part] = block * jnp.exp2(TOP - power)
-            aux = jnp.where(row == 3 + which, power, aux)
-        out_ref[k, 2 * part :] = aux
-
-
-def states(x, w, b, c, tail, reach, edge, parts):
+    powers = jnp.zeros((8, LANES), F32)
+    for which, state in enumerate((state_of(x_ref, b_ref, tail_ref), state_of(w_ref, c_ref, reach_ref))):
+        power = exponent_of(state)
+        powers = jnp.where(row == which, jnp.broadcast_to(power, powers.shape), powers)
+        state = state * jnp.exp2(TOP - power)
+        for k in range(messages):
+            lanes = slice(k // fold * LANES, (k // fold + 1) * LANES)
+            here = slice(k % fold * part, (k % fold + 1) * part)
+            out_ref[k, which * part : (which + 1) * part] = state[here, lanes]
+    power_ref[0] = powers
+
+
+def states(x, w, b, c, tail, reach, parts):
     tokens, channels = x.shape
     wide = channels // GROUPS
     per = tail.shape[2]
-    rows = 2 * STATE * channels // (parts * LANES) + 8
+    rows = 2 * STATE * channels // (parts * LANES)
     values = pl.BlockSpec((tokens, wide), lambda g: (0, g))
     proj = pl.BlockSpec((tokens, STATE), lambda g: (0, g))
     small = pl.BlockSpec((1, tokens, per), lambda g: (g, 0, 0))
     return pl.pallas_call(
         state_kernel,
         grid=(GROUPS,),
-        in_specs=[values, values, proj, proj, small, small, pl.BlockSpec((1, 8, per), lambda g: (g, 0, 0))],
-        out_specs=pl.BlockSpec((parts // GROUPS, rows, LANES), lambda g: (g, 0, 0)),
-        out_shape=jax.ShapeDtypeStruct((parts, rows, LANES), F32),
+        in_specs=[values, values, proj, proj, small, small],
+        out_specs=[
+            pl.BlockSpec((parts // GROUPS, rows, LANES), lambda g: (g, 0, 0)),
+            pl.BlockSpec((1, 8, LANES), lambda g: (g, 0, 0)),
+        ],
+        out_shape=[
+            jax.ShapeDtypeStruct((parts, rows, LANES), F32),
+            jax.ShapeDtypeStruct((GROUPS, 8, LANES), F32),
+        ],
         compiler_params=PARAMS,
         cost_estimate=pl.CostEstimate(flops=8 * tokens * STATE * channels, bytes_accessed=7000000, transcendentals=0),
         name="states",
-    )(x, w, b, c, tail, reach, edge)
-
-
-def keep_row(pay_ref, i, part):
-    side = pay_ref[i, 2 * part :]
-    return jnp.exp((side[0:1] + side[1:2] + side[2:3]) * (1.0 / 128.0))
-
-
-def unscaled(pay_ref, i, part, which):
-    power = pay_ref[i, 2 * part :][3 + which : 4 + which]
-    return pay_ref[i, which * part : (which + 1) * part] * jnp.exp2(power - TOP)
-
-
-def total_kernel(pay_ref, out_ref):
+    )(x, w, b, c, tail, reach)
+
+
+def block_of(pay_ref, side_ref, i, which):
+    part = pay_ref.shape[1] // 2
+    return pay_ref[i, which * part : (which + 1) * part] * side_ref[1 + which, pl.ds(i, 1)]
+
+
+def total_kernel(pay_ref, side_ref, most_ref, out_ref):
     blocks, rows, _ = pay_ref.shape
-    part = (rows - 8) // 2
+    part = rows // 2
 
     def step(k, carry):
         forth, back, through = carry
-        forth = keep_row(pay_ref, k, part) * forth + unscaled(pay_ref, k, part, 0)
         late = blocks - 1 - k
-        keep = keep_row(pay_ref, late, part)
-        return forth, unscaled(pay_ref, late, part, 1) + keep * back, through * keep
+        keep, keep_late = side_ref[0, pl.ds(k, 1)], side_ref[0, pl.ds(late, 1)]
+        forth = keep * forth + block_of(pay_ref, side_ref, k, 0)
+        back = keep_late * back + block_of(pay_ref, side_ref, late, 1)
+        return forth, back, through * keep
 
     zero = jnp.zeros((part, LANES), F32)
     forth, back, through = lax.fori_loop(0, blocks, step, (zero, zero, jnp.ones((1, LANES), F32)), unroll=8)
+    row = iota((8, LANES), 0)
+    side = jnp.where(row == 0, through, most_ref[...])
     for which, state in enumerate((forth, back)):
         out_ref[which, 0:part] = state
-        out_ref[which, part:] = jnp.broadcast_to(through, (8, LANES))
-
-
-def totals(pay):
-    _, rows, _ = pay.shape
-    part = (rows - 8) // 2
+        out_ref[which, part:] = side
+
+
+def totals(pay, side, most):
+    part = pay.shape[1] // 2
     return pl.pallas_call(
         total_kernel,
         out_shape=jax.ShapeDtypeStruct((2, part + 8, LANES), F32),
         compiler_params=PARAMS,
         cost_estimate=pl.CostEstimate(flops=2 * pay.size, bytes_accessed=4 * pay.size, transcendentals=0),
         name="totals",
-    )(pay)
-
-
-def enter_kernel(pay_ref, forth_ref, back_ref, out_ref):
+    )(pay, side, most)
+
+
+def enter_kernel(pay_ref, side_ref, own_ref, far_ref, mask_ref, out_ref, most_ref):
     blocks, rows, _ = pay_ref.shape
-    part = (rows - 8) // 2
-    row = iota((8, LANES), 0)
-
-    def put(i, which, state):
-        power = exponent_of(state)
-        out_ref[i, which * part : (which + 1) * part] = state * jnp.exp2(TOP - power)
-        return power
+    part = rows // 2
+    others = far_ref.shape[0]
+    most = own_ref[0, part:]
+    for k in range(others):
+        most = jnp.maximum(most, far_ref[k, 0, part:])
+    most_ref[...] = most
+    starts = []
+    for which in range(2):
+        state = jnp.zeros((part, LANES), F32)
+        for by in range(others, 0, -1):
+            k = by - 1 if which == 0 else others - by
+            far = far_ref[k, which]
+            valid = mask_ref[which * others + by - 1 : which * others + by] > 0.0
+            state = jnp.where(valid, far[0:part] + far[part : part + 1] * state, state)
+        starts.append(state)
+    scales = []
+    for which in range(2):
+        mine = mask_ref[2 * others + which : 2 * others + which + 1]
+        power = jnp.sum(most[1:2] * mine, axis=1, keepdims=True)
+        scales.append(jnp.exp2(TOP + 2.0 - BITS - power))
 
     def step(k, carry):
         forth, back = carry
         late = blocks - 1 - k
-        out_ref[k, 2 * part :] = jnp.where(row == 3, put(k, 0, forth), out_ref[k, 2 * part :])
-        out_ref[late, 2 * part :] = jnp.where(row == 4, put(late, 1, back), out_ref[late, 2 * part :])
-        forth = keep_row(pay_ref, k, part) * forth + unscaled(pay_ref, k, part, 0)
-        back = keep_row(pay_ref, late, part) * back + unscaled(pay_ref, late, part, 1)
+        out_ref[k, 0:part] = forth * scales[0]
+        out_ref[late, part:] = back * scales[1]
+        forth = side_ref[0, pl.ds(k, 1)] * forth + block_of(pay_ref, side_ref, k, 0)
+        back = side_ref[0, pl.ds(late, 1)] * back + block_of(pay_ref, side_ref, late, 1)
         return forth, back
 
-    out_ref[:, 2 * part :, :] = jnp.zeros((blocks, 8, LANES), F32)
-    lax.fori_loop(0, blocks, step, (forth_ref[0:part], back_ref[0:part]), unroll=8)
-
-
-def entering(pay, forth, back):
+    lax.fori_loop(0, blocks, step, tuple(starts), unroll=8)
+
+
+def entering(pay, side, own, far, mask):
     return pl.pallas_call(
         enter_kernel,
-        out_shape=jax.ShapeDtypeStruct(pay.shape, F32),
+        out_shape=[jax.ShapeDtypeStruct(pay.shape, F32), jax.ShapeDtypeStruct((8, LANES), F32)],
         compiler_params=PARAMS,
         cost_estimate=pl.CostEstimate(flops=4 * pay.size, bytes_accessed=8 * pay.size, transcendentals=0),
         name="entering",
-    )(pay, forth, back)
-
-
-def carried_in(total, reverse):
-    count = lax.axis_size("far")
-
-    def moved(by):
-        if reverse:
-            pairs = [(s, s - by) for s in range(by, count)]
-        else:
-            pairs = [(s, s + by) for s in range(count - by)]
-        return lax.ppermute(total, "far", pairs)
-
-    def joined(near, far):
-        through = near[-8:]
-        state = near[:-8] + through[0:1] * far[:-8]
-        return jnp.concatenate([state, through * far[-8:]], axis=0)
-
-    return functools.reduce(joined, [moved(by) for by in range(1, count)])
+    )(pay, side, own, far, mask)
 
 
 def inner_kernel(x_ref, w_ref, b_ref, c_ref, run_ref, runt_ref, bias_ref, skip_ref, y_ref, gx_ref, gb_ref, gc_ref, col_ref, diff_ref):
@@ -331,14 +323,18 @@
     )(x, w, b, c, run, runt, bias, skip)
 
 
-def state_from(pay_ref, which):
+def state_from(pay_ref, most_ref, group, which):
     messages, rows, _ = pay_ref.shape
-    part = (rows - 8) // 2
+    part = rows // 2
     fold = STATE // part
+    here = slice(which * part, (which + 1) * part)
+    most = most_ref[1:2]
+    mine = iota(most.shape, 1) == which * GROUPS + group
+    power = jnp.sum(jnp.where(mine, most, 0.0), axis=1, keepdims=True)
     columns = []
     for first in range(0, messages, fold):
-        columns.append(jnp.concatenate([unscaled(pay_ref, first + k, part, which) for k in range(fold)], axis=0))
-    return jnp.concatenate(columns, axis=1)
+        columns.append(jnp.concatenate([pay_ref[first + k, here] for k in range(fold)], axis=0))
+    return jnp.concatenate(columns, axis=1) * jnp.exp2(power - (TOP + 2.0 - BITS))
 
 
 def carried_terms(state, values, scale_ref, proj_ref):
@@ -353,13 +349,13 @@
 
 
 def finish_kernel(
-    pay_ref, x_ref, w_ref, b_ref, c_ref, tail_ref, reach_ref, y_ref, gx_ref, gb_ref, gc_ref, col_ref, diff_ref, size_ref, sig_ref, edge_ref,
+    pay_ref, most_ref, x_ref, w_ref, b_ref, c_ref, tail_ref, reach_ref, y_ref, gx_ref, gb_ref, gc_ref, col_ref, diff_ref, size_ref, sig_ref, edge_ref,
     mixed_ref, gradx_ref, dt_ref, gradb_ref, gradc_ref, all_ref,
 ):
     g = pl.program_id(0)
     tokens, _ = x_ref.shape
     per = tail_ref.shape[2]
-    enter, leave = state_from(pay_ref, 0), state_from(pay_ref, 1)
+    enter, leave = state_from(pay_ref, most_ref, g, 0), state_from(pay_ref, most_ref, g, 1)
     terms, grad, rows = carried_terms(enter, w_ref[...].astype(F32), reach_ref, c_ref)
     mixed_ref[...] = (y_ref[...] + terms).astype(BF16)
     gradc_ref[...] = (gc_ref[...] + grad).astype(BF16)
@@ -369,7 +365,7 @@
     met = jnp.sum(enter * leave, axis=0, keepdims=True)
     met = head_sums(jnp.broadcast_to(met, (8, met.shape[1])))[0:1]
     edge = edge_ref[0]
-    keep, decay = edge[4:5], edge[5:6]
+    keep, decay = edge[1:2], edge[2:3]
     shape = (tokens, tokens)
     from_here = (iota(shape, 0) <= iota(shape, 1)).astype(F32)
     before = (iota(shape, 0) > iota(shape, 1)).astype(F32)
@@ -389,7 +385,7 @@
     dt_ref[...] = all_ref[...].astype(BF16)
 
 
-def finish(pay, x, w, b, c, tail, reach, y, gx, gb, gc, col, diff, size, sig, edge):
+def finish(pay, most, x, w, b, c, tail, reach, y, gx, gb, gc, col, diff, size, sig, edge):
     tokens, channels = x.shape
     parts, rows, _ = pay.shape
     wide = channels // GROUPS
@@ -402,6 +398,7 @@
         grid=(GROUPS,),
         in_specs=[
             pl.BlockSpec((parts // GROUPS, rows, LANES), lambda g: (g, 0, 0)),
+            pl.BlockSpec((8, LANES), lambda g: (0, 0)),
             values, values, proj, proj, small, small, values, values, proj, proj, small, small, small, small,
             pl.BlockSpec((1, 8, per), lambda g: (g, 0, 0)),
         ],
@@ -417,7 +414,7 @@
         compiler_params=PARAMS,
         cost_estimate=pl.CostEstimate(flops=20 * tokens * STATE * channels, bytes_accessed=14_000_000, transcendentals=0),
         name="finish",
-    )(pay, x, w, b, c, tail, reach, y, gx, gb, gc, col, diff, size, sig, edge)
+    )(pay, most, x, w, b, c, tail, reach, y, gx, gb, gc, col, diff, size, sig, edge)
 
 
 GROUP = ("near", "head")
@@ -435,6 +432,26 @@
     whole = jnp.where(iota((8, 128), 1) // per_dev == mine, jnp.tile(own, (1, 128 // per_dev)), 0.0)
     whole = jnp.broadcast_to(whole[None], (parts, 8, 128))
     return lax.all_to_all(whole, "head", split_axis=0, concat_axis=0, tiled=True).sum(axis=0)[:, :heads]
+
+
+def around(value, axis, stride, count):
+    size = lax.axis_size(axis)
+    digit = lax.axis_index(axis) // stride % count
+    place = iota((count,) + (1,) * value.ndim, 0)
+    whole = jnp.where(place == digit, value[None], 0.0)
+    for k in range(1, count):
+        pairs = [(p, p + ((p // stride + k) % count - p // stride % count) * stride) for p in range(size)]
+        came = lax.ppermute(value, axis, pairs)
+        whole = whole + jnp.where(place == (digit - k) % count, came[None], 0.0)
+    return whole
+
+
+def known_around(edge, powers, heads):
+    own = jnp.concatenate([edge[:, 0].reshape(1, heads), powers[:, 0:2, 0].T.reshape(1, 2 * GROUPS)], axis=1)
+    own = jnp.pad(own, ((0, 0), (0, LANES - own.shape[1])))
+    table = around(own[0], "head", 1, 4)
+    table = around(table, "head", 4, lax.axis_size("head") // 4).reshape(-1, LANES)
+    return around(table, "near", 1, lax.axis_size("near")).reshape(-1, LANES)
 
 
 def per_device(features, dt_raw, b_proj, c_proj, cotangent, starts, a_log, dt_bias, d_skip):
@@ -445,12 +462,27 @@
     marks = jnp.broadcast_to(marks[None], (8, tokens))
     skip = jnp.broadcast_to(jnp.repeat(params[2], HEADDIM)[None], (8, heads * HEADDIM))
     size, sig, run, runt, reach, tail, bias, edge = prep(dt_raw, params, marks)
-    came = exchanged(states(features, cotangent, b_proj, c_proj, tail, reach, edge, parts))
+    sent, powers = states(features, cotangent, b_proj, c_proj, tail, reach, parts)
+    came = exchanged(sent)
+    table = known_around(edge, powers, heads)
     y, gx, gb, gc, col, diff = inner(features, cotangent, b_proj, c_proj, run, runt, bias, skip)
-    total = totals(came)
-    back = exchanged(entering(came, carried_in(total[0], False), carried_in(total[1], True)))
+    pair = lax.axis_index(GROUP) // (parts * 2 // heads)
+    group = pair // (heads // 2 // GROUPS)
+    decays = lax.dynamic_slice(table, (0, 2 * pair), (parts, 2))
+    column = lambda at: lax.dynamic_slice(table, (0, at), (parts, 1))
+    scales = [jnp.broadcast_to(jnp.exp2(column(heads + k * GROUPS + group) - TOP), (parts, LANES)) for k in range(2)]
+    side = jnp.stack([jnp.repeat(jnp.exp(decays), HEADDIM, axis=1)] + scales)
+    most = jnp.pad(jnp.max(table[:, heads : heads + 2 * GROUPS], axis=0), (0, LANES - 2 * GROUPS))
+    total = totals(came, side, jnp.broadcast_to(most[None], (8, LANES)))
+    count, here = lax.axis_size("far"), lax.axis_index("far")
+    far = [lax.ppermute(total, "far", [(p, (p + by) % count) for p in range(count)]) for by in range(1, count)]
+    lane = jnp.arange(LANES)
+    mask = [jnp.full((LANES,), here - by >= 0) for by in range(1, count)]
+    mask += [jnp.full((LANES,), here + by < count) for by in range(1, count)]
+    mask += [lane == group, lane == GROUPS + group]
+    left, most = entering(came, side, total, jnp.stack(far), jnp.stack(mask).astype(F32))
     return finish(
-        back, features, cotangent, b_proj, c_proj, tail, reach, y, gx, gb, gc, col, diff, size, sig, edge
+        exchanged(left), most, features, cotangent, b_proj, c_proj, tail, reach, y, gx, gb, gc, col, diff, size, sig, edge
     )
 
 

time: 319 us -> 338 us (1.060)
  the two profiles are of different devices: /device:TPU:2 before, /device:TPU:8 now
where the time goes in v3:
time: 338 us; the launch traced here: 337 us
  waiting for transfers between devices  180 us (53%)
  starting transfers between devices  98.7 us (29%)
  local copies, waits for them, and re-layouts  23.4 us (7%)
  Pallas kernels  23.3 us (7%)
  other arithmetic  9.56 us (3%)
    all_to_all x2, waiting for transfers between devices, exchanged(): lax.all_to_all(messages.astype(jnp.float16), GROUP, split_axis=0, concat_...  84.8 us
    ppermute x13, waiting for transfers between devices, around(): came = lax.ppermute(value, axis, pairs)  79.2 us
    ppermute x13, starting transfers between devices, around(): came = lax.ppermute(value, axis, pairs)  54.2 us
    all_to_all x1, starting transfers between devices, gathered(): lax.all_to_all(whole, 'head', split_axis=0, concat_axis=0, tiled=True)  18.2 us
    unnamed x53, local copies, waits for them, and re-layouts  17.4 us
    all_to_all x2, starting transfers between devices, exchanged(): lax.all_to_all(messages.astype(jnp.float16), GROUP, split_axis=0, concat_...  16.2 us
    all_to_all x1, waiting for transfers between devices, gathered(): lax.all_to_all(whole, 'head', split_axis=0, concat_axis=0, tiled=True)  11.9 us
    ppermute x3, starting transfers between devices, per_device(): lax.ppermute(total, 'far', [(p, (p + by) % count) for p in range(count)])  10.2 us
  transfers between devices with their start and end apart: 19, of which 8 were waited for; matrix products, arithmetic and copies ran while one was open for 2% of the time, Pallas kernels for 2%

profile of v3, /device:TPU:8, one launch (start us, length us, event | category | flops | bytes accessed | tf_op | source)
XLA Modules:
  0.0 337.1 jit_solution(17238102023512613678)
XLA Ops:
  0.7 0.9 stack.40
  2.5 18.2 %all-to-all-start = ((f32[16,8,128]{2,1,0:T(8,128)}), f32[16,8,128]{2,1,0:T(8,128)S(1)}, u32[]{:S(2)}, u32[]{:S(2)}) async-start(f32[16,8,128]{2,1,0:T(8,128)} %broadcast_in_dim.325), calls=%async_computation | async-start | bytes 131072 | tf_op jit(solution)/shard_map/all_to_all | solution.py:434
  20.7 0.8 copy.41.dt_ref
  21.5 0.8 dynamic-slice_convert_fusion
  22.3 11.9 %all-to-all-done = f32[16,8,128]{2,1,0:T(8,128)S(1)} async-done(((f32[16,8,128]{2,1,0:T(8,128)}), f32[16,8,128]{2,1,0:T(8,128)S(1)}, u32[]{:S(2)}, u32[]{:S(2)}) %all-to-all-start) | async-done | bytes 65568 | tf_op jit(solution)/shard_map/all_to_all | solution.py:434
  35.5 1.2 copy-done.2
  36.7 1.2 copy-done.4
  37.9 0.9 copy-done.10
  38.8 0.9 copy-done.12
  39.7 3.9 %states.1 = (f32[128,64,128]{2,1,0:T(8,128)S(1)}, f32[4,8,128]{2,1,0:T(8,128)S(1)}) custom-call(bf16[128,4096]{1,0:T(8,128)(2,1)S(1)} %copy-done.2, bf16[128,4096]{1,0:T(8,128)(2,1)S(1)} %copy-done.4, bf16[128,512]{1,0:T(8,128)(2,1)S(1)} %copy-done.10, bf16[128,512]{1,0:T(8,128)(2,1)S(1)} %copy-done.12, f32[4,128,16]{2,1,0:T(8,128)S(1)} %get-tuple-element.23.tail_ref, ...), custom_call_target="tpu_custom_call" | custom-call | flops 536870912 | bytes 7000000 | tf_op jit(solution)/shard_map/states/pallas_call | solution.py:149
  43.6 1.9 convert_element_type.23
  45.5 7.9 %all-to-all-start.1 = ((f16[128,64,128]{2,1,0:T(8,128)(2,1)}), f16[128,64,128]{2,1,0:T(8,128)(2,1)}, u32[]{:S(2)}, u32[]{:S(2)}) async-start(f16[128,64,128]{2,1,0:T(8,128)(2,1)} %convert_element_type.23), calls=%async_computation.1 | async-start | bytes 4194304 | tf_op jit(solution)/shard_map/all_to_all | solution.py:424
  54.1 7.3 %collective-permute-start.2 = (f32[128]{0:T(128)S(1)}, f32[128]{0:T(128)S(1)}, u32[]{:S(2)}, u32[]{:S(2)}) collective-permute-start(f32[128]{0:T(128)S(1)} %fusion.6), channel_id=1, source_target_pairs={{0,3},{1,0},{2,1},{3,2},{4,7},{5,4},{6,5},{7,6},{8,11},{9,8},{10,9... | collective-permute-start | bytes 1544 | tf_op jit(solution)/shard_map/ppermute | solution.py:444
  61.4 7.3 %collective-permute-start.1 = (f32[128]{0:T(128)S(1)}, f32[128]{0:T(128)S(1)}, u32[]{:S(2)}, u32[]{:S(2)}) collective-permute-start(f32[128]{0:T(128)S(1)} %fusion.6), channel_id=1, source_target_pairs={{0,2},{1,3},{2,0},{3,1},{4,6},{5,7},{6,4},{7,5},{8,10},{9,11},{10,... | collective-permute-start | bytes 1544 | tf_op jit(solution)/shard_map/ppermute | solution.py:444
  68.7 7.3 %collective-permute-start = (f32[128]{0:T(128)S(1)}, f32[128]{0:T(128)S(1)}, u32[]{:S(2)}, u32[]{:S(2)}) collective-permute-start(f32[128]{0:T(128)S(1)} %fusion.6), channel_id=1, source_target_pairs={{0,1},{1,2},{2,3},{3,0},{4,5},{5,6},{6,7},{7,4},{8,9},{9,10},{10,1... | collective-permute-start | bytes 1544 | tf_op jit(solution)/shard_map/ppermute | solution.py:444
  76.0 68.0 %collective-permute-done.2 = f32[128]{0:T(128)S(1)} collective-permute-done((f32[128]{0:T(128)S(1)}, f32[128]{0:T(128)S(1)}, u32[]{:S(2)}, u32[]{:S(2)}) %collective-permute-start.2) | collective-permute-done | bytes 544 | tf_op jit(solution)/shard_map/ppermute | solution.py:444
  144.0 8.3 %collective-permute-done.1 = f32[128]{0:T(128)S(1)} collective-permute-done((f32[128]{0:T(128)S(1)}, f32[128]{0:T(128)S(1)}, u32[]{:S(2)}, u32[]{:S(2)}) %collective-permute-start.1) | collective-permute-done | bytes 544 | tf_op jit(solution)/shard_map/ppermute | solution.py:444
  152.4 2.4 collective-permute-start.5
  154.8 4.3 %collective-permute-start.4 = (f32[4,128]{1,0:T(4,128)S(1)}, f32[4,128]{1,0:T(4,128)S(1)}, u32[]{:S(2)}, u32[]{:S(2)}) collective-permute-start(f32[4,128]{1,0:T(4,128)S(1)} %select_add_fusion.2), channel_id=1, source_target_pairs={{0,8},{1,9},{2,10},{3,11},{4,12},{5,13},{6,14},{7,15},{8,0},{9,1},... | collective-permute-start | bytes 6152 | tf_op jit(solution)/shard_map/ppermute | solution.py:444
  159.1 4.3 %collective-permute-start.3 = (f32[4,128]{1,0:T(4,128)S(1)}, f32[4,128]{1,0:T(4,128)S(1)}, u32[]{:S(2)}, u32[]{:S(2)}) collective-permute-start(f32[4,128]{1,0:T(4,128)S(1)} %select_add_fusion.2), channel_id=1, source_target_pairs={{0,4},{1,5},{2,6},{3,7},{4,8},{5,9},{6,10},{7,11},{8,12},{9,13},{1... | collective-permute-start | bytes 6152 | tf_op jit(solution)/shard_map/ppermute | solution.py:444
  164.8 3.8 %collective-permute-start.7 = (f32[16,128]{1,0:T(8,128)S(1)}, f32[16,128]{1,0:T(8,128)S(1)}, u32[]{:S(2)}, u32[]{:S(2)}) collective-permute-start(f32[16,128]{1,0:T(8,128)S(1)} %select_add_fusion.1), channel_id=1, source_target_pairs={{0,32},{16,48},{32,64},{48,80},{64,96},{80,112},{96,0},{112,16},{1... | collective-permute-start | bytes 24584 | tf_op jit(solution)/shard_map/ppermute | solution.py:444
  168.6 1.9 collective-permute-start.6
  170.5 5.4 %collective-permute-start.12 = (f32[16,128]{1,0:T(8,128)S(1)}, f32[16,128]{1,0:T(8,128)S(1)}, u32[]{:S(2)}, u32[]{:S(2)}) collective-permute-start(f32[16,128]{1,0:T(8,128)S(1)} %select_add_fusion.1), channel_id=1, source_target_pairs={{0,112},{16,0},{32,16},{48,32},{64,48},{80,64},{96,80},{112,96},{1... | collective-permute-start | bytes 24584 | tf_op jit(solution)/shard_map/ppermute | solution.py:444
  176.0 2.1 collective-permute-start.11
  178.1 1.9 collective-permute-start.10
  180.0 4.4 %collective-permute-start.9 = (f32[16,128]{1,0:T(8,128)S(1)}, f32[16,128]{1,0:T(8,128)S(1)}, u32[]{:S(2)}, u32[]{:S(2)}) collective-permute-start(f32[16,128]{1,0:T(8,128)S(1)} %select_add_fusion.1), channel_id=1, source_target_pairs={{0,64},{16,80},{32,96},{48,112},{64,0},{80,16},{96,32},{112,48},{1... | collective-permute-start | bytes 24584 | tf_op jit(solution)/shard_map/ppermute | solution.py:444
  184.4 1.9 collective-permute-start.8
  188.1 2.2 collective-permute-done.8
  191.4 2.1 convert_element_type.24.pay_ref
  194.1 1.4 copy-done
  195.4 4.7 %collective-permute-start.15 = (f32[2,40,128]{2,1,0:T(8,128)S(1)}, f32[2,40,128]{2,1,0:T(8,128)S(1)}, u32[]{:S(2)}, u32[]{:S(2)}) collective-permute-start(f32[2,40,128]{2,1,0:T(8,128)S(1)} %totals.1.own_ref), channel_id=1, source_target_pairs={{0,384},{128,0},{256,128},{384,256},{1,385},{129,1},{257,129},{385... | collective-permute-start | bytes 122888 | tf_op jit(solution)/shard_map/ppermute | solution.py:478
  200.1 2.7 collective-permute-start.14
  202.8 2.8 collective-permute-start.13
  205.8 1.8 collective-permute-done.14
  207.6 2.7 collective-permute-done.13
  210.4 2.2 copy-done.1
  212.5 0.9 entering.1
  213.5 1.9 convert_element_type.26
  215.4 8.3 %all-to-all-start.2 = ((f16[128,64,128]{2,1,0:T(8,128)(2,1)}), f16[128,64,128]{2,1,0:T(8,128)(2,1)}, u32[]{:S(2)}, u32[]{:S(2)}) async-start(f16[128,64,128]{2,1,0:T(8,128)(2,1)} %convert_element_type.26), calls=%async_computation.2 | async-start | bytes 4194304 | tf_op jit(solution)/shard_map/all_to_all | solution.py:424
  223.9 0.9 copy-done.23
  224.8 0.8 copy-done.25
  225.6 8.1 %inner.1 = (f32[128,4096]{1,0:T(8,128)S(1)}, f32[128,4096]{1,0:T(8,128)S(1)}, f32[128,512]{1,0:T(8,128)S(1)}, f32[128,512]{1,0:T(8,128)S(1)}, f32[4,128,16]{2,1,0:T(8,128)S(1)}, /*index=5*/f32[4,128,16]{2,1,0:T(8,128)S(1)}) custom-call(bf16[128,4096]{1,0:T(8,128)(2,1)S(1)} %copy-done.3, bf16[128,4096]{1,0:T(8,128)(2,1)S(1)} %copy-done.5, ...), custom_call_target="tpu_custom_call" | custom-call | flops 20000000000 | bytes 8000000 | tf_op jit(solution)/shard_map/inner/pallas_call | solution.py:298
  233.7 1.3 copy-done.6
  235.0 1.4 copy-done.8
  237.8 0.7 copy-done.18
  239.2 84.8 %all-to-all-done.2 = f16[128,64,128]{2,1,0:T(8,128)(2,1)} async-done(((f16[128,64,128]{2,1,0:T(8,128)(2,1)}), f16[128,64,128]{2,1,0:T(8,128)(2,1)}, u32[]{:S(2)}, u32[]{:S(2)}) %all-to-all-start.2) | async-done | bytes 2097184 | tf_op jit(solution)/shard_map/all_to_all | solution.py:424
  324.1 2.2 convert_element_type.27.pay_ref
  327.1 9.3 %finish.1 = (bf16[128,4096]{1,0:T(8,128)(2,1)}, bf16[128,4096]{1,0:T(8,128)(2,1)}, bf16[128,64]{1,0:T(8,128)(2,1)S(1)}, bf16[128,512]{1,0:T(8,128)(2,1)}, bf16[128,512]{1,0:T(8,128)(2,1)}) custom-call(f32[128,64,128]{2,1,0:T(8,128)S(1)} %convert_element_type.27.pay_ref, f32[8,128]{1,0:T(8,128)S(1)} %get-tuple-element.29.most_ref, ...), custom_call_target="tpu_custom_call" | custom-call | flops 1342177280 | bytes 14000000 | tf_op jit(solution)/shard_map/finish/pallas_call | solution.py:396
  (156 shorter events, 11.1 us)
Async XLA Ops:
  2.5 31.7 %all-to-all-start = ((f32[16,8,128]{2,1,0:T(8,128)}), f32[16,8,128]{2,1,0:T(8,128)S(1)}, u32[]{:S(2)}, u32[]{:S(2)}) async-start(f32[16,8,128]{2,1,0:T(8,128)} %broadcast_in_dim.325), calls=%async_computation | async-start | bytes 131072 | tf_op jit(solution)/shard_map/all_to_all | solution.py:434
  34.8 0.7 copy-start.22
  35.5 10.0 %copy-start.24 = (f32[4,16,128]{2,1,0:T(8,128)}, f32[4,16,128]{2,1,0:T(8,128)S(1)}, u32[]{:S(2)}) copy-start(f32[4,16,128]{2,1,0:T(8,128)S(1)} %get-tuple-element.31.runt_ref) | copy-start | bytes 98308
  35.5 1.2 copy-start.2
  36.7 1.2 copy-start.4
  37.9 0.9 copy-start.10
  38.8 0.9 copy-start.12
  45.5 145.9 %all-to-all-start.1 = ((f16[128,64,128]{2,1,0:T(8,128)(2,1)}), f16[128,64,128]{2,1,0:T(8,128)(2,1)}, u32[]{:S(2)}, u32[]{:S(2)}) async-start(f16[128,64,128]{2,1,0:T(8,128)(2,1)} %convert_element_type.23), calls=%async_computation.1 | async-start | bytes 4194304 | tf_op jit(solution)/shard_map/all_to_all | solution.py:424
  54.1 89.9 %collective-permute-start.2 = (f32[128]{0:T(128)S(1)}, f32[128]{0:T(128)S(1)}, u32[]{:S(2)}, u32[]{:S(2)}) collective-permute-start(f32[128]{0:T(128)S(1)} %fusion.6), channel_id=1, source_target_pairs={{0,3},{1,0},{2,1},{3,2},{4,7},{5,4},{6,5},{7,6},{8,11},{9,8},{10,9... | collective-permute-start | bytes 1544 | tf_op jit(solution)/shard_map/ppermute | solution.py:444
  61.4 90.9 %collective-permute-start.1 = (f32[128]{0:T(128)S(1)}, f32[128]{0:T(128)S(1)}, u32[]{:S(2)}, u32[]{:S(2)}) collective-permute-start(f32[128]{0:T(128)S(1)} %fusion.6), channel_id=1, source_target_pairs={{0,2},{1,3},{2,0},{3,1},{4,6},{5,7},{6,4},{7,5},{8,10},{9,11},{10,... | collective-permute-start | bytes 1544 | tf_op jit(solution)/shard_map/ppermute | solution.py:444
  68.7 83.6 %collective-permute-start = (f32[128]{0:T(128)S(1)}, f32[128]{0:T(128)S(1)}, u32[]{:S(2)}, u32[]{:S(2)}) collective-permute-start(f32[128]{0:T(128)S(1)} %fusion.6), channel_id=1, source_target_pairs={{0,1},{1,2},{2,3},{3,0},{4,5},{5,6},{6,7},{7,4},{8,9},{9,10},{10,1... | collective-permute-start | bytes 1544 | tf_op jit(solution)/shard_map/ppermute | solution.py:444
  152.4 11.7 %collective-permute-start.5 = (f32[4,128]{1,0:T(4,128)S(1)}, f32[4,128]{1,0:T(4,128)S(1)}, u32[]{:S(2)}, u32[]{:S(2)}) collective-permute-start(f32[4,128]{1,0:T(4,128)S(1)} %select_add_fusion.2), channel_id=1, source_target_pairs={{0,12},{1,13},{2,14},{3,15},{4,0},{5,1},{6,2},{7,3},{8,4},{9,5},{1... | collective-permute-start | bytes 6152 | tf_op jit(solution)/shard_map/ppermute | solution.py:444
  154.8 9.3 %collective-permute-start.4 = (f32[4,128]{1,0:T(4,128)S(1)}, f32[4,128]{1,0:T(4,128)S(1)}, u32[]{:S(2)}, u32[]{:S(2)}) collective-permute-start(f32[4,128]{1,0:T(4,128)S(1)} %select_add_fusion.2), channel_id=1, source_target_pairs={{0,8},{1,9},{2,10},{3,11},{4,12},{5,13},{6,14},{7,15},{8,0},{9,1},... | collective-permute-start | bytes 6152 | tf_op jit(solution)/shard_map/ppermute | solution.py:444
  159.1 5.6 %collective-permute-start.3 = (f32[4,128]{1,0:T(4,128)S(1)}, f32[4,128]{1,0:T(4,128)S(1)}, u32[]{:S(2)}, u32[]{:S(2)}) collective-permute-start(f32[4,128]{1,0:T(4,128)S(1)} %select_add_fusion.2), channel_id=1, source_target_pairs={{0,4},{1,5},{2,6},{3,7},{4,8},{5,9},{6,10},{7,11},{8,12},{9,13},{1... | collective-permute-start | bytes 6152 | tf_op jit(solution)/shard_map/ppermute | solution.py:444
  164.8 15.2 %collective-permute-start.7 = (f32[16,128]{1,0:T(8,128)S(1)}, f32[16,128]{1,0:T(8,128)S(1)}, u32[]{:S(2)}, u32[]{:S(2)}) collective-permute-start(f32[16,128]{1,0:T(8,128)S(1)} %select_add_fusion.1), channel_id=1, source_target_pairs={{0,32},{16,48},{32,64},{48,80},{64,96},{80,112},{96,0},{112,16},{1... | collective-permute-start | bytes 24584 | tf_op jit(solution)/shard_map/ppermute | solution.py:444
  168.6 15.8 %collective-permute-start.6 = (f32[16,128]{1,0:T(8,128)S(1)}, f32[16,128]{1,0:T(8,128)S(1)}, u32[]{:S(2)}, u32[]{:S(2)}) collective-permute-start(f32[16,128]{1,0:T(8,128)S(1)} %select_add_fusion.1), channel_id=1, source_target_pairs={{0,16},{16,32},{32,48},{48,64},{64,80},{80,96},{96,112},{112,0},{1... | collective-permute-start | bytes 24584 | tf_op jit(solution)/shard_map/ppermute | solution.py:444
  170.5 20.2 %collective-permute-start.12 = (f32[16,128]{1,0:T(8,128)S(1)}, f32[16,128]{1,0:T(8,128)S(1)}, u32[]{:S(2)}, u32[]{:S(2)}) collective-permute-start(f32[16,128]{1,0:T(8,128)S(1)} %select_add_fusion.1), channel_id=1, source_target_pairs={{0,112},{16,0},{32,16},{48,32},{64,48},{80,64},{96,80},{112,96},{1... | collective-permute-start | bytes 24584 | tf_op jit(solution)/shard_map/ppermute | solution.py:444
  176.0 14.6 %collective-permute-start.11 = (f32[16,128]{1,0:T(8,128)S(1)}, f32[16,128]{1,0:T(8,128)S(1)}, u32[]{:S(2)}, u32[]{:S(2)}) collective-permute-start(f32[16,128]{1,0:T(8,128)S(1)} %select_add_fusion.1), channel_id=1, source_target_pairs={{0,96},{16,112},{32,0},{48,16},{64,32},{80,48},{96,64},{112,80},{1... | collective-permute-start | bytes 24584 | tf_op jit(solution)/shard_map/ppermute | solution.py:444
  178.1 12.4 %collective-permute-start.10 = (f32[16,128]{1,0:T(8,128)S(1)}, f32[16,128]{1,0:T(8,128)S(1)}, u32[]{:S(2)}, u32[]{:S(2)}) collective-permute-start(f32[16,128]{1,0:T(8,128)S(1)} %select_add_fusion.1), channel_id=1, source_target_pairs={{0,80},{16,96},{32,112},{48,0},{64,16},{80,32},{96,48},{112,64},{1... | collective-permute-start | bytes 24584 | tf_op jit(solution)/shard_map/ppermute | solution.py:444
  180.0 10.4 %collective-permute-start.9 = (f32[16,128]{1,0:T(8,128)S(1)}, f32[16,128]{1,0:T(8,128)S(1)}, u32[]{:S(2)}, u32[]{:S(2)}) collective-permute-start(f32[16,128]{1,0:T(8,128)S(1)} %select_add_fusion.1), channel_id=1, source_target_pairs={{0,64},{16,80},{32,96},{48,112},{64,0},{80,16},{96,32},{112,48},{1... | collective-permute-start | bytes 24584 | tf_op jit(solution)/shard_map/ppermute | solution.py:444
  184.4 5.9 %collective-permute-start.8 = (f32[16,128]{1,0:T(8,128)S(1)}, f32[16,128]{1,0:T(8,128)S(1)}, u32[]{:S(2)}, u32[]{:S(2)}) collective-permute-start(f32[16,128]{1,0:T(8,128)S(1)} %select_add_fusion.1), channel_id=1, source_target_pairs={{0,48},{16,64},{32,80},{48,96},{64,112},{80,0},{96,16},{112,32},{1... | collective-permute-start | bytes 24584 | tf_op jit(solution)/shard_map/ppermute | solution.py:444
  193.5 2.0 copy-start
  195.4 10.4 %collective-permute-start.15 = (f32[2,40,128]{2,1,0:T(8,128)S(1)}, f32[2,40,128]{2,1,0:T(8,128)S(1)}, u32[]{:S(2)}, u32[]{:S(2)}) collective-permute-start(f32[2,40,128]{2,1,0:T(8,128)S(1)} %totals.1.own_ref), channel_id=1, source_target_pairs={{0,384},{128,0},{256,128},{384,256},{1,385},{129,1},{257,129},{385... | collective-permute-start | bytes 122888 | tf_op jit(solution)/shard_map/ppermute | solution.py:478
  200.1 7.5 %collective-permute-start.14 = (f32[2,40,128]{2,1,0:T(8,128)S(1)}, f32[2,40,128]{2,1,0:T(8,128)S(1)}, u32[]{:S(2)}, u32[]{:S(2)}) collective-permute-start(f32[2,40,128]{2,1,0:T(8,128)S(1)} %totals.1.own_ref), channel_id=1, source_target_pairs={{0,256},{128,384},{256,0},{384,128},{1,257},{129,385},{257,1},{385... | collective-permute-start | bytes 122888 | tf_op jit(solution)/shard_map/ppermute | solution.py:478
  202.8 7.5 %collective-permute-start.13 = (f32[2,40,128]{2,1,0:T(8,128)S(1)}, f32[2,40,128]{2,1,0:T(8,128)S(1)}, u32[]{:S(2)}, u32[]{:S(2)}) collective-permute-start(f32[2,40,128]{2,1,0:T(8,128)S(1)} %totals.1.own_ref), channel_id=1, source_target_pairs={{0,128},{128,256},{256,384},{384,0},{1,129},{129,257},{257,385},{3... | collective-permute-start | bytes 122888 | tf_op jit(solution)/shard_map/ppermute | solution.py:478
  210.3 2.2 copy-start.1
  215.4 8.5 %copy-start.3 = (bf16[128,4096]{1,0:T(8,128)(2,1)S(1)}, bf16[128,4096]{1,0:T(8,128)(2,1)}, u32[]{:S(2)}) copy-start(bf16[128,4096]{1,0:T(8,128)(2,1)} %x_ref.5) | copy-start | bytes 3145732
  215.4 8.5 %copy-start.5 = (bf16[128,4096]{1,0:T(8,128)(2,1)S(1)}, bf16[128,4096]{1,0:T(8,128)(2,1)}, u32[]{:S(2)}) copy-start(bf16[128,4096]{1,0:T(8,128)(2,1)} %w_ref.5) | copy-start | bytes 3145732
  215.4 8.5 %copy-start.11 = (bf16[128,512]{1,0:T(8,128)(2,1)S(1)}, bf16[128,512]{1,0:T(8,128)(2,1)}, u32[]{:S(2)}) copy-start(bf16[128,512]{1,0:T(8,128)(2,1)} %b_ref.5) | copy-start | bytes 393220
  215.4 8.5 %copy-start.13 = (bf16[128,512]{1,0:T(8,128)(2,1)S(1)}, bf16[128,512]{1,0:T(8,128)(2,1)}, u32[]{:S(2)}) copy-start(bf16[128,512]{1,0:T(8,128)(2,1)} %c_ref.5) | copy-start | bytes 393220
  215.4 108.6 %all-to-all-start.2 = ((f16[128,64,128]{2,1,0:T(8,128)(2,1)}), f16[128,64,128]{2,1,0:T(8,128)(2,1)}, u32[]{:S(2)}, u32[]{:S(2)}) async-start(f16[128,64,128]{2,1,0:T(8,128)(2,1)} %convert_element_type.26), calls=%async_computation.2 | async-start | bytes 4194304 | tf_op jit(solution)/shard_map/all_to_all | solution.py:424
  223.9 1.0 copy-start.23
  224.8 0.8 copy-start.25
  233.7 1.4 copy-start.6
  235.0 1.4 copy-start.8
  236.4 0.7 copy-start.14
  237.1 0.7 copy-start.16
  237.8 0.7 copy-start.18
  238.5 0.7 copy-start.20
  324.0 2.3 copy-start.7
  324.0 2.9 copy-start.9
  324.0 2.9 copy-start.15
  324.0 2.9 copy-start.17
  324.0 3.0 copy-start.19
  324.1 3.1 copy-start.21

commit v4 on v3

--- a/solution.py
+++ b/solution.py
@@ -13,7 +13,7 @@
 LANES = 128
 BITS = 10.0
 TOP = 13.0
-CUT = -1000.0
+CUT = -65000.0
 F32 = jnp.float32
 BF16 = jnp.bfloat16
 PRECISE = lax.Precision.HIGHEST
@@ -80,9 +80,12 @@
     linked = (doc_col == doc_row) & (iota(shape, 0) >= iota(shape, 1))
     bias_ref[...] = jnp.where(linked, 0.0, -1e30)
     turned = (running - jnp.log(sizes)).T
-    through = jnp.where(doc_last == 0.0, last, CUT)
-    keep = jnp.exp(through)
-    edge = jnp.concatenate([through, keep, decay] + [decay] * 5, axis=0)
+    through = jnp.where(doc_last == 0.0, last * 128.0, CUT)
+    high = through.astype(BF16).astype(F32)
+    mid = (through - high).astype(BF16).astype(F32)
+    low = (through - high - mid).astype(BF16).astype(F32)
+    keep = jnp.exp((high + mid + low) * (1.0 / 128.0))
+    edge = jnp.concatenate([high, mid, low, keep, decay, decay, decay, decay], axis=0)
     for g in range(GROUPS):
         mine = slice(g * per, (g + 1) * per)
         size_ref[g] = sizes[:, mine]
@@ -121,95 +124,118 @@
     return dot(jnp.concatenate([proj, proj], axis=0), jnp.concatenate([high, low], axis=0), ((0,), (0,)))
 
 
-def state_kernel(x_ref, w_ref, b_ref, c_ref, tail_ref, reach_ref, out_ref, power_ref):
+def state_kernel(x_ref, w_ref, b_ref, c_ref, tail_ref, reach_ref, edge_ref, out_ref, piece_ref, power_ref):
+    g = pl.program_id(0)
     messages, rows, _ = out_ref.shape
-    part = rows // 2
+    part = (rows - 8) // 2
     fold = STATE // part
-    row = iota((8, LANES), 0)
+    per_group = messages // GROUPS
+    row, lane = iota((8, LANES), 0), iota((8, LANES), 1)
+    piece_ref[g] = dot(edge_ref[0].astype(BF16), spread_map(tail_ref.shape[2], BF16))
     powers = jnp.zeros((8, LANES), F32)
     for which, state in enumerate((state_of(x_ref, b_ref, tail_ref), state_of(w_ref, c_ref, reach_ref))):
         power = exponent_of(state)
-        powers = jnp.where(row == which, jnp.broadcast_to(power, powers.shape), powers)
+        powers = jnp.where(lane == which * GROUPS + g, power, powers)
         state = state * jnp.exp2(TOP - power)
-        for k in range(messages):
+        for k in range(per_group):
             lanes = slice(k // fold * LANES, (k // fold + 1) * LANES)
             here = slice(k % fold * part, (k % fold + 1) * part)
-            out_ref[k, which * part : (which + 1) * part] = state[here, lanes]
-    power_ref[0] = powers
-
-
-def states(x, w, b, c, tail, reach, parts):
+            out_ref[g * per_group + k, which * part : (which + 1) * part] = state[here, lanes]
+
+    @pl.when(g == 0)
+    def _():
+        power_ref[...] = powers
+
+    @pl.when(g > 0)
+    def _():
+        power_ref[...] += powers
+
+    @pl.when(g == GROUPS - 1)
+    def _():
+        side = jnp.where(row == 3, power_ref[...], 0.0)
+        for k in range(messages):
+            lanes = slice(k % per_group // fold * LANES, (k % per_group // fold + 1) * LANES)
+            out_ref[k, 2 * part :] = jnp.where(row < 3, piece_ref[k // per_group, :, lanes], side)
+
+
+def states(x, w, b, c, tail, reach, edge, parts):
     tokens, channels = x.shape
     wide = channels // GROUPS
     per = tail.shape[2]
-    rows = 2 * STATE * channels // (parts * LANES)
+    rows = 2 * STATE * channels // (parts * LANES) + 8
     values = pl.BlockSpec((tokens, wide), lambda g: (0, g))
     proj = pl.BlockSpec((tokens, STATE), lambda g: (0, g))
     small = pl.BlockSpec((1, tokens, per), lambda g: (g, 0, 0))
     return pl.pallas_call(
         state_kernel,
         grid=(GROUPS,),
-        in_specs=[values, values, proj, proj, small, small],
-        out_specs=[
-            pl.BlockSpec((parts // GROUPS, rows, LANES), lambda g: (g, 0, 0)),
-            pl.BlockSpec((1, 8, LANES), lambda g: (g, 0, 0)),
-        ],
-        out_shape=[
-            jax.ShapeDtypeStruct((parts, rows, LANES), F32),
-            jax.ShapeDtypeStruct((GROUPS, 8, LANES), F32),
-        ],
+        in_specs=[values, values, proj, proj, small, small, pl.BlockSpec((1, 8, per), lambda g: (g, 0, 0))],
+        out_specs=pl.BlockSpec((parts, rows, LANES), lambda g: (0, 0, 0)),
+        out_shape=jax.ShapeDtypeStruct((parts, rows, LANES), F32),
+        scratch_shapes=[pltpu.VMEM((GROUPS, 8, wide), F32), pltpu.VMEM((8, LANES), F32)],
         compiler_params=PARAMS,
         cost_estimate=pl.CostEstimate(flops=8 * tokens * STATE * channels, bytes_accessed=7000000, transcendentals=0),
         name="states",
-    )(x, w, b, c, tail, reach)
-
-
-def block_of(pay_ref, side_ref, i, which):
-    part = pay_ref.shape[1] // 2
-    return pay_ref[i, which * part : (which + 1) * part] * side_ref[1 + which, pl.ds(i, 1)]
-
-
-def total_kernel(pay_ref, side_ref, most_ref, out_ref):
+    )(x, w, b, c, tail, reach, edge)
+
+
+def keep_of(pay_ref, i, part):
+    side = pay_ref[i, 2 * part :]
+    return jnp.exp((side[0:1] + side[1:2] + side[2:3]) * (1.0 / 128.0))
+
+
+def lane_of(row, mask_ref, which):
+    mine = mask_ref[mask_ref.shape[0] - 2 + which : mask_ref.shape[0] - 1 + which]
+    return jnp.sum(row * mine, axis=1, keepdims=True)
+
+
+def block_of(pay_ref, mask_ref, i, part, which):
+    power = lane_of(pay_ref[i, 2 * part :][3:4], mask_ref, which)
+    return pay_ref[i, which * part : (which + 1) * part] * jnp.exp2(power - TOP)
+
+
+def total_kernel(pay_ref, mask_ref, out_ref):
     blocks, rows, _ = pay_ref.shape
-    part = rows // 2
+    part = (rows - 8) // 2
 
     def step(k, carry):
-        forth, back, through = carry
+        forth, back, through, most = carry
         late = blocks - 1 - k
-        keep, keep_late = side_ref[0, pl.ds(k, 1)], side_ref[0, pl.ds(late, 1)]
-        forth = keep * forth + block_of(pay_ref, side_ref, k, 0)
-        back = keep_late * back + block_of(pay_ref, side_ref, late, 1)
-        return forth, back, through * keep
+        keep = keep_of(pay_ref, k, part)
+        forth = keep * forth + block_of(pay_ref, mask_ref, k, part, 0)
+        back = keep_of(pay_ref, late, part) * back + block_of(pay_ref, mask_ref, late, part, 1)
+        return forth, back, through * keep, jnp.maximum(most, pay_ref[k, 2 * part :][3:4])
 
     zero = jnp.zeros((part, LANES), F32)
-    forth, back, through = lax.fori_loop(0, blocks, step, (zero, zero, jnp.ones((1, LANES), F32)), unroll=8)
+    one = jnp.ones((1, LANES), F32)
+    forth, back, through, most = lax.fori_loop(0, blocks, step, (zero, zero, one, -1000.0 * one), unroll=8)
     row = iota((8, LANES), 0)
-    side = jnp.where(row == 0, through, most_ref[...])
+    side = jnp.where(row == 0, through, most)
     for which, state in enumerate((forth, back)):
         out_ref[which, 0:part] = state
         out_ref[which, part:] = side
 
 
-def totals(pay, side, most):
-    part = pay.shape[1] // 2
+def totals(pay, mask):
+    part = (pay.shape[1] - 8) // 2
     return pl.pallas_call(
         total_kernel,
         out_shape=jax.ShapeDtypeStruct((2, part + 8, LANES), F32),
         compiler_params=PARAMS,
         cost_estimate=pl.CostEstimate(flops=2 * pay.size, bytes_accessed=4 * pay.size, transcendentals=0),
         name="totals",
-    )(pay, side, most)
-
-
-def enter_kernel(pay_ref, side_ref, own_ref, far_ref, mask_ref, out_ref, most_ref):
+    )(pay, mask)
+
+
+def enter_kernel(pay_ref, own_ref, far_ref, mask_ref, out_ref, most_ref):
     blocks, rows, _ = pay_ref.shape
-    part = rows // 2
+    part = (rows - 8) // 2
     others = far_ref.shape[0]
     most = own_ref[0, part:]
     for k in range(others):
         most = jnp.maximum(most, far_ref[k, 0, part:])
     most_ref[...] = most
-    starts = []
+    starts, scales = [], []
     for which in range(2):
         state = jnp.zeros((part, LANES), F32)
         for by in range(others, 0, -1):
@@ -218,32 +244,29 @@
             valid = mask_ref[which * others + by - 1 : which * others + by] > 0.0
             state = jnp.where(valid, far[0:part] + far[part : part + 1] * state, state)
         starts.append(state)
-    scales = []
-    for which in range(2):
-        mine = mask_ref[2 * others + which : 2 * others + which + 1]
-        power = jnp.sum(most[1:2] * mine, axis=1, keepdims=True)
-        scales.append(jnp.exp2(TOP + 2.0 - BITS - power))
+        scales.append(jnp.exp2(TOP + 2.0 - BITS - lane_of(most[1:2], mask_ref, which)))
 
     def step(k, carry):
         forth, back = carry
         late = blocks - 1 - k
         out_ref[k, 0:part] = forth * scales[0]
         out_ref[late, part:] = back * scales[1]
-        forth = side_ref[0, pl.ds(k, 1)] * forth + block_of(pay_ref, side_ref, k, 0)
-        back = side_ref[0, pl.ds(late, 1)] * back + block_of(pay_ref, side_ref, late, 1)
+        forth = keep_of(pay_ref, k, part) * forth + block_of(pay_ref, mask_ref, k, part, 0)
+        back = keep_of(pay_ref, late, part) * back + block_of(pay_ref, mask_ref, late, part, 1)
         return forth, back
 
     lax.fori_loop(0, blocks, step, tuple(starts), unroll=8)
 
 
-def entering(pay, side, own, far, mask):
+def entering(pay, own, far, mask):
+    blocks, rows, _ = pay.shape
     return pl.pallas_call(
         enter_kernel,
-        out_shape=[jax.ShapeDtypeStruct(pay.shape, F32), jax.ShapeDtypeStruct((8, LANES), F32)],
+        out_shape=[jax.ShapeDtypeStruct((blocks, rows - 8, LANES), F32), jax.ShapeDtypeStruct((8, LANES), F32)],
         compiler_params=PARAMS,
         cost_estimate=pl.CostEstimate(flops=4 * pay.size, bytes_accessed=8 * pay.size, transcendentals=0),
         name="entering",
-    )(pay, side, own, far, mask)
+    )(pay, own, far, mask)
 
 
 def inner_kernel(x_ref, w_ref, b_ref, c_ref, run_ref, runt_ref, bias_ref, skip_ref, y_ref, gx_ref, gb_ref, gc_ref, col_ref, diff_ref):
@@ -350,11 +373,10 @@
 
 def finish_kernel(
     pay_ref, most_ref, x_ref, w_ref, b_ref, c_ref, tail_ref, reach_ref, y_ref, gx_ref, gb_ref, gc_ref, col_ref, diff_ref, size_ref, sig_ref, edge_ref,
-    mixed_ref, gradx_ref, dt_ref, gradb_ref, gradc_ref, all_ref,
+    mixed_ref, gradx_ref, dt_ref, gradb_ref, gradc_ref, rows_ref, cols_ref, met_ref,
 ):
     g = pl.program_id(0)
     tokens, _ = x_ref.shape
-    per = tail_ref.shape[2]
     enter, leave = state_from(pay_ref, most_ref, g, 0), state_from(pay_ref, most_ref, g, 1)
     terms, grad, rows = carried_terms(enter, w_ref[...].astype(F32), reach_ref, c_ref)
     mixed_ref[...] = (y_ref[...] + terms).astype(BF16)
@@ -363,26 +385,28 @@
     gradx_ref[...] = (gx_ref[...] + terms).astype(BF16)
     gradb_ref[...] = (gb_ref[...] + grad).astype(BF16)
     met = jnp.sum(enter * leave, axis=0, keepdims=True)
-    met = head_sums(jnp.broadcast_to(met, (8, met.shape[1])))[0:1]
-    edge = edge_ref[0]
-    keep, decay = edge[1:2], edge[2:3]
-    shape = (tokens, tokens)
-    from_here = (iota(shape, 0) <= iota(shape, 1)).astype(F32)
-    before = (iota(shape, 0) > iota(shape, 1)).astype(F32)
-    grad_rate = dot(from_here, diff_ref[0] + rows, precision=PRECISE) + dot(before, cols, precision=PRECISE) + keep * met
-    grad_size = (col_ref[0] + cols) / size_ref[0] + decay * grad_rate
-    place = (iota((per, GROUPS * per), 0) + g * per == iota((per, GROUPS * per), 1)).astype(F32)
-    placed = dot(grad_size * sig_ref[0], place, precision=PRECISE)
-
-    @pl.when(g == 0)
+    rows_ref[g] = rows
+    cols_ref[g] = cols
+    met_ref[g] = head_sums(jnp.broadcast_to(met, (8, met.shape[1])))
+
+    @pl.when(g == GROUPS - 1)
     def _():
-        all_ref[...] = placed
-
-    @pl.when(g > 0)
-    def _():
-        all_ref[...] += placed
-
-    dt_ref[...] = all_ref[...].astype(BF16)
+        def whole(ref):
+            return jnp.concatenate([ref[k] for k in range(GROUPS)], axis=1)
+
+        edge = whole(edge_ref)
+        keep, decay = edge[3:4], edge[4:5]
+        shape = (tokens, tokens)
+        from_here = (iota(shape, 0) <= iota(shape, 1)).astype(F32)
+        before = (iota(shape, 0) > iota(shape, 1)).astype(F32)
+        late = whole(cols_ref)
+        grad_rate = (
+            dot(from_here, whole(diff_ref) + whole(rows_ref), precision=PRECISE)
+            + dot(before, late, precision=PRECISE)
+            + keep * whole(met_ref)[0:1]
+        )
+        grad_size = (whole(col_ref) + late) / whole(size_ref) + decay * grad_rate
+        dt_ref[...] = (grad_size * whole(sig_ref)).astype(BF16)
 
 
 def finish(pay, most, x, w, b, c, tail, reach, y, gx, gb, gc, col, diff, size, sig, edge):
@@ -393,14 +417,15 @@
     values = pl.BlockSpec((tokens, wide), lambda g: (0, g))
     proj = pl.BlockSpec((tokens, STATE), lambda g: (0, g))
     small = pl.BlockSpec((1, tokens, per), lambda g: (g, 0, 0))
+    every = pl.BlockSpec((GROUPS, tokens, per), lambda g: (0, 0, 0))
     return pl.pallas_call(
         finish_kernel,
         grid=(GROUPS,),
         in_specs=[
             pl.BlockSpec((parts // GROUPS, rows, LANES), lambda g: (g, 0, 0)),
             pl.BlockSpec((8, LANES), lambda g: (0, 0)),
-            values, values, proj, proj, small, small, values, values, proj, proj, small, small, small, small,
-            pl.BlockSpec((1, 8, per), lambda g: (g, 0, 0)),
+            values, values, proj, proj, small, small, values, values, proj, proj, every, every, every, every,
+            pl.BlockSpec((GROUPS, 8, per), lambda g: (0, 0, 0)),
         ],
         out_specs=[values, values, pl.BlockSpec((tokens, GROUPS * per), lambda g: (0, 0)), proj, proj],
         out_shape=[
@@ -410,7 +435,11 @@
             jax.ShapeDtypeStruct((tokens, GROUPS * STATE), BF16),
             jax.ShapeDtypeStruct((tokens, GROUPS * STATE), BF16),
         ],
-        scratch_shapes=[pltpu.VMEM((tokens, GROUPS * per), F32)],
+        scratch_shapes=[
+            pltpu.VMEM((GROUPS, tokens, per), F32),
+            pltpu.VMEM((GROUPS, tokens, per), F32),
+            pltpu.VMEM((GROUPS, 8, per), F32),
+        ],
         compiler_params=PARAMS,
         cost_estimate=pl.CostEstimate(flops=20 * tokens * STATE * channels, bytes_accessed=14_000_000, transcendentals=0),
         name="finish",
@@ -432,26 +461,6 @@
     whole = jnp.where(iota((8, 128), 1) // per_dev == mine, jnp.tile(own, (1, 128 // per_dev)), 0.0)
     whole = jnp.broadcast_to(whole[None], (parts, 8, 128))
     return lax.all_to_all(whole, "head", split_axis=0, concat_axis=0, tiled=True).sum(axis=0)[:, :heads]
-
-
-def around(value, axis, stride, count):
-    size = lax.axis_size(axis)
-    digit = lax.axis_index(axis) // stride % count
-    place = iota((count,) + (1,) * value.ndim, 0)
-    whole = jnp.where(place == digit, value[None], 0.0)
-    for k in range(1, count):
-        pairs = [(p, p + ((p // stride + k) % count - p // stride % count) * stride) for p in range(size)]
-        came = lax.ppermute(value, axis, pairs)
-        whole = whole + jnp.where(place == (digit - k) % count, came[None], 0.0)
-    return whole
-
-
-def known_around(edge, powers, heads):
-    own = jnp.concatenate([edge[:, 0].reshape(1, heads), powers[:, 0:2, 0].T.reshape(1, 2 * GROUPS)], axis=1)
-    own = jnp.pad(own, ((0, 0), (0, LANES - own.shape[1])))
-    table = around(own[0], "head", 1, 4)
-    table = around(table, "head", 4, lax.axis_size("head") // 4).reshape(-1, LANES)
-    return around(table, "near", 1, lax.axis_size("near")).reshape(-1, LANES)
 
 
 def per_device(features, dt_raw, b_proj, c_proj, cotangent, starts, a_log, dt_bias, d_skip):
@@ -462,25 +471,18 @@
     marks = jnp.broadcast_to(marks[None], (8, tokens))
     skip = jnp.broadcast_to(jnp.repeat(params[2], HEADDIM)[None], (8, heads * HEADDIM))
     size, sig, run, runt, reach, tail, bias, edge = prep(dt_raw, params, marks)
-    sent, powers = states(features, cotangent, b_proj, c_proj, tail, reach, parts)
-    came = exchanged(sent)
-    table = known_around(edge, powers, heads)
+    came = exchanged(states(features, cotangent, b_proj, c_proj, tail, reach, edge, parts))
     y, gx, gb, gc, col, diff = inner(features, cotangent, b_proj, c_proj, run, runt, bias, skip)
-    pair = lax.axis_index(GROUP) // (parts * 2 // heads)
-    group = pair // (heads // 2 // GROUPS)
-    decays = lax.dynamic_slice(table, (0, 2 * pair), (parts, 2))
-    column = lambda at: lax.dynamic_slice(table, (0, at), (parts, 1))
-    scales = [jnp.broadcast_to(jnp.exp2(column(heads + k * GROUPS + group) - TOP), (parts, LANES)) for k in range(2)]
-    side = jnp.stack([jnp.repeat(jnp.exp(decays), HEADDIM, axis=1)] + scales)
-    most = jnp.pad(jnp.max(table[:, heads : heads + 2 * GROUPS], axis=0), (0, LANES - 2 * GROUPS))
-    total = totals(came, side, jnp.broadcast_to(most[None], (8, LANES)))
     count, here = lax.axis_size("far"), lax.axis_index("far")
-    far = [lax.ppermute(total, "far", [(p, (p + by) % count) for p in range(count)]) for by in range(1, count)]
+    group = lax.axis_index(GROUP) * GROUPS // parts
     lane = jnp.arange(LANES)
     mask = [jnp.full((LANES,), here - by >= 0) for by in range(1, count)]
     mask += [jnp.full((LANES,), here + by < count) for by in range(1, count)]
     mask += [lane == group, lane == GROUPS + group]
-    left, most = entering(came, side, total, jnp.stack(far), jnp.stack(mask).astype(F32))
+    mask = jnp.stack(mask).astype(F32)
+    total = totals(came, mask)
+    far = [lax.ppermute(total, "far", [(p, (p + by) % count) for p in range(count)]) for by in range(1, count)]
+    left, most = entering(came, total, jnp.stack(far), mask)
     return finish(
         exchanged(left), most, features, cotangent, b_proj, c_proj, tail, reach, y, gx, gb, gc, col, diff, size, sig, edge
     )

time: 338 us -> 308 us (0.911)
  starting transfers between devices: 98.7 us -> 43.8 us
  waiting for transfers between devices: 180 us -> 212 us
  local copies, waits for them, and re-layouts: 23.4 us -> 16.6 us
    all_to_all x2, waiting for transfers between devices: 84.8 us -> 196 us  [exchanged(): lax.all_to_all(messages.astype(jnp.float16), GROUP, split_axis=0, concat_...]
    ppermute x13 -> x0, waiting for transfers between devices: 79.2 us -> none  [around(): came = lax.ppermute(value, axis, pairs)]
    ppermute x13 -> x0, starting transfers between devices: 54.2 us -> none  [around(): came = lax.ppermute(value, axis, pairs)]
    unnamed x53 -> x49, local copies, waits for them, and re-layouts: 17.4 us -> 13.9 us
  transfers between devices with their start and end apart: 19 -> 6, of which waited for: 8 -> 5; matrix products, arithmetic and copies ran while one was open for 2% -> 1% of each run, Pallas kernels for 2% -> 3%
where the time goes in v4:
time: 308 us; the launch traced here: 307 us
  waiting for transfers between devices  212 us (69%)
  starting transfers between devices  43.8 us (14%)
  Pallas kernels  24.4 us (8%)
  local copies, waits for them, and re-layouts  16.6 us (5%)
  other arithmetic  8.77 us (3%)
    all_to_all x2, waiting for transfers between devices, exchanged(): lax.all_to_all(messages.astype(jnp.float16), GROUP, split_axis=0, concat_...  196 us
    all_to_all x1, starting transfers between devices, gathered(): lax.all_to_all(whole, 'head', split_axis=0, concat_axis=0, tiled=True)  18.2 us
    all_to_all x2, starting transfers between devices, exchanged(): lax.all_to_all(messages.astype(jnp.float16), GROUP, split_axis=0, concat_...  15.4 us
    unnamed x49, local copies, waits for them, and re-layouts  13.9 us
    all_to_all x1, waiting for transfers between devices, gathered(): lax.all_to_all(whole, 'head', split_axis=0, concat_axis=0, tiled=True)  11.9 us
    ppermute x3, starting transfers between devices, per_device(): lax.ppermute(total, 'far', [(p, (p + by) % count) for p in range(count)])  10.2 us
    pallas_call x1, Pallas kernels, inner(): pl.pallas_call(inner_kernel, grid=(GROUPS,), in_specs=[values, values, pr...  8.04 us
    pallas_call x1, Pallas kernels, finish(): pl.pallas_call(finish_kernel, grid=(GROUPS,), in_specs=[pl.BlockSpec((par...  7.86 us
  transfers between devices with their start and end apart: 6, of which 5 were waited for; matrix products, arithmetic and copies ran while one was open for 1% of the time, Pallas kernels for 3%

profile of v4, /device:TPU:8, one launch (start us, length us, event | category | flops | bytes accessed | tf_op | source)
XLA Modules:
  0.0 307.0 jit_solution(11732931108954770186)
XLA Ops:
  0.7 0.9 stack.37
  1.6 0.1 copy.20
  1.7 0.1 fusion
  1.8 0.7 broadcast_in_dim.27
  2.5 18.2 %all-to-all-start = ((f32[16,8,128]{2,1,0:T(8,128)}), f32[16,8,128]{2,1,0:T(8,128)S(1)}, u32[]{:S(2)}, u32[]{:S(2)}) async-start(f32[16,8,128]{2,1,0:T(8,128)} %broadcast_in_dim.27), calls=%async_computation | async-start | bytes 131072 | tf_op jit(solution)/shard_map/all_to_all | solution.py:463
  20.7 0.8 copy.22.dt_ref
  21.5 0.8 dynamic-slice_convert_fusion
  22.3 11.9 %all-to-all-done = f32[16,8,128]{2,1,0:T(8,128)S(1)} async-done(((f32[16,8,128]{2,1,0:T(8,128)}), f32[16,8,128]{2,1,0:T(8,128)S(1)}, u32[]{:S(2)}, u32[]{:S(2)}) %all-to-all-start) | async-done | bytes 65568 | tf_op jit(solution)/shard_map/all_to_all | solution.py:463
  34.2 0.6 prep.1
  34.8 0.0 copy-start.20
  34.8 0.7 copy-done.20
  35.5 1.2 copy-done
  36.7 1.2 copy-done.2
  37.9 0.9 copy-done.8
  38.8 0.9 copy-done.10
  39.7 3.9 %states.1 = f32[128,72,128]{2,1,0:T(8,128)S(1)} custom-call(bf16[128,4096]{1,0:T(8,128)(2,1)S(1)} %copy-done, bf16[128,4096]{1,0:T(8,128)(2,1)S(1)} %copy-done.2, bf16[128,512]{1,0:T(8,128)(2,1)S(1)} %copy-done.8, bf16[128,512]{1,0:T(8,128)(2,1)S(1)} %copy-done.10, f32[4,128,16]{2,1,0:T(8,128)S(1)} %get-tuple-element.21.tail_ref, ...), custom_call_target="tpu_custom_call" | custom-call | flops 536870912 | bytes 7000000 | tf_op jit(solution)/shard_map/states/pallas_call | solution.py:169
  43.7 1.7 convert_element_type.19
  45.4 7.8 %all-to-all-start.1 = ((f16[128,72,128]{2,1,0:T(8,128)(2,1)}), f16[128,72,128]{2,1,0:T(8,128)(2,1)}, u32[]{:S(2)}, u32[]{:S(2)}) async-start(f16[128,72,128]{2,1,0:T(8,128)(2,1)} %convert_element_type.19), calls=%async_computation.1 | async-start | bytes 4718592 | tf_op jit(solution)/shard_map/all_to_all | solution.py:453
  53.5 111.5 %all-to-all-done.1 = f16[128,72,128]{2,1,0:T(8,128)(2,1)} async-done(((f16[128,72,128]{2,1,0:T(8,128)(2,1)}), f16[128,72,128]{2,1,0:T(8,128)(2,1)}, u32[]{:S(2)}, u32[]{:S(2)}) %all-to-all-start.1) | async-done | bytes 2359328 | tf_op jit(solution)/shard_map/all_to_all | solution.py:453
  164.9 2.0 convert_element_type.20.pay_ref
  166.9 1.9 totals.1.own_ref
  168.8 4.7 %collective-permute-start.2 = (f32[2,40,128]{2,1,0:T(8,128)S(1)}, f32[2,40,128]{2,1,0:T(8,128)S(1)}, u32[]{:S(2)}, u32[]{:S(2)}) collective-permute-start(f32[2,40,128]{2,1,0:T(8,128)S(1)} %totals.1.own_ref), channel_id=1, source_target_pairs={{0,384},{128,0},{256,128},{384,256},{1,385},{129,1},{257,129},{385... | collective-permute-start | bytes 122888 | tf_op jit(solution)/shard_map/ppermute | solution.py:484
  173.5 2.7 collective-permute-start.1
  176.2 2.8 collective-permute-start
  179.0 1.9 collective-permute-done.1
  180.9 2.4 collective-permute-done
  183.3 2.1 entering.1
  185.5 1.9 convert_element_type.22
  187.3 7.6 %all-to-all-start.2 = ((f16[128,64,128]{2,1,0:T(8,128)(2,1)}), f16[128,64,128]{2,1,0:T(8,128)(2,1)}, u32[]{:S(2)}, u32[]{:S(2)}) async-start(f16[128,64,128]{2,1,0:T(8,128)(2,1)} %convert_element_type.22), calls=%async_computation.2 | async-start | bytes 4194304 | tf_op jit(solution)/shard_map/all_to_all | solution.py:453
  195.0 0.1 broadcast_in_dim.29
  195.0 0.1 broadcast_in_dim.30
  195.2 0.9 copy-done.21
  196.1 0.8 copy-done.23
  196.9 8.0 %inner.1 = (f32[128,4096]{1,0:T(8,128)S(1)}, f32[128,4096]{1,0:T(8,128)S(1)}, f32[128,512]{1,0:T(8,128)S(1)}, f32[128,512]{1,0:T(8,128)S(1)}, f32[4,128,16]{2,1,0:T(8,128)S(1)}, /*index=5*/f32[4,128,16]{2,1,0:T(8,128)S(1)}) custom-call(bf16[128,4096]{1,0:T(8,128)(2,1)S(1)} %copy-done.1, bf16[128,4096]{1,0:T(8,128)(2,1)S(1)} %copy-done.3, ...), custom_call_target="tpu_custom_call" | custom-call | flops 20000000000 | bytes 8000000 | tf_op jit(solution)/shard_map/inner/pallas_call | solution.py:321
  204.9 1.4 copy-done.4
  206.3 1.4 copy-done.6
  207.7 0.7 copy-done.12
  208.4 0.7 copy-done.14
  209.1 0.7 copy-done.16
  209.9 0.7 copy-done.18
  210.6 84.8 %all-to-all-done.2 = f16[128,64,128]{2,1,0:T(8,128)(2,1)} async-done(((f16[128,64,128]{2,1,0:T(8,128)(2,1)}), f16[128,64,128]{2,1,0:T(8,128)(2,1)}, u32[]{:S(2)}, u32[]{:S(2)}) %all-to-all-start.2) | async-done | bytes 2097184 | tf_op jit(solution)/shard_map/all_to_all | solution.py:453
  295.4 2.2 convert_element_type.23.pay_ref
  297.6 0.6 copy-done.7
  298.2 0.1 copy-done.15
  298.3 0.1 copy-done.17
  298.3 0.1 copy-done.19
  298.4 7.9 %finish.1 = (bf16[128,4096]{1,0:T(8,128)(2,1)}, bf16[128,4096]{1,0:T(8,128)(2,1)}, bf16[128,64]{1,0:T(8,128)(2,1)S(1)}, bf16[128,512]{1,0:T(8,128)(2,1)}, bf16[128,512]{1,0:T(8,128)(2,1)}) custom-call(f32[128,64,128]{2,1,0:T(8,128)S(1)} %convert_element_type.23.pay_ref, f32[8,128]{1,0:T(8,128)S(1)} %get-tuple-element.25.most_ref, ...), custom_call_target="tpu_custom_call" | custom-call | flops 1342177280 | bytes 14000000 | tf_op jit(solution)/shard_map/finish/pallas_call | solution.py:421
  306.3 0.7 copy.23
  (49 shorter events, 0.3 us)
Async XLA Ops:
  2.5 31.7 %all-to-all-start = ((f32[16,8,128]{2,1,0:T(8,128)}), f32[16,8,128]{2,1,0:T(8,128)S(1)}, u32[]{:S(2)}, u32[]{:S(2)}) async-start(f32[16,8,128]{2,1,0:T(8,128)} %broadcast_in_dim.27), calls=%async_computation | async-start | bytes 131072 | tf_op jit(solution)/shard_map/all_to_all | solution.py:463
  34.8 0.7 copy-start.20
  35.5 8.2 %copy-start.22 = (f32[4,16,128]{2,1,0:T(8,128)}, f32[4,16,128]{2,1,0:T(8,128)S(1)}, u32[]{:S(2)}) copy-start(f32[4,16,128]{2,1,0:T(8,128)S(1)} %get-tuple-element.27.runt_ref) | copy-start | bytes 98308
  35.5 1.2 copy-start
  36.7 1.2 copy-start.2
  37.9 0.9 copy-start.8
  38.8 0.9 copy-start.10
  45.4 119.5 %all-to-all-start.1 = ((f16[128,72,128]{2,1,0:T(8,128)(2,1)}), f16[128,72,128]{2,1,0:T(8,128)(2,1)}, u32[]{:S(2)}, u32[]{:S(2)}) async-start(f16[128,72,128]{2,1,0:T(8,128)(2,1)} %convert_element_type.19), calls=%async_computation.1 | async-start | bytes 4718592 | tf_op jit(solution)/shard_map/all_to_all | solution.py:453
  168.8 10.2 %collective-permute-start.2 = (f32[2,40,128]{2,1,0:T(8,128)S(1)}, f32[2,40,128]{2,1,0:T(8,128)S(1)}, u32[]{:S(2)}, u32[]{:S(2)}) collective-permute-start(f32[2,40,128]{2,1,0:T(8,128)S(1)} %totals.1.own_ref), channel_id=1, source_target_pairs={{0,384},{128,0},{256,128},{384,256},{1,385},{129,1},{257,129},{385... | collective-permute-start | bytes 122888 | tf_op jit(solution)/shard_map/ppermute | solution.py:484
  173.5 7.4 %collective-permute-start.1 = (f32[2,40,128]{2,1,0:T(8,128)S(1)}, f32[2,40,128]{2,1,0:T(8,128)S(1)}, u32[]{:S(2)}, u32[]{:S(2)}) collective-permute-start(f32[2,40,128]{2,1,0:T(8,128)S(1)} %totals.1.own_ref), channel_id=1, source_target_pairs={{0,256},{128,384},{256,0},{384,128},{1,257},{129,385},{257,1},{385... | collective-permute-start | bytes 122888 | tf_op jit(solution)/shard_map/ppermute | solution.py:484
  176.2 7.1 %collective-permute-start = (f32[2,40,128]{2,1,0:T(8,128)S(1)}, f32[2,40,128]{2,1,0:T(8,128)S(1)}, u32[]{:S(2)}, u32[]{:S(2)}) collective-permute-start(f32[2,40,128]{2,1,0:T(8,128)S(1)} %totals.1.own_ref), channel_id=1, source_target_pairs={{0,128},{128,256},{256,384},{384,0},{1,129},{129,257},{257,385},{3... | collective-permute-start | bytes 122888 | tf_op jit(solution)/shard_map/ppermute | solution.py:484
  187.3 7.8 %copy-start.1 = (bf16[128,4096]{1,0:T(8,128)(2,1)S(1)}, bf16[128,4096]{1,0:T(8,128)(2,1)}, u32[]{:S(2)}) copy-start(bf16[128,4096]{1,0:T(8,128)(2,1)} %x_ref.5) | copy-start | bytes 3145732
  187.3 7.8 %copy-start.3 = (bf16[128,4096]{1,0:T(8,128)(2,1)S(1)}, bf16[128,4096]{1,0:T(8,128)(2,1)}, u32[]{:S(2)}) copy-start(bf16[128,4096]{1,0:T(8,128)(2,1)} %w_ref.5) | copy-start | bytes 3145732
  187.3 7.8 %copy-start.9 = (bf16[128,512]{1,0:T(8,128)(2,1)S(1)}, bf16[128,512]{1,0:T(8,128)(2,1)}, u32[]{:S(2)}) copy-start(bf16[128,512]{1,0:T(8,128)(2,1)} %b_ref.5) | copy-start | bytes 393220
  187.3 7.8 %copy-start.11 = (bf16[128,512]{1,0:T(8,128)(2,1)S(1)}, bf16[128,512]{1,0:T(8,128)(2,1)}, u32[]{:S(2)}) copy-start(bf16[128,512]{1,0:T(8,128)(2,1)} %c_ref.5) | copy-start | bytes 393220
  187.3 108.0 %all-to-all-start.2 = ((f16[128,64,128]{2,1,0:T(8,128)(2,1)}), f16[128,64,128]{2,1,0:T(8,128)(2,1)}, u32[]{:S(2)}, u32[]{:S(2)}) async-start(f16[128,64,128]{2,1,0:T(8,128)(2,1)} %convert_element_type.22), calls=%async_computation.2 | async-start | bytes 4194304 | tf_op jit(solution)/shard_map/all_to_all | solution.py:453
  195.2 1.0 copy-start.21
  196.1 0.8 copy-start.23
  204.9 1.4 copy-start.4
  206.3 1.4 copy-start.6
  207.7 0.7 copy-start.12
  208.4 0.7 copy-start.14
  209.1 0.7 copy-start.16
  209.9 0.7 copy-start.18
  295.3 2.3 copy-start.5
  295.3 2.9 copy-start.7
  295.3 2.9 copy-start.13
  295.4 2.9 copy-start.15
  295.4 3.0 copy-start.17
  295.4 3.1 copy-start.19

commit v5 on v4

--- a/solution.py
+++ b/solution.py
@@ -18,6 +18,7 @@
 BF16 = jnp.bfloat16
 PRECISE = lax.Precision.HIGHEST
 PARAMS = pltpu.CompilerParams(vmem_limit_bytes=40 * 1024 * 1024)
+STATES_VMEM = 62 * 1024 * 1024
 
 
 def iota(shape, axis):
@@ -48,8 +49,8 @@
     heads = value.shape[1] // HEADDIM
     shape = (heads * HEADDIM, heads)
     fold = (iota(shape, 0) // HEADDIM == iota(shape, 1)).astype(BF16)
-    high, low = split(value)
-    return dot(high, fold) + dot(low, fold)
+    both = dot(jnp.concatenate(split(value), axis=0), fold)
+    return both[: value.shape[0]] + both[value.shape[0] :]
 
 
 def exponent_of(block):
@@ -57,7 +58,7 @@
     return jnp.clip(jnp.floor(jnp.log(jnp.maximum(top, 1e-30)) * 1.4426950408889634), -90.0, 40.0)
 
 
-def prep_kernel(dt_ref, par_ref, st_ref, size_ref, sig_ref, run_ref, runt_ref, reach_ref, tail_ref, bias_ref, edge_ref):
+def fill_tables(dt_ref, par_ref, st_ref, size_ref, sig_ref, run_ref, runt_ref, reach_ref, tail_ref, bias_ref, edge_ref):
     tokens, heads = dt_ref.shape
     per = heads // GROUPS
     par = par_ref[...]
@@ -97,86 +98,82 @@
         edge_ref[g] = edge[:, mine]
 
 
-def prep(dt_raw, params, marks):
-    tokens, heads = dt_raw.shape
-    per = heads // GROUPS
-    token_head = jax.ShapeDtypeStruct((GROUPS, tokens, per), F32)
-    return pl.pallas_call(
-        prep_kernel,
-        out_shape=[
-            token_head,
-            token_head,
-            token_head,
-            jax.ShapeDtypeStruct((GROUPS, per, tokens), F32),
-            token_head,
-            token_head,
-            jax.ShapeDtypeStruct((tokens, tokens), F32),
-            jax.ShapeDtypeStruct((GROUPS, 8, per), F32),
-        ],
-        compiler_params=PARAMS,
-        name="prep",
-    )(dt_raw, params, marks)
-
-
-def state_of(val_ref, proj_ref, scale_ref):
-    high, low = split(val_ref[...].astype(F32) * widen(scale_ref[0]))
+def state_of(val_ref, proj_ref, scale):
+    high, low = split(val_ref[...].astype(F32) * widen(scale))
     proj = proj_ref[...]
     return dot(jnp.concatenate([proj, proj], axis=0), jnp.concatenate([high, low], axis=0), ((0,), (0,)))
 
 
-def state_kernel(x_ref, w_ref, b_ref, c_ref, tail_ref, reach_ref, edge_ref, out_ref, piece_ref, power_ref):
+def state_kernel(
+    x_ref, w_ref, b_ref, c_ref, dt_ref, par_ref, st_ref,
+    out_ref, size_ref, sig_ref, run_ref, runt_ref, reach_ref, tail_ref, bias_ref, edge_ref,
+    piece_ref, power_ref, spread_ref,
+):
     g = pl.program_id(0)
     messages, rows, _ = out_ref.shape
     part = (rows - 8) // 2
     fold = STATE // part
     per_group = messages // GROUPS
     row, lane = iota((8, LANES), 0), iota((8, LANES), 1)
-    piece_ref[g] = dot(edge_ref[0].astype(BF16), spread_map(tail_ref.shape[2], BF16))
-    powers = jnp.zeros((8, LANES), F32)
-    for which, state in enumerate((state_of(x_ref, b_ref, tail_ref), state_of(w_ref, c_ref, reach_ref))):
+
+    @pl.when(g == 0)
+    def _():
+        fill_tables(
+            dt_ref, par_ref, st_ref, size_ref, sig_ref, run_ref, runt_ref, reach_ref, tail_ref, bias_ref, edge_ref
+        )
+        power_ref[...] = jnp.zeros((8, LANES), F32)
+
+    piece_ref[g] = dot(edge_ref[g].astype(BF16), spread_map(tail_ref.shape[2], BF16))
+    spread = jnp.zeros((8, LANES), F32)
+    for which, scale_ref in enumerate((tail_ref, reach_ref)):
+        state = state_of((x_ref, w_ref)[which], (b_ref, c_ref)[which], scale_ref[g])
         power = exponent_of(state)
-        powers = jnp.where(lane == which * GROUPS + g, power, powers)
+        spread = jnp.where(row == 4 + which, power, spread)
+        power_ref[...] += jnp.where(lane == which * GROUPS + g, power, 0.0)
         state = state * jnp.exp2(TOP - power)
         for k in range(per_group):
             lanes = slice(k // fold * LANES, (k // fold + 1) * LANES)
             here = slice(k % fold * part, (k % fold + 1) * part)
             out_ref[g * per_group + k, which * part : (which + 1) * part] = state[here, lanes]
-
-    @pl.when(g == 0)
-    def _():
-        power_ref[...] = powers
-
-    @pl.when(g > 0)
-    def _():
-        power_ref[...] += powers
+    spread_ref[g] = spread
 
     @pl.when(g == GROUPS - 1)
     def _():
-        side = jnp.where(row == 3, power_ref[...], 0.0)
         for k in range(messages):
             lanes = slice(k % per_group // fold * LANES, (k % per_group // fold + 1) * LANES)
+            side = jnp.where(row == 3, power_ref[...], spread_ref[k // per_group])
             out_ref[k, 2 * part :] = jnp.where(row < 3, piece_ref[k // per_group, :, lanes], side)
 
 
-def states(x, w, b, c, tail, reach, edge, parts):
+def states(x, w, b, c, dt_raw, params, marks, parts):
     tokens, channels = x.shape
     wide = channels // GROUPS
-    per = tail.shape[2]
+    heads = dt_raw.shape[1]
+    per = heads // GROUPS
     rows = 2 * STATE * channels // (parts * LANES) + 8
     values = pl.BlockSpec((tokens, wide), lambda g: (0, g))
     proj = pl.BlockSpec((tokens, STATE), lambda g: (0, g))
-    small = pl.BlockSpec((1, tokens, per), lambda g: (g, 0, 0))
+
+    def every(shape):
+        return pl.BlockSpec(shape, lambda g: (0,) * len(shape))
+
+    shapes = [(parts, rows, LANES)] + [(GROUPS, tokens, per)] * 3 + [(GROUPS, per, tokens)]
+    shapes += [(GROUPS, tokens, per)] * 2 + [(tokens, tokens), (GROUPS, 8, per)]
     return pl.pallas_call(
         state_kernel,
         grid=(GROUPS,),
-        in_specs=[values, values, proj, proj, small, small, pl.BlockSpec((1, 8, per), lambda g: (g, 0, 0))],
-        out_specs=pl.BlockSpec((parts, rows, LANES), lambda g: (0, 0, 0)),
-        out_shape=jax.ShapeDtypeStruct((parts, rows, LANES), F32),
-        scratch_shapes=[pltpu.VMEM((GROUPS, 8, wide), F32), pltpu.VMEM((8, LANES), F32)],
-        compiler_params=PARAMS,
+        in_specs=[values, values, proj, proj, every(dt_raw.shape), every(params.shape), every(marks.shape)],
+        out_specs=[every(shape) for shape in shapes],
+        out_shape=[jax.ShapeDtypeStruct(shape, F32) for shape in shapes],
+        scratch_shapes=[
+            pltpu.VMEM((GROUPS, 8, wide), F32),
+            pltpu.VMEM((8, LANES), F32),
+            pltpu.VMEM((GROUPS, 8, LANES), F32),
+        ],
+        compiler_params=pltpu.CompilerParams(vmem_limit_bytes=STATES_VMEM),
         cost_estimate=pl.CostEstimate(flops=8 * tokens * STATE * channels, bytes_accessed=7000000, transcendentals=0),
         name="states",
-    )(x, w, b, c, tail, reach, edge)
+    )(x, w, b, c, dt_raw, params, marks)
 
 
 def keep_of(pay_ref, i, part):
@@ -189,12 +186,12 @@
     return jnp.sum(row * mine, axis=1, keepdims=True)
 
 
-def block_of(pay_ref, mask_ref, i, part, which):
-    power = lane_of(pay_ref[i, 2 * part :][3:4], mask_ref, which)
+def block_of(pay_ref, i, part, which):
+    power = pay_ref[i, 2 * part :][4 + which : 5 + which]
     return pay_ref[i, which * part : (which + 1) * part] * jnp.exp2(power - TOP)
 
 
-def total_kernel(pay_ref, mask_ref, out_ref):
+def total_kernel(pay_ref, out_ref):
     blocks, rows, _ = pay_ref.shape
     part = (rows - 8) // 2
 
@@ -202,8 +199,8 @@
         forth, back, through, most = carry
         late = blocks - 1 - k
         keep = keep_of(pay_ref, k, part)
-        forth = keep * forth + block_of(pay_ref, mask_ref, k, part, 0)
-        back = keep_of(pay_ref, late, part) * back + block_of(pay_ref, mask_ref, late, part, 1)
+        forth = keep * forth + block_of(pay_ref, k, part, 0)
+        back = keep_of(pay_ref, late, part) * back + block_of(pay_ref, late, part, 1)
         return forth, back, through * keep, jnp.maximum(most, pay_ref[k, 2 * part :][3:4])
 
     zero = jnp.zeros((part, LANES), F32)
@@ -216,7 +213,7 @@
         out_ref[which, part:] = side
 
 
-def totals(pay, mask):
+def totals(pay):
     part = (pay.shape[1] - 8) // 2
     return pl.pallas_call(
         total_kernel,
@@ -224,7 +221,7 @@
         compiler_params=PARAMS,
         cost_estimate=pl.CostEstimate(flops=2 * pay.size, bytes_accessed=4 * pay.size, transcendentals=0),
         name="totals",
-    )(pay, mask)
+    )(pay)
 
 
 def enter_kernel(pay_ref, own_ref, far_ref, mask_ref, out_ref, most_ref):
@@ -251,8 +248,8 @@
         late = blocks - 1 - k
         out_ref[k, 0:part] = forth * scales[0]
         out_ref[late, part:] = back * scales[1]
-        forth = keep_of(pay_ref, k, part) * forth + block_of(pay_ref, mask_ref, k, part, 0)
-        back = keep_of(pay_ref, late, part) * back + block_of(pay_ref, mask_ref, late, part, 1)
+        forth = keep_of(pay_ref, k, part) * forth + block_of(pay_ref, k, part, 0)
+        back = keep_of(pay_ref, late, part) * back + block_of(pay_ref, late, part, 1)
         return forth, back
 
     lax.fori_loop(0, blocks, step, tuple(starts), unroll=8)
@@ -367,7 +364,9 @@
     terms = dot(jnp.concatenate([proj, proj], axis=1), jnp.concatenate([high, low], axis=0)) * wide
     left_high, left_low = split(values * wide)
     last = ((1,), (1,))
-    grad = dot(left_high, high, last) + (dot(left_high, low, last) + dot(left_low, high, last))
+    both = dot(jnp.concatenate([left_high, left_low], axis=0), high, last)
+    tokens = values.shape[0]
+    grad = both[:tokens] + (both[tokens:] + dot(left_high, low, last))
     return terms, grad, head_sums(terms * values)
 
 
@@ -470,8 +469,10 @@
     marks = lax.dynamic_slice(starts, (lax.axis_index("head") * tokens,), (tokens,)).astype(F32)
     marks = jnp.broadcast_to(marks[None], (8, tokens))
     skip = jnp.broadcast_to(jnp.repeat(params[2], HEADDIM)[None], (8, heads * HEADDIM))
-    size, sig, run, runt, reach, tail, bias, edge = prep(dt_raw, params, marks)
-    came = exchanged(states(features, cotangent, b_proj, c_proj, tail, reach, edge, parts))
+    sent, size, sig, run, runt, reach, tail, bias, edge = states(
+        features, cotangent, b_proj, c_proj, dt_raw, params, marks, parts
+    )
+    came = exchanged(sent)
     y, gx, gb, gc, col, diff = inner(features, cotangent, b_proj, c_proj, run, runt, bias, skip)
     count, here = lax.axis_size("far"), lax.axis_index("far")
     group = lax.axis_index(GROUP) * GROUPS // parts
@@ -480,7 +481,7 @@
     mask += [jnp.full((LANES,), here + by < count) for by in range(1, count)]
     mask += [lane == group, lane == GROUPS + group]
     mask = jnp.stack(mask).astype(F32)
-    total = totals(came, mask)
+    total = totals(came)
     far = [lax.ppermute(total, "far", [(p, (p + by) % count) for p in range(count)]) for by in range(1, count)]
     left, most = entering(came, total, jnp.stack(far), mask)
     return finish(

time: 308 us -> 309 us (level)
    pallas_call x1, Pallas kernels: 3.94 us -> 8.2 us  [states(): pl.pallas_call(state_kernel, grid=(GROUPS,), in_specs=[values, values, pr...]
    unnamed x49 -> x53, local copies, waits for them, and re-layouts: 13.9 us -> 11.3 us
where the time goes in v5:
time: 309 us; the launch traced here: 308 us
  waiting for transfers between devices  213 us (69%)
  starting transfers between devices  42.9 us (14%)
  Pallas kernels  26.2 us (8%)
  local copies, waits for them, and re-layouts  15.3 us (5%)
  other arithmetic  10.1 us (3%)
    all_to_all x2, waiting for transfers between devices, exchanged(): lax.all_to_all(messages.astype(jnp.float16), GROUP, split_axis=0, concat_...  198 us
    all_to_all x1, starting transfers between devices, gathered(): lax.all_to_all(whole, 'head', split_axis=0, concat_axis=0, tiled=True)  18.2 us
    all_to_all x2, starting transfers between devices, exchanged(): lax.all_to_all(messages.astype(jnp.float16), GROUP, split_axis=0, concat_...  14.5 us
    unnamed x53, local copies, waits for them, and re-layouts  11.3 us
    all_to_all x1, waiting for transfers between devices, gathered(): lax.all_to_all(whole, 'head', split_axis=0, concat_axis=0, tiled=True)  11.3 us
    ppermute x3, starting transfers between devices, per_device(): lax.ppermute(total, 'far', [(p, (p + by) % count) for p in range(count)])  10.2 us
    pallas_call x1, Pallas kernels, states(): pl.pallas_call(state_kernel, grid=(GROUPS,), in_specs=[values, values, pr...  8.2 us
    pallas_call x1, Pallas kernels, inner(): pl.pallas_call(inner_kernel, grid=(GROUPS,), in_specs=[values, values, pr...  8.18 us
  transfers between devices with their start and end apart: 6, of which 5 were waited for; matrix products, arithmetic and copies ran while one was open for 1% of the time, Pallas kernels for 3%

profile of v5, /device:TPU:8, one launch (start us, length us, event | category | flops | bytes accessed | tf_op | source)
XLA Modules:
  0.0 308.4 jit_solution(15768780749665086886)
XLA Ops:
  0.7 0.9 stack.37
  1.6 0.1 copy.20
  1.7 0.1 fusion
  1.8 0.7 broadcast_in_dim.27
  2.5 18.2 %all-to-all-start = ((f32[16,8,128]{2,1,0:T(8,128)}), f32[16,8,128]{2,1,0:T(8,128)S(1)}, u32[]{:S(2)}, u32[]{:S(2)}) async-start(f32[16,8,128]{2,1,0:T(8,128)} %broadcast_in_dim.27), calls=%async_computation | async-start | bytes 131072 | tf_op jit(solution)/shard_map/all_to_all | solution.py:462
  20.7 1.4 copy.22.dt_ref
  22.1 0.8 dynamic-slice_convert_fusion
  22.9 11.3 %all-to-all-done = f32[16,8,128]{2,1,0:T(8,128)S(1)} async-done(((f32[16,8,128]{2,1,0:T(8,128)}), f32[16,8,128]{2,1,0:T(8,128)S(1)}, u32[]{:S(2)}, u32[]{:S(2)}) %all-to-all-start) | async-done | bytes 65568 | tf_op jit(solution)/shard_map/all_to_all | solution.py:462
  34.1 0.6 reduce_sum.9
  34.8 0.6 broadcast_in_dim.28.st_ref
  35.4 8.2 %states.1 = (f32[128,72,128]{2,1,0:T(8,128)}, f32[4,128,16]{2,1,0:T(8,128)}, f32[4,128,16]{2,1,0:T(8,128)}, f32[4,128,16]{2,1,0:T(8,128)}, f32[4,16,128]{2,1,0:T...) custom-call(bf16[128,4096]{1,0:T(8,128)(2,1)} %x_ref.5, ...), custom_call_target="tpu_custom_call" | custom-call | flops 536870912 | bytes 7000000 | tf_op jit(solution)/shard_map/states/pallas_call | solution.py:162
  43.6 4.1 %convert_element_type.19 = f16[128,72,128]{2,1,0:T(8,128)(2,1)} convert(f32[128,72,128]{2,1,0:T(8,128)} %get-tuple-element.22) | non-fusion elementwise | flops 1179648 | bytes 7077888 | tf_op jit(solution)/shard_map/convert_element_type | solution.py:452
  47.6 7.0 %all-to-all-start.1 = ((f16[128,72,128]{2,1,0:T(8,128)(2,1)}), f16[128,72,128]{2,1,0:T(8,128)(2,1)S(1)}, u32[]{:S(2)}, u32[]{:S(2)}) async-start(f16[128,72,128]{2,1,0:T(8,128)(2,1)} %convert_element_type.19), calls=%async_computation.1 | async-start | bytes 4718592 | tf_op jit(solution)/shard_map/all_to_all | solution.py:452
  54.6 111.9 %all-to-all-done.1 = f16[128,72,128]{2,1,0:T(8,128)(2,1)S(1)} async-done(((f16[128,72,128]{2,1,0:T(8,128)(2,1)}), f16[128,72,128]{2,1,0:T(8,128)(2,1)S(1)}, u32[]{:S(2)}, u32[]{:S(2)}) %all-to-all-start.1) | async-done | bytes 2359328 | tf_op jit(solution)/shard_map/all_to_all | solution.py:452
  166.5 0.3 convert_element_type.20.pay_ref
  166.8 0.9 totals.1.own_ref
  167.7 1.2 copy-done
  169.0 4.7 %collective-permute-start.2 = (f32[2,40,128]{2,1,0:T(8,128)S(1)}, f32[2,40,128]{2,1,0:T(8,128)S(1)}, u32[]{:S(2)}, u32[]{:S(2)}) collective-permute-start(f32[2,40,128]{2,1,0:T(8,128)S(1)} %totals.1.own_ref), channel_id=1, source_target_pairs={{0,384},{128,0},{256,128},{384,256},{1,385},{129,1},{257,129},{385... | collective-permute-start | bytes 122888 | tf_op jit(solution)/shard_map/ppermute | solution.py:485
  173.6 2.7 collective-permute-start.1
  176.4 2.8 collective-permute-start
  179.3 0.0 collective-permute-done.2
  179.3 1.7 collective-permute-done.1
  181.0 2.4 collective-permute-done
  183.5 2.3 copy-done.1
  185.8 1.2 entering.1
  187.0 1.9 convert_element_type.22
  188.9 0.0 copy-start.24
  188.9 0.0 copy-start.25
  188.9 7.6 %all-to-all-start.2 = ((f16[128,64,128]{2,1,0:T(8,128)(2,1)}), f16[128,64,128]{2,1,0:T(8,128)(2,1)}, u32[]{:S(2)}, u32[]{:S(2)}) async-start(f16[128,64,128]{2,1,0:T(8,128)(2,1)} %convert_element_type.22), calls=%async_computation.2 | async-start | bytes 4194304 | tf_op jit(solution)/shard_map/all_to_all | solution.py:452
  196.5 0.7 slice_bitcast_fusion
  197.2 0.1 broadcast_in_dim.29
  197.2 0.1 broadcast_in_dim.30
  197.4 8.2 %inner.1 = (f32[128,4096]{1,0:T(8,128)S(1)}, f32[128,4096]{1,0:T(8,128)S(1)}, f32[128,512]{1,0:T(8,128)S(1)}, f32[128,512]{1,0:T(8,128)S(1)}, f32[4,128,16]{2,1,0:T(8,128)S(1)}, /*index=5*/f32[4,128,16]{2,1,0:T(8,128)S(1)}) custom-call(bf16[128,4096]{1,0:T(8,128)(2,1)S(1)} %copy-done.2, bf16[128,4096]{1,0:T(8,128)(2,1)S(1)} %copy-done.3, ...), custom_call_target="tpu_custom_call" | custom-call | flops 20000000000 | bytes 8000000 | tf_op jit(solution)/shard_map/inner/pallas_call | solution.py:318
  205.6 1.4 copy-done.4
  207.0 1.4 copy-done.6
  208.4 0.7 copy-done.14
  209.1 0.7 copy-done.16
  209.8 0.7 copy-done.18
  210.4 0.7 copy-done.20
  211.2 0.0 copy-start.22
  211.2 85.7 %all-to-all-done.2 = f16[128,64,128]{2,1,0:T(8,128)(2,1)} async-done(((f16[128,64,128]{2,1,0:T(8,128)(2,1)}), f16[128,64,128]{2,1,0:T(8,128)(2,1)}, u32[]{:S(2)}, u32[]{:S(2)}) %all-to-all-start.2) | async-done | bytes 2097184 | tf_op jit(solution)/shard_map/all_to_all | solution.py:452
  296.9 2.2 convert_element_type.23.pay_ref
  299.2 0.5 copy-done.7
  299.7 0.1 copy-done.17
  299.8 0.1 copy-done.19
  299.9 0.1 copy-done.21
  299.9 7.8 %finish.1 = (bf16[128,4096]{1,0:T(8,128)(2,1)}, bf16[128,4096]{1,0:T(8,128)(2,1)}, bf16[128,64]{1,0:T(8,128)(2,1)S(1)}, bf16[128,512]{1,0:T(8,128)(2,1)}, bf16[128,512]{1,0:T(8,128)(2,1)}) custom-call(f32[128,64,128]{2,1,0:T(8,128)S(1)} %convert_element_type.23.pay_ref, f32[8,128]{1,0:T(8,128)S(1)} %get-tuple-element.24.most_ref, ...), custom_call_target="tpu_custom_call" | custom-call | flops 1342177280 | bytes 14000000 | tf_op jit(solution)/shard_map/finish/pallas_call | solution.py:420
  307.7 0.7 copy.23
  (52 shorter events, 0.3 us)
Async XLA Ops:
  2.5 31.7 %all-to-all-start = ((f32[16,8,128]{2,1,0:T(8,128)}), f32[16,8,128]{2,1,0:T(8,128)S(1)}, u32[]{:S(2)}, u32[]{:S(2)}) async-start(f32[16,8,128]{2,1,0:T(8,128)} %broadcast_in_dim.27), calls=%async_computation | async-start | bytes 131072 | tf_op jit(solution)/shard_map/all_to_all | solution.py:462
  47.6 118.9 %all-to-all-start.1 = ((f16[128,72,128]{2,1,0:T(8,128)(2,1)}), f16[128,72,128]{2,1,0:T(8,128)(2,1)S(1)}, u32[]{:S(2)}, u32[]{:S(2)}) async-start(f16[128,72,128]{2,1,0:T(8,128)(2,1)} %convert_element_type.19), calls=%async_computation.1 | async-start | bytes 4718592 | tf_op jit(solution)/shard_map/all_to_all | solution.py:452
  166.8 2.2 copy-start
  169.0 10.4 %collective-permute-start.2 = (f32[2,40,128]{2,1,0:T(8,128)S(1)}, f32[2,40,128]{2,1,0:T(8,128)S(1)}, u32[]{:S(2)}, u32[]{:S(2)}) collective-permute-start(f32[2,40,128]{2,1,0:T(8,128)S(1)} %totals.1.own_ref), channel_id=1, source_target_pairs={{0,384},{128,0},{256,128},{384,256},{1,385},{129,1},{257,129},{385... | collective-permute-start | bytes 122888 | tf_op jit(solution)/shard_map/ppermute | solution.py:485
  173.6 7.4 %collective-permute-start.1 = (f32[2,40,128]{2,1,0:T(8,128)S(1)}, f32[2,40,128]{2,1,0:T(8,128)S(1)}, u32[]{:S(2)}, u32[]{:S(2)}) collective-permute-start(f32[2,40,128]{2,1,0:T(8,128)S(1)} %totals.1.own_ref), channel_id=1, source_target_pairs={{0,256},{128,384},{256,0},{384,128},{1,257},{129,385},{257,1},{385... | collective-permute-start | bytes 122888 | tf_op jit(solution)/shard_map/ppermute | solution.py:485
  176.4 7.1 %collective-permute-start = (f32[2,40,128]{2,1,0:T(8,128)S(1)}, f32[2,40,128]{2,1,0:T(8,128)S(1)}, u32[]{:S(2)}, u32[]{:S(2)}) collective-permute-start(f32[2,40,128]{2,1,0:T(8,128)S(1)} %totals.1.own_ref), channel_id=1, source_target_pairs={{0,128},{128,256},{256,384},{384,0},{1,129},{129,257},{257,385},{3... | collective-permute-start | bytes 122888 | tf_op jit(solution)/shard_map/ppermute | solution.py:485
  183.5 2.3 copy-start.1
  188.9 8.5 %copy-start.2 = (bf16[128,4096]{1,0:T(8,128)(2,1)S(1)}, bf16[128,4096]{1,0:T(8,128)(2,1)}, u32[]{:S(2)}) copy-start(bf16[128,4096]{1,0:T(8,128)(2,1)} %x_ref.5) | copy-start | bytes 3145732
  188.9 8.5 %copy-start.3 = (bf16[128,4096]{1,0:T(8,128)(2,1)S(1)}, bf16[128,4096]{1,0:T(8,128)(2,1)}, u32[]{:S(2)}) copy-start(bf16[128,4096]{1,0:T(8,128)(2,1)} %w_ref.5) | copy-start | bytes 3145732
  188.9 8.5 %copy-start.8 = (bf16[128,512]{1,0:T(8,128)(2,1)S(1)}, bf16[128,512]{1,0:T(8,128)(2,1)}, u32[]{:S(2)}) copy-start(bf16[128,512]{1,0:T(8,128)(2,1)} %b_ref.5) | copy-start | bytes 393220
  188.9 8.5 %copy-start.9 = (bf16[128,512]{1,0:T(8,128)(2,1)S(1)}, bf16[128,512]{1,0:T(8,128)(2,1)}, u32[]{:S(2)}) copy-start(bf16[128,512]{1,0:T(8,128)(2,1)} %c_ref.5) | copy-start | bytes 393220
  188.9 8.5 %copy-start.23 = (f32[4,128,16]{2,1,0:T(8,128)S(1)}, f32[4,128,16]{2,1,0:T(8,128)}, u32[]{:S(2)}) copy-start(f32[4,128,16]{2,1,0:T(8,128)} %get-tuple-element.27.run_ref) | copy-start | bytes 98308
  188.9 8.5 %copy-start.24 = (f32[128,128]{1,0:T(8,128)S(1)}, f32[128,128]{1,0:T(8,128)}, u32[]{:S(2)}) copy-start(f32[128,128]{1,0:T(8,128)} %get-tuple-element.29.bias_ref) | copy-start | bytes 196612
  188.9 8.5 %copy-start.25 = (f32[4,16,128]{2,1,0:T(8,128)S(1)}, f32[4,16,128]{2,1,0:T(8,128)}, u32[]{:S(2)}) copy-start(f32[4,16,128]{2,1,0:T(8,128)} %get-tuple-element.28.runt_ref) | copy-start | bytes 98308
  188.9 108.0 %all-to-all-start.2 = ((f16[128,64,128]{2,1,0:T(8,128)(2,1)}), f16[128,64,128]{2,1,0:T(8,128)(2,1)}, u32[]{:S(2)}, u32[]{:S(2)}) async-start(f16[128,64,128]{2,1,0:T(8,128)(2,1)} %convert_element_type.22), calls=%async_computation.2 | async-start | bytes 4194304 | tf_op jit(solution)/shard_map/all_to_all | solution.py:452
  205.6 1.4 copy-start.4
  207.0 1.4 copy-start.6
  208.4 0.7 copy-start.14
  209.0 0.7 copy-start.16
  209.7 0.7 copy-start.18
  210.4 0.7 copy-start.20
  211.1 88.0 %copy-start.10 = (f32[4,128,16]{2,1,0:T(8,128)S(1)}, f32[4,128,16]{2,1,0:T(8,128)}, u32[]{:S(2)}) copy-start(f32[4,128,16]{2,1,0:T(8,128)} %get-tuple-element.36.size_ref) | copy-start | bytes 98308
  211.1 88.0 %copy-start.11 = (f32[4,128,16]{2,1,0:T(8,128)S(1)}, f32[4,128,16]{2,1,0:T(8,128)}, u32[]{:S(2)}) copy-start(f32[4,128,16]{2,1,0:T(8,128)} %get-tuple-element.37.sig_ref) | copy-start | bytes 98308
  211.1 88.0 %copy-start.12 = (f32[4,128,16]{2,1,0:T(8,128)S(1)}, f32[4,128,16]{2,1,0:T(8,128)}, u32[]{:S(2)}) copy-start(f32[4,128,16]{2,1,0:T(8,128)} %get-tuple-element.26.reach_ref) | copy-start | bytes 98308
  211.2 88.0 %copy-start.13 = (f32[4,128,16]{2,1,0:T(8,128)S(1)}, f32[4,128,16]{2,1,0:T(8,128)}, u32[]{:S(2)}) copy-start(f32[4,128,16]{2,1,0:T(8,128)} %get-tuple-element.25.tail_ref) | copy-start | bytes 98308
  211.2 88.0 %copy-start.22 = (f32[4,8,16]{2,1,0:T(8,128)S(1)}, f32[4,8,16]{2,1,0:T(8,128)}, u32[]{:S(2)}) copy-start(f32[4,8,16]{2,1,0:T(8,128)} %get-tuple-element.38.edge_ref) | copy-start | bytes 6148
  296.9 2.3 copy-start.5
  296.9 2.9 copy-start.7
  296.9 2.9 copy-start.15
  296.9 2.9 copy-start.17
  296.9 3.0 copy-start.19
  296.9 3.1 copy-start.21

commit v6 on v4

--- a/solution.py
+++ b/solution.py
@@ -17,7 +17,7 @@
 F32 = jnp.float32
 BF16 = jnp.bfloat16
 PRECISE = lax.Precision.HIGHEST
-PARAMS = pltpu.CompilerParams(vmem_limit_bytes=40 * 1024 * 1024)
+PARAMS = pltpu.CompilerParams(vmem_limit_bytes=24 * 1024 * 1024)
 
 
 def iota(shape, axis):
@@ -57,7 +57,7 @@
     return jnp.clip(jnp.floor(jnp.log(jnp.maximum(top, 1e-30)) * 1.4426950408889634), -90.0, 40.0)
 
 
-def prep_kernel(dt_ref, par_ref, st_ref, size_ref, sig_ref, run_ref, runt_ref, reach_ref, tail_ref, bias_ref, edge_ref):
+def prep_kernel(urgent, dt_ref, par_ref, st_ref, *outs):
     tokens, heads = dt_ref.shape
     per = heads // GROUPS
     par = par_ref[...]
@@ -65,7 +65,6 @@
     decay = -jnp.exp(a_log)
     value = dt_ref[...].astype(F32) + dt_bias
     sizes = jnp.maximum(value, 0.0) + jnp.log1p(jnp.exp(-jnp.abs(value)))
-    sigmoid = 1.0 / (1.0 + jnp.exp(-value))
     shape = (tokens, tokens)
     lower = (iota(shape, 0) >= iota(shape, 1)).astype(F32)
     upper = (iota(shape, 0) <= iota(shape, 1)).astype(F32)
@@ -74,48 +73,65 @@
     doc_row = dot(marks, upper)[0:1]
     doc_col = dot(lower, marks, ((1,), (1,)))[:, 0:1]
     doc_last = doc_row[:, tokens - 1 :]
-    last = running[tokens - 1 :]
-    reach = jnp.where(doc_col == 0.0, jnp.exp(running), 0.0)
-    tail = jnp.where(doc_col == doc_last, jnp.exp(last - running), 0.0) * sizes
-    linked = (doc_col == doc_row) & (iota(shape, 0) >= iota(shape, 1))
-    bias_ref[...] = jnp.where(linked, 0.0, -1e30)
-    turned = (running - jnp.log(sizes)).T
-    through = jnp.where(doc_last == 0.0, last * 128.0, CUT)
-    high = through.astype(BF16).astype(F32)
-    mid = (through - high).astype(BF16).astype(F32)
-    low = (through - high - mid).astype(BF16).astype(F32)
-    keep = jnp.exp((high + mid + low) * (1.0 / 128.0))
-    edge = jnp.concatenate([high, mid, low, keep, decay, decay, decay, decay], axis=0)
-    for g in range(GROUPS):
-        mine = slice(g * per, (g + 1) * per)
-        size_ref[g] = sizes[:, mine]
-        sig_ref[g] = sigmoid[:, mine]
-        run_ref[g] = running[:, mine]
-        runt_ref[g] = turned[mine]
-        reach_ref[g] = reach[:, mine]
-        tail_ref[g] = tail[:, mine]
-        edge_ref[g] = edge[:, mine]
-
-
-def prep(dt_raw, params, marks):
+    groups = [slice(g * per, (g + 1) * per) for g in range(GROUPS)]
+    if urgent:
+        reach_ref, tail_ref, edge_ref = outs
+        last = running[tokens - 1 :]
+        reach = jnp.where(doc_col == 0.0, jnp.exp(running), 0.0)
+        tail = jnp.where(doc_col == doc_last, jnp.exp(last - running), 0.0) * sizes
+        through = jnp.where(doc_last == 0.0, last * 128.0, CUT)
+        high = through.astype(BF16).astype(F32)
+        mid = (through - high).astype(BF16).astype(F32)
+        low = (through - high - mid).astype(BF16).astype(F32)
+        keep = jnp.exp((high + mid + low) * (1.0 / 128.0))
+        edge = jnp.concatenate([high, mid, low, keep, decay, decay, decay, decay], axis=0)
+        for g, mine in enumerate(groups):
+            reach_ref[g] = reach[:, mine]
+            tail_ref[g] = tail[:, mine]
+            edge_ref[g] = edge[:, mine]
+    else:
+        size_ref, sig_ref, run_ref, runt_ref, bias_ref = outs
+        linked = (doc_col == doc_row) & (iota(shape, 0) >= iota(shape, 1))
+        bias_ref[...] = jnp.where(linked, 0.0, -1e30)
+        turned = (running - jnp.log(sizes)).T
+        sigmoid = 1.0 / (1.0 + jnp.exp(-value))
+        for g, mine in enumerate(groups):
+            size_ref[g] = sizes[:, mine]
+            sig_ref[g] = sigmoid[:, mine]
+            run_ref[g] = running[:, mine]
+            runt_ref[g] = turned[mine]
+
+
+def prep(dt_raw, params, marks, urgent):
     tokens, heads = dt_raw.shape
     per = heads // GROUPS
-    token_head = jax.ShapeDtypeStruct((GROUPS, tokens, per), F32)
-    return pl.pallas_call(
-        prep_kernel,
-        out_shape=[
-            token_head,
-            token_head,
-            token_head,
-            jax.ShapeDtypeStruct((GROUPS, per, tokens), F32),
-            token_head,
-            token_head,
-            jax.ShapeDtypeStruct((tokens, tokens), F32),
-            jax.ShapeDtypeStruct((GROUPS, 8, per), F32),
-        ],
+    small = (GROUPS, tokens, per)
+    if urgent:
+        shapes = [small, small, (GROUPS, 8, per)]
+    else:
+        shapes = [small, small, small, (GROUPS, per, tokens), (tokens, tokens)]
+    return pl.pallas_call(
+        functools.partial(prep_kernel, urgent),
+        out_shape=[jax.ShapeDtypeStruct(shape, F32) for shape in shapes],
         compiler_params=PARAMS,
         name="prep",
     )(dt_raw, params, marks)
+
+
+def stage_kernel(*refs):
+    half = len(refs) // 2
+    for source, target in zip(refs[:half], refs[half:]):
+        target[...] = source[...]
+
+
+def staged(*arrays):
+    return pl.pallas_call(
+        stage_kernel,
+        out_shape=[jax.ShapeDtypeStruct(array.shape, array.dtype) for array in arrays],
+        compiler_params=PARAMS,
+        cost_estimate=pl.CostEstimate(flops=0, bytes_accessed=2 * sum(2 * array.size for array in arrays), transcendentals=0),
+        name="staged",
+    )(*arrays)
 
 
 def state_of(val_ref, proj_ref, scale_ref):
@@ -124,7 +140,7 @@
     return dot(jnp.concatenate([proj, proj], axis=0), jnp.concatenate([high, low], axis=0), ((0,), (0,)))
 
 
-def state_kernel(x_ref, w_ref, b_ref, c_ref, tail_ref, reach_ref, edge_ref, out_ref, piece_ref, power_ref):
+def state_kernel(x_ref, w_ref, b_ref, c_ref, tail_ref, reach_ref, edge_ref, out_ref, piece_ref, power_ref, spread_ref):
     g = pl.program_id(0)
     messages, rows, _ = out_ref.shape
     part = (rows - 8) // 2
@@ -133,14 +149,17 @@
     row, lane = iota((8, LANES), 0), iota((8, LANES), 1)
     piece_ref[g] = dot(edge_ref[0].astype(BF16), spread_map(tail_ref.shape[2], BF16))
     powers = jnp.zeros((8, LANES), F32)
+    spread = jnp.zeros((8, LANES), F32)
     for which, state in enumerate((state_of(x_ref, b_ref, tail_ref), state_of(w_ref, c_ref, reach_ref))):
         power = exponent_of(state)
+        spread = jnp.where(row == 4 + which, power, spread)
         powers = jnp.where(lane == which * GROUPS + g, power, powers)
         state = state * jnp.exp2(TOP - power)
         for k in range(per_group):
             lanes = slice(k // fold * LANES, (k // fold + 1) * LANES)
             here = slice(k % fold * part, (k % fold + 1) * part)
             out_ref[g * per_group + k, which * part : (which + 1) * part] = state[here, lanes]
+    spread_ref[g] = spread
 
     @pl.when(g == 0)
     def _():
@@ -152,9 +171,9 @@
 
     @pl.when(g == GROUPS - 1)
     def _():
-        side = jnp.where(row == 3, power_ref[...], 0.0)
         for k in range(messages):
             lanes = slice(k % per_group // fold * LANES, (k % per_group // fold + 1) * LANES)
+            side = jnp.where(row == 3, power_ref[...], spread_ref[k // per_group])
             out_ref[k, 2 * part :] = jnp.where(row < 3, piece_ref[k // per_group, :, lanes], side)
 
 
@@ -172,7 +191,11 @@
         in_specs=[values, values, proj, proj, small, small, pl.BlockSpec((1, 8, per), lambda g: (g, 0, 0))],
         out_specs=pl.BlockSpec((parts, rows, LANES), lambda g: (0, 0, 0)),
         out_shape=jax.ShapeDtypeStruct((parts, rows, LANES), F32),
-        scratch_shapes=[pltpu.VMEM((GROUPS, 8, wide), F32), pltpu.VMEM((8, LANES), F32)],
+        scratch_shapes=[
+            pltpu.VMEM((GROUPS, 8, wide), F32),
+            pltpu.VMEM((8, LANES), F32),
+            pltpu.VMEM((GROUPS, 8, LANES), F32),
+        ],
         compiler_params=PARAMS,
         cost_estimate=pl.CostEstimate(flops=8 * tokens * STATE * channels, bytes_accessed=7000000, transcendentals=0),
         name="states",
@@ -189,12 +212,12 @@
     return jnp.sum(row * mine, axis=1, keepdims=True)
 
 
-def block_of(pay_ref, mask_ref, i, part, which):
-    power = lane_of(pay_ref[i, 2 * part :][3:4], mask_ref, which)
+def block_of(pay_ref, i, part, which):
+    power = pay_ref[i, 2 * part :][4 + which : 5 + which]
     return pay_ref[i, which * part : (which + 1) * part] * jnp.exp2(power - TOP)
 
 
-def total_kernel(pay_ref, mask_ref, out_ref):
+def total_kernel(pay_ref, out_ref):
     blocks, rows, _ = pay_ref.shape
     part = (rows - 8) // 2
 
@@ -202,8 +225,8 @@
         forth, back, through, most = carry
         late = blocks - 1 - k
         keep = keep_of(pay_ref, k, part)
-        forth = keep * forth + block_of(pay_ref, mask_ref, k, part, 0)
-        back = keep_of(pay_ref, late, part) * back + block_of(pay_ref, mask_ref, late, part, 1)
+        forth = keep * forth + block_of(pay_ref, k, part, 0)
+        back = keep_of(pay_ref, late, part) * back + block_of(pay_ref, late, part, 1)
         return forth, back, through * keep, jnp.maximum(most, pay_ref[k, 2 * part :][3:4])
 
     zero = jnp.zeros((part, LANES), F32)
@@ -216,7 +239,7 @@
         out_ref[which, part:] = side
 
 
-def totals(pay, mask):
+def totals(pay):
     part = (pay.shape[1] - 8) // 2
     return pl.pallas_call(
         total_kernel,
@@ -224,7 +247,7 @@
         compiler_params=PARAMS,
         cost_estimate=pl.CostEstimate(flops=2 * pay.size, bytes_accessed=4 * pay.size, transcendentals=0),
         name="totals",
-    )(pay, mask)
+    )(pay)
 
 
 def enter_kernel(pay_ref, own_ref, far_ref, mask_ref, out_ref, most_ref):
@@ -251,8 +274,8 @@
         late = blocks - 1 - k
         out_ref[k, 0:part] = forth * scales[0]
         out_ref[late, part:] = back * scales[1]
-        forth = keep_of(pay_ref, k, part) * forth + block_of(pay_ref, mask_ref, k, part, 0)
-        back = keep_of(pay_ref, late, part) * back + block_of(pay_ref, mask_ref, late, part, 1)
+        forth = keep_of(pay_ref, k, part) * forth + block_of(pay_ref, k, part, 0)
+        back = keep_of(pay_ref, late, part) * back + block_of(pay_ref, late, part, 1)
         return forth, back
 
     lax.fori_loop(0, blocks, step, tuple(starts), unroll=8)
@@ -450,28 +473,42 @@
 
 
 def exchanged(messages):
-    sent = lax.all_to_all(messages.astype(jnp.float16), GROUP, split_axis=0, concat_axis=0, tiled=True)
-    return sent.astype(F32)
-
-
-def gathered(own, heads):
+    return lax.all_to_all(messages.astype(jnp.float16), GROUP, split_axis=0, concat_axis=0, tiled=True)
+
+
+def message_kernel(mine_ref, a_ref, bias_ref, skip_ref, out_ref):
+    row, lane = iota((8, LANES), 0), iota((8, LANES), 1)
+    per_dev = a_ref.shape[0]
+    value = jnp.zeros((8, LANES), F32)
+    for k, ref in enumerate((a_ref, bias_ref, skip_ref)):
+        for i in range(per_dev):
+            value = jnp.where((row == k) & (lane == mine_ref[0] * per_dev + i), ref[i], value)
+    out_ref[...] = jnp.broadcast_to(value[None], out_ref.shape)
+
+
+def gathered(a_log, dt_bias, d_skip, heads):
     parts = lax.axis_size("head")
-    per_dev = own.shape[1]
-    mine = lax.axis_index("head")
-    whole = jnp.where(iota((8, 128), 1) // per_dev == mine, jnp.tile(own, (1, 128 // per_dev)), 0.0)
-    whole = jnp.broadcast_to(whole[None], (parts, 8, 128))
-    return lax.all_to_all(whole, "head", split_axis=0, concat_axis=0, tiled=True).sum(axis=0)[:, :heads]
+    message = pl.pallas_call(
+        message_kernel,
+        in_specs=[pl.BlockSpec(memory_space=pltpu.SMEM)] * 4,
+        out_shape=jax.ShapeDtypeStruct((parts, 8, LANES), F32),
+        compiler_params=PARAMS,
+        name="message",
+    )(lax.axis_index("head").reshape(1), a_log, dt_bias, d_skip)
+    return lax.all_to_all(message, "head", split_axis=0, concat_axis=0, tiled=True).sum(axis=0)[:, :heads]
 
 
 def per_device(features, dt_raw, b_proj, c_proj, cotangent, starts, a_log, dt_bias, d_skip):
     parts = lax.axis_size(GROUP)
     tokens, heads = dt_raw.shape
-    params = gathered(jnp.stack([a_log, dt_bias, d_skip] + [d_skip] * 5), heads)
+    params = gathered(a_log, dt_bias, d_skip, heads)
     marks = lax.dynamic_slice(starts, (lax.axis_index("head") * tokens,), (tokens,)).astype(F32)
     marks = jnp.broadcast_to(marks[None], (8, tokens))
     skip = jnp.broadcast_to(jnp.repeat(params[2], HEADDIM)[None], (8, heads * HEADDIM))
-    size, sig, run, runt, reach, tail, bias, edge = prep(dt_raw, params, marks)
-    came = exchanged(states(features, cotangent, b_proj, c_proj, tail, reach, edge, parts))
+    reach, tail, edge = prep(dt_raw, params, marks, True)
+    size, sig, run, runt, bias = prep(dt_raw, params, marks, False)
+    near = staged(features, cotangent, b_proj, c_proj)
+    came = exchanged(states(*near, tail, reach, edge, parts))
     y, gx, gb, gc, col, diff = inner(features, cotangent, b_proj, c_proj, run, runt, bias, skip)
     count, here = lax.axis_size("far"), lax.axis_index("far")
     group = lax.axis_index(GROUP) * GROUPS // parts
@@ -480,11 +517,12 @@
     mask += [jnp.full((LANES,), here + by < count) for by in range(1, count)]
     mask += [lane == group, lane == GROUPS + group]
     mask = jnp.stack(mask).astype(F32)
-    total = totals(came, mask)
+    total = totals(came.astype(F32))
+    came, total = lax.optimization_barrier((came, total))
     far = [lax.ppermute(total, "far", [(p, (p + by) % count) for p in range(count)]) for by in range(1, count)]
-    left, most = entering(came, total, jnp.stack(far), mask)
+    left, most = entering(came.astype(F32), total, jnp.stack(far), mask)
     return finish(
-        exchanged(left), most, features, cotangent, b_proj, c_proj, tail, reach, y, gx, gb, gc, col, diff, size, sig, edge
+        exchanged(left).astype(F32), most, features, cotangent, b_proj, c_proj, tail, reach, y, gx, gb, gc, col, diff, size, sig, edge
     )
 
 

time: 308 us -> 303 us (0.984)
  waiting for transfers between devices: 212 us -> 204 us
    all_to_all x1, waiting for transfers between devices: 11.9 us -> 7.45 us  [gathered(): lax.all_to_all(message, 'head', split_axis=0, concat_axis=0, tiled=True)]
    unnamed x49 -> x55, local copies, waits for them, and re-layouts: 13.9 us -> 16.5 us
    convert_element_type x2 -> x3, other arithmetic: 4.22 us -> 6.17 us  [the longest x1 2.23 us: per_device(): exchanged(left).astype(F32)]
  transfers between devices with their start and end apart: 6 -> 6, of which waited for: 5 -> 4; matrix products, arithmetic and copies ran while one was open for 1% -> 1% of each run, Pallas kernels for 3% -> 3%
where the time goes in v6:
time: 303 us; the launch traced here: 302 us
  waiting for transfers between devices  204 us (67%)
  starting transfers between devices  44.7 us (15%)
  Pallas kernels  24.2 us (8%)
  local copies, waits for them, and re-layouts  17.5 us (6%)
  other arithmetic  10.6 us (3%)
    all_to_all x2, waiting for transfers between devices, exchanged(): lax.all_to_all(messages.astype(jnp.float16), GROUP, split_axis=0, concat_...  195 us
    all_to_all x1, starting transfers between devices, gathered(): lax.all_to_all(message, 'head', split_axis=0, concat_axis=0, tiled=True)  18.2 us
    unnamed x55, local copies, waits for them, and re-layouts  16.5 us
    all_to_all x2, starting transfers between devices, exchanged(): lax.all_to_all(messages.astype(jnp.float16), GROUP, split_axis=0, concat_...  16.3 us
    ppermute x3, starting transfers between devices, per_device(): lax.ppermute(total, 'far', [(p, (p + by) % count) for p in range(count)])  10.2 us
    pallas_call x1, Pallas kernels, inner(): pl.pallas_call(inner_kernel, grid=(GROUPS,), in_specs=[values, values, pr...  8.1 us
    pallas_call x1, Pallas kernels, finish(): pl.pallas_call(finish_kernel, grid=(GROUPS,), in_specs=[pl.BlockSpec((par...  7.85 us
    all_to_all x1, waiting for transfers between devices, gathered(): lax.all_to_all(message, 'head', split_axis=0, concat_axis=0, tiled=True)  7.45 us
  transfers between devices with their start and end apart: 6, of which 4 were waited for; matrix products, arithmetic and copies ran while one was open for 1% of the time, Pallas kernels for 3%

profile of v6, /device:TPU:8, one launch (start us, length us, event | category | flops | bytes accessed | tf_op | source)
XLA Modules:
  0.0 302.0 jit_solution(13645339258411340084)
XLA Ops:
  0.6 0.6 copy-done.20
  1.3 0.7 copy-done.21
  2.0 0.7 copy-done.22
  2.6 1.2 message.1
  3.8 18.2 %all-to-all-start = ((f32[16,8,128]{2,1,0:T(8,128)}), f32[16,8,128]{2,1,0:T(8,128)S(1)}, u32[]{:S(2)}, u32[]{:S(2)}) async-start(f32[16,8,128]{2,1,0:T(8,128)} %message.1), calls=%async_computation | async-start | bytes 131072 | tf_op jit(solution)/shard_map/all_to_all | solution.py:498
  22.0 0.8 copy.14.dt_ref
  22.8 1.2 copy-done
  24.1 1.2 copy-done.2
  25.3 0.9 copy-done.8
  26.2 0.9 copy-done.10
  27.1 0.2 staged.1
  27.2 0.8 dynamic-slice_convert_fusion
  28.0 7.5 %all-to-all-done = f32[16,8,128]{2,1,0:T(8,128)S(1)} async-done(((f32[16,8,128]{2,1,0:T(8,128)}), f32[16,8,128]{2,1,0:T(8,128)S(1)}, u32[]{:S(2)}, u32[]{:S(2)}) %all-to-all-start) | async-done | bytes 65568 | tf_op jit(solution)/shard_map/all_to_all | solution.py:498
  35.5 0.5 prep.2
  36.0 3.9 %states.1 = f32[128,72,128]{2,1,0:T(8,128)S(1)} custom-call(bf16[128,4096]{1,0:T(8,128)(2,1)S(1)} %get-tuple-element.27.x_ref, bf16[128,4096]{1,0:T(8,128)(2,1)S(1)} %get-tuple-element.28.w_ref, bf16[128,512]{1,0:T(8,128)(2,1)S(1)} %get-tuple-element.29.b_ref, bf16[128,512]{1,0:T(8,128)(2,1)S(1)} %get-tuple-element.30.c_ref, ...), custom_call_target="tpu_custom_call" | custom-call | flops 536870912 | bytes 7000000 | tf_op jit(solution)/shard_map/states/pallas_call | solution.py:188
  39.9 1.7 convert_element_type.22
  41.7 8.7 %all-to-all-start.1 = ((f16[128,72,128]{2,1,0:T(8,128)(2,1)}), f16[128,72,128]{2,1,0:T(8,128)(2,1)}, u32[]{:S(2)}, u32[]{:S(2)}) async-start(f16[128,72,128]{2,1,0:T(8,128)(2,1)} %convert_element_type.22), calls=%async_computation.1 | async-start | bytes 4718592 | tf_op jit(solution)/shard_map/all_to_all | solution.py:476
  50.4 111.6 %all-to-all-done.1 = f16[128,72,128]{2,1,0:T(8,128)(2,1)} async-done(((f16[128,72,128]{2,1,0:T(8,128)(2,1)}), f16[128,72,128]{2,1,0:T(8,128)(2,1)}, u32[]{:S(2)}, u32[]{:S(2)}) %all-to-all-start.1) | async-done | bytes 2359328 | tf_op jit(solution)/shard_map/all_to_all | solution.py:476
  162.0 2.0 convert_element_type.23.pay_ref
  164.0 0.9 totals.1.own_ref
  164.9 4.7 %collective-permute-start.2 = (f32[2,40,128]{2,1,0:T(8,128)S(1)}, f32[2,40,128]{2,1,0:T(8,128)S(1)}, u32[]{:S(2)}, u32[]{:S(2)}) collective-permute-start(f32[2,40,128]{2,1,0:T(8,128)S(1)} %totals.1.own_ref), channel_id=1, source_target_pairs={{0,384},{128,0},{256,128},{384,256},{1,385},{129,1},{257,129},{385... | collective-permute-start | bytes 122888 | tf_op jit(solution)/shard_map/ppermute | solution.py:522
  169.5 2.7 collective-permute-start.1
  172.2 2.8 collective-permute-start
  175.2 2.0 convert_element_type.24.pay_ref
  177.2 2.1 collective-permute-done
  179.4 1.2 entering.1
  180.5 1.9 convert_element_type.26
  182.4 7.6 %all-to-all-start.2 = ((f16[128,64,128]{2,1,0:T(8,128)(2,1)}), f16[128,64,128]{2,1,0:T(8,128)(2,1)}, u32[]{:S(2)}, u32[]{:S(2)}) async-start(f16[128,64,128]{2,1,0:T(8,128)(2,1)} %convert_element_type.26), calls=%async_computation.2 | async-start | bytes 4194304 | tf_op jit(solution)/shard_map/all_to_all | solution.py:476
  190.0 0.4 prep.3
  190.5 0.7 copy-done.23
  191.2 0.6 copy-done.25
  191.9 0.1 broadcast_in_dim.18
  192.0 0.9 copy-done.24
  193.0 0.8 copy-done.26
  193.7 8.1 %inner.1 = (f32[128,4096]{1,0:T(8,128)S(1)}, f32[128,4096]{1,0:T(8,128)S(1)}, f32[128,512]{1,0:T(8,128)S(1)}, f32[128,512]{1,0:T(8,128)S(1)}, f32[4,128,16]{2,1,0:T(8,128)S(1)}, /*index=5*/f32[4,128,16]{2,1,0:T(8,128)S(1)}) custom-call(bf16[128,4096]{1,0:T(8,128)(2,1)S(1)} %copy-done.1, bf16[128,4096]{1,0:T(8,128)(2,1)S(1)} %copy-done.3, ...), custom_call_target="tpu_custom_call" | custom-call | flops 20000000000 | bytes 8000000 | tf_op jit(solution)/shard_map/inner/pallas_call | solution.py:344
  201.8 1.4 copy-done.4
  203.2 1.4 copy-done.6
  204.6 0.7 copy-done.12
  205.3 0.7 copy-done.14
  206.0 0.7 copy-done.16
  206.8 0.7 copy-done.18
  207.5 82.9 %all-to-all-done.2 = f16[128,64,128]{2,1,0:T(8,128)(2,1)} async-done(((f16[128,64,128]{2,1,0:T(8,128)(2,1)}), f16[128,64,128]{2,1,0:T(8,128)(2,1)}, u32[]{:S(2)}, u32[]{:S(2)}) %all-to-all-start.2) | async-done | bytes 2097184 | tf_op jit(solution)/shard_map/all_to_all | solution.py:476
  290.4 2.2 convert_element_type.27.pay_ref
  292.7 0.6 copy-done.7
  293.3 0.1 copy-done.17
  293.4 0.1 copy-done.19
  293.5 7.8 %finish.1 = (bf16[128,4096]{1,0:T(8,128)(2,1)}, bf16[128,4096]{1,0:T(8,128)(2,1)}, bf16[128,64]{1,0:T(8,128)(2,1)S(1)}, bf16[128,512]{1,0:T(8,128)(2,1)}, bf16[128,512]{1,0:T(8,128)(2,1)}) custom-call(f32[128,64,128]{2,1,0:T(8,128)S(1)} %convert_element_type.27.pay_ref, f32[8,128]{1,0:T(8,128)S(1)} %get-tuple-element.37.most_ref, ...), custom_call_target="tpu_custom_call" | custom-call | flops 1342177280 | bytes 14000000 | tf_op jit(solution)/shard_map/finish/pallas_call | solution.py:444
  301.3 0.7 copy.16
  (51 shorter events, 0.4 us)
Async XLA Ops:
  0.6 0.7 copy-start.20
  1.3 0.7 copy-start.21
  1.9 0.7 copy-start.22
  3.8 31.7 %all-to-all-start = ((f32[16,8,128]{2,1,0:T(8,128)}), f32[16,8,128]{2,1,0:T(8,128)S(1)}, u32[]{:S(2)}, u32[]{:S(2)}) async-start(f32[16,8,128]{2,1,0:T(8,128)} %message.1), calls=%async_computation | async-start | bytes 131072 | tf_op jit(solution)/shard_map/all_to_all | solution.py:498
  22.8 1.2 copy-start
  24.1 1.2 copy-start.2
  25.3 0.9 copy-start.8
  26.2 0.9 copy-start.10
  41.7 120.3 %all-to-all-start.1 = ((f16[128,72,128]{2,1,0:T(8,128)(2,1)}), f16[128,72,128]{2,1,0:T(8,128)(2,1)}, u32[]{:S(2)}, u32[]{:S(2)}) async-start(f16[128,72,128]{2,1,0:T(8,128)(2,1)} %convert_element_type.22), calls=%async_computation.1 | async-start | bytes 4718592 | tf_op jit(solution)/shard_map/all_to_all | solution.py:476
  164.9 12.3 %collective-permute-start.2 = (f32[2,40,128]{2,1,0:T(8,128)S(1)}, f32[2,40,128]{2,1,0:T(8,128)S(1)}, u32[]{:S(2)}, u32[]{:S(2)}) collective-permute-start(f32[2,40,128]{2,1,0:T(8,128)S(1)} %totals.1.own_ref), channel_id=1, source_target_pairs={{0,384},{128,0},{256,128},{384,256},{1,385},{129,1},{257,129},{385... | collective-permute-start | bytes 122888 | tf_op jit(solution)/shard_map/ppermute | solution.py:522
  169.5 7.7 %collective-permute-start.1 = (f32[2,40,128]{2,1,0:T(8,128)S(1)}, f32[2,40,128]{2,1,0:T(8,128)S(1)}, u32[]{:S(2)}, u32[]{:S(2)}) collective-permute-start(f32[2,40,128]{2,1,0:T(8,128)S(1)} %totals.1.own_ref), channel_id=1, source_target_pairs={{0,256},{128,384},{256,0},{384,128},{1,257},{129,385},{257,1},{385... | collective-permute-start | bytes 122888 | tf_op jit(solution)/shard_map/ppermute | solution.py:522
  172.2 7.1 %collective-permute-start = (f32[2,40,128]{2,1,0:T(8,128)S(1)}, f32[2,40,128]{2,1,0:T(8,128)S(1)}, u32[]{:S(2)}, u32[]{:S(2)}) collective-permute-start(f32[2,40,128]{2,1,0:T(8,128)S(1)} %totals.1.own_ref), channel_id=1, source_target_pairs={{0,128},{128,256},{256,384},{384,0},{1,129},{129,257},{257,385},{3... | collective-permute-start | bytes 122888 | tf_op jit(solution)/shard_map/ppermute | solution.py:522
  182.4 9.5 %copy-start.1 = (bf16[128,4096]{1,0:T(8,128)(2,1)S(1)}, bf16[128,4096]{1,0:T(8,128)(2,1)}, u32[]{:S(2)}) copy-start(bf16[128,4096]{1,0:T(8,128)(2,1)} %x_ref.3) | copy-start | bytes 3145732
  182.4 9.6 %copy-start.3 = (bf16[128,4096]{1,0:T(8,128)(2,1)S(1)}, bf16[128,4096]{1,0:T(8,128)(2,1)}, u32[]{:S(2)}) copy-start(bf16[128,4096]{1,0:T(8,128)(2,1)} %w_ref.3) | copy-start | bytes 3145732
  182.4 9.6 %copy-start.9 = (bf16[128,512]{1,0:T(8,128)(2,1)S(1)}, bf16[128,512]{1,0:T(8,128)(2,1)}, u32[]{:S(2)}) copy-start(bf16[128,512]{1,0:T(8,128)(2,1)} %b_ref.3) | copy-start | bytes 393220
  182.4 9.6 %copy-start.11 = (bf16[128,512]{1,0:T(8,128)(2,1)S(1)}, bf16[128,512]{1,0:T(8,128)(2,1)}, u32[]{:S(2)}) copy-start(bf16[128,512]{1,0:T(8,128)(2,1)} %c_ref.3) | copy-start | bytes 393220
  182.4 108.0 %all-to-all-start.2 = ((f16[128,64,128]{2,1,0:T(8,128)(2,1)}), f16[128,64,128]{2,1,0:T(8,128)(2,1)}, u32[]{:S(2)}, u32[]{:S(2)}) async-start(f16[128,64,128]{2,1,0:T(8,128)(2,1)} %convert_element_type.26), calls=%async_computation.2 | async-start | bytes 4194304 | tf_op jit(solution)/shard_map/all_to_all | solution.py:476
  190.5 0.7 copy-start.23
  191.2 0.6 copy-start.25
  192.0 1.0 copy-start.24
  193.0 0.8 copy-start.26
  201.8 1.4 copy-start.4
  203.2 1.4 copy-start.6
  204.6 0.7 copy-start.12
  205.3 0.7 copy-start.14
  206.0 0.7 copy-start.16
  206.8 0.7 copy-start.18
  290.4 2.3 copy-start.5
  290.4 2.9 copy-start.7
  290.4 2.9 copy-start.13
  290.4 2.9 copy-start.15
  290.4 3.0 copy-start.17
  290.4 3.1 %copy-start.19 = (f32[4,128,16]{2,1,0:T(8,128)S(1)}, f32[4,128,16]{2,1,0:T(8,128)}, u32[]{:S(2)}) copy-start(f32[4,128,16]{2,1,0:T(8,128)} %copy-done.18) | copy-start | bytes 98308

commit v7 on v6

--- a/solution.py
+++ b/solution.py
@@ -134,68 +134,50 @@
     )(*arrays)
 
 
-def state_of(val_ref, proj_ref, scale_ref):
-    high, low = split(val_ref[...].astype(F32) * widen(scale_ref[0]))
-    proj = proj_ref[...]
+def state_of(values, proj, scale):
+    high, low = split(values.astype(F32) * widen(scale))
     return dot(jnp.concatenate([proj, proj], axis=0), jnp.concatenate([high, low], axis=0), ((0,), (0,)))
 
 
-def state_kernel(x_ref, w_ref, b_ref, c_ref, tail_ref, reach_ref, edge_ref, out_ref, piece_ref, power_ref, spread_ref):
-    g = pl.program_id(0)
+def state_kernel(x_ref, w_ref, b_ref, c_ref, tail_ref, reach_ref, edge_ref, out_ref):
     messages, rows, _ = out_ref.shape
+    wide = x_ref.shape[1] // GROUPS
     part = (rows - 8) // 2
     fold = STATE // part
     per_group = messages // GROUPS
     row, lane = iota((8, LANES), 0), iota((8, LANES), 1)
-    piece_ref[g] = dot(edge_ref[0].astype(BF16), spread_map(tail_ref.shape[2], BF16))
-    powers = jnp.zeros((8, LANES), F32)
-    spread = jnp.zeros((8, LANES), F32)
-    for which, state in enumerate((state_of(x_ref, b_ref, tail_ref), state_of(w_ref, c_ref, reach_ref))):
-        power = exponent_of(state)
-        spread = jnp.where(row == 4 + which, power, spread)
-        powers = jnp.where(lane == which * GROUPS + g, power, powers)
-        state = state * jnp.exp2(TOP - power)
+    all_powers = jnp.zeros((8, LANES), F32)
+    sides = []
+    for g in range(GROUPS):
+        mine, own = slice(g * wide, (g + 1) * wide), slice(g * STATE, (g + 1) * STATE)
+        pieces = dot(edge_ref[g].astype(BF16), spread_map(tail_ref.shape[2], BF16))
+        spread = jnp.zeros((8, LANES), F32)
+        for which, (val_ref, proj_ref, scale_ref) in enumerate(
+            ((x_ref, b_ref, tail_ref), (w_ref, c_ref, reach_ref))
+        ):
+            state = state_of(val_ref[:, mine], proj_ref[:, own], scale_ref[g])
+            power = exponent_of(state)
+            spread = jnp.where(row == 4 + which, power, spread)
+            all_powers = jnp.where(lane == which * GROUPS + g, power, all_powers)
+            state = state * jnp.exp2(TOP - power)
+            for k in range(per_group):
+                lanes = slice(k // fold * LANES, (k // fold + 1) * LANES)
+                here = slice(k % fold * part, (k % fold + 1) * part)
+                out_ref[g * per_group + k, which * part : (which + 1) * part] = state[here, lanes]
+        sides.append((pieces, spread))
+    for g, (pieces, spread) in enumerate(sides):
+        side = jnp.where(row == 3, all_powers, spread)
         for k in range(per_group):
             lanes = slice(k // fold * LANES, (k // fold + 1) * LANES)
-            here = slice(k % fold * part, (k % fold + 1) * part)
-            out_ref[g * per_group + k, which * part : (which + 1) * part] = state[here, lanes]
-    spread_ref[g] = spread
-
-    @pl.when(g == 0)
-    def _():
-        power_ref[...] = powers
-
-    @pl.when(g > 0)
-    def _():
-        power_ref[...] += powers
-
-    @pl.when(g == GROUPS - 1)
-    def _():
-        for k in range(messages):
-            lanes = slice(k % per_group // fold * LANES, (k % per_group // fold + 1) * LANES)
-            side = jnp.where(row == 3, power_ref[...], spread_ref[k // per_group])
-            out_ref[k, 2 * part :] = jnp.where(row < 3, piece_ref[k // per_group, :, lanes], side)
+            out_ref[g * per_group + k, 2 * part :] = jnp.where(row < 3, pieces[:, lanes], side)
 
 
 def states(x, w, b, c, tail, reach, edge, parts):
     tokens, channels = x.shape
-    wide = channels // GROUPS
-    per = tail.shape[2]
     rows = 2 * STATE * channels // (parts * LANES) + 8
-    values = pl.BlockSpec((tokens, wide), lambda g: (0, g))
-    proj = pl.BlockSpec((tokens, STATE), lambda g: (0, g))
-    small = pl.BlockSpec((1, tokens, per), lambda g: (g, 0, 0))
     return pl.pallas_call(
         state_kernel,
-        grid=(GROUPS,),
-        in_specs=[values, values, proj, proj, small, small, pl.BlockSpec((1, 8, per), lambda g: (g, 0, 0))],
-        out_specs=pl.BlockSpec((parts, rows, LANES), lambda g: (0, 0, 0)),
         out_shape=jax.ShapeDtypeStruct((parts, rows, LANES), F32),
-        scratch_shapes=[
-            pltpu.VMEM((GROUPS, 8, wide), F32),
-            pltpu.VMEM((8, LANES), F32),
-            pltpu.VMEM((GROUPS, 8, LANES), F32),
-        ],
         compiler_params=PARAMS,
         cost_estimate=pl.CostEstimate(flops=8 * tokens * STATE * channels, bytes_accessed=7000000, transcendentals=0),
         name="states",
@@ -371,98 +353,95 @@
 
 def state_from(pay_ref, most_ref, group, which):
     messages, rows, _ = pay_ref.shape
+    per_group = messages // GROUPS
     part = rows // 2
     fold = STATE // part
     here = slice(which * part, (which + 1) * part)
-    most = most_ref[1:2]
-    mine = iota(most.shape, 1) == which * GROUPS + group
-    power = jnp.sum(jnp.where(mine, most, 0.0), axis=1, keepdims=True)
+    lane = which * GROUPS + group
+    power = most_ref[1:2, lane : lane + 1]
     columns = []
-    for first in range(0, messages, fold):
+    for first in range(group * per_group, (group + 1) * per_group, fold):
         columns.append(jnp.concatenate([pay_ref[first + k, here] for k in range(fold)], axis=0))
     return jnp.concatenate(columns, axis=1) * jnp.exp2(power - (TOP + 2.0 - BITS))
 
 
-def carried_terms(state, values, scale_ref, proj_ref):
-    wide = widen(scale_ref[0])
-    proj = proj_ref[...]
+def carried_terms(state, values, scale, proj):
+    wide = widen(scale)
     high, low = split(state)
     terms = dot(jnp.concatenate([proj, proj], axis=1), jnp.concatenate([high, low], axis=0)) * wide
     left_high, left_low = split(values * wide)
     last = ((1,), (1,))
-    grad = dot(left_high, high, last) + (dot(left_high, low, last) + dot(left_low, high, last))
+    both = dot(jnp.concatenate([left_high, left_low], axis=0), high, last)
+    tokens = values.shape[0]
+    grad = both[:tokens] + (both[tokens:] + dot(left_high, low, last))
     return terms, grad, head_sums(terms * values)
 
 
 def finish_kernel(
     pay_ref, most_ref, x_ref, w_ref, b_ref, c_ref, tail_ref, reach_ref, y_ref, gx_ref, gb_ref, gc_ref, col_ref, diff_ref, size_ref, sig_ref, edge_ref,
-    mixed_ref, gradx_ref, dt_ref, gradb_ref, gradc_ref, rows_ref, cols_ref, met_ref,
+    mixed_out, gradx_out, dt_ref, gradb_out, gradc_out, mixed_ref, gradx_ref, gradb_ref, gradc_ref, sems,
 ):
-    g = pl.program_id(0)
-    tokens, _ = x_ref.shape
-    enter, leave = state_from(pay_ref, most_ref, g, 0), state_from(pay_ref, most_ref, g, 1)
-    terms, grad, rows = carried_terms(enter, w_ref[...].astype(F32), reach_ref, c_ref)
-    mixed_ref[...] = (y_ref[...] + terms).astype(BF16)
-    gradc_ref[...] = (gc_ref[...] + grad).astype(BF16)
-    terms, grad, cols = carried_terms(leave, x_ref[...].astype(F32), tail_ref, b_ref)
-    gradx_ref[...] = (gx_ref[...] + terms).astype(BF16)
-    gradb_ref[...] = (gb_ref[...] + grad).astype(BF16)
-    met = jnp.sum(enter * leave, axis=0, keepdims=True)
-    rows_ref[g] = rows
-    cols_ref[g] = cols
-    met_ref[g] = head_sums(jnp.broadcast_to(met, (8, met.shape[1])))
-
-    @pl.when(g == GROUPS - 1)
-    def _():
-        def whole(ref):
-            return jnp.concatenate([ref[k] for k in range(GROUPS)], axis=1)
-
-        edge = whole(edge_ref)
-        keep, decay = edge[3:4], edge[4:5]
-        shape = (tokens, tokens)
-        from_here = (iota(shape, 0) <= iota(shape, 1)).astype(F32)
-        before = (iota(shape, 0) > iota(shape, 1)).astype(F32)
-        late = whole(cols_ref)
-        grad_rate = (
-            dot(from_here, whole(diff_ref) + whole(rows_ref), precision=PRECISE)
-            + dot(before, late, precision=PRECISE)
-            + keep * whole(met_ref)[0:1]
-        )
-        grad_size = (whole(col_ref) + late) / whole(size_ref) + decay * grad_rate
-        dt_ref[...] = (grad_size * whole(sig_ref)).astype(BF16)
+    tokens, channels = x_ref.shape
+    wide = channels // GROUPS
+    rows, cols, met, copies = [], [], [], []
+    for g in range(GROUPS):
+        mine, own = slice(g * wide, (g + 1) * wide), slice(g * STATE, (g + 1) * STATE)
+        enter, leave = state_from(pay_ref, most_ref, g, 0), state_from(pay_ref, most_ref, g, 1)
+        terms, grad, sums = carried_terms(enter, w_ref[:, mine].astype(F32), reach_ref[g], c_ref[:, own])
+        mixed_ref[:, mine] = (y_ref[:, mine] + terms).astype(BF16)
+        gradc_ref[:, own] = (gc_ref[:, own] + grad).astype(BF16)
+        rows.append(sums)
+        terms, grad, sums = carried_terms(leave, x_ref[:, mine].astype(F32), tail_ref[g], b_ref[:, own])
+        gradx_ref[:, mine] = (gx_ref[:, mine] + terms).astype(BF16)
+        gradb_ref[:, own] = (gb_ref[:, own] + grad).astype(BF16)
+        cols.append(sums)
+        for k, (source, target, here) in enumerate(
+            (
+                (mixed_ref, mixed_out, mine),
+                (gradx_ref, gradx_out, mine),
+                (gradb_ref, gradb_out, own),
+                (gradc_ref, gradc_out, own),
+            )
+        ):
+            copy = pltpu.make_async_copy(source.at[:, here], target.at[:, here], sems.at[g, k])
+            copy.start()
+            copies.append(copy)
+        both = jnp.sum(enter * leave, axis=0, keepdims=True)
+        met.append(head_sums(jnp.broadcast_to(both, (8, wide))))
+
+    def whole(parts):
+        return jnp.concatenate([parts[k] for k in range(GROUPS)], axis=1)
+
+    edge = whole(edge_ref)
+    keep, decay = edge[3:4], edge[4:5]
+    shape = (tokens, tokens)
+    from_here = (iota(shape, 0) <= iota(shape, 1)).astype(F32)
+    before = (iota(shape, 0) > iota(shape, 1)).astype(F32)
+    late = whole(cols)
+    grad_rate = (
+        dot(from_here, whole(diff_ref) + whole(rows), precision=PRECISE)
+        + dot(before, late, precision=PRECISE)
+        + keep * whole(met)[0:1]
+    )
+    grad_size = (whole(col_ref) + late) / whole(size_ref) + decay * grad_rate
+    dt_ref[...] = (grad_size * whole(sig_ref)).astype(BF16)
+    for copy in copies:
+        copy.wait()
 
 
 def finish(pay, most, x, w, b, c, tail, reach, y, gx, gb, gc, col, diff, size, sig, edge):
     tokens, channels = x.shape
-    parts, rows, _ = pay.shape
-    wide = channels // GROUPS
-    per = tail.shape[2]
-    values = pl.BlockSpec((tokens, wide), lambda g: (0, g))
-    proj = pl.BlockSpec((tokens, STATE), lambda g: (0, g))
-    small = pl.BlockSpec((1, tokens, per), lambda g: (g, 0, 0))
-    every = pl.BlockSpec((GROUPS, tokens, per), lambda g: (0, 0, 0))
+    heads = channels // HEADDIM
+    shapes = [(tokens, channels), (tokens, channels), (tokens, heads), b.shape, b.shape]
+    close = pl.BlockSpec(memory_space=pltpu.VMEM)
+    far = pl.BlockSpec(memory_space=pl.ANY)
     return pl.pallas_call(
         finish_kernel,
-        grid=(GROUPS,),
-        in_specs=[
-            pl.BlockSpec((parts // GROUPS, rows, LANES), lambda g: (g, 0, 0)),
-            pl.BlockSpec((8, LANES), lambda g: (0, 0)),
-            values, values, proj, proj, small, small, values, values, proj, proj, every, every, every, every,
-            pl.BlockSpec((GROUPS, 8, per), lambda g: (0, 0, 0)),
-        ],
-        out_specs=[values, values, pl.BlockSpec((tokens, GROUPS * per), lambda g: (0, 0)), proj, proj],
-        out_shape=[
-            jax.ShapeDtypeStruct((tokens, channels), BF16),
-            jax.ShapeDtypeStruct((tokens, channels), BF16),
-            jax.ShapeDtypeStruct((tokens, GROUPS * per), BF16),
-            jax.ShapeDtypeStruct((tokens, GROUPS * STATE), BF16),
-            jax.ShapeDtypeStruct((tokens, GROUPS * STATE), BF16),
-        ],
-        scratch_shapes=[
-            pltpu.VMEM((GROUPS, tokens, per), F32),
-            pltpu.VMEM((GROUPS, tokens, per), F32),
-            pltpu.VMEM((GROUPS, 8, per), F32),
-        ],
+        in_specs=[close] * 17,
+        out_specs=[far, far, close, far, far],
+        out_shape=[jax.ShapeDtypeStruct(shape, BF16) for shape in shapes],
+        scratch_shapes=[pltpu.VMEM(shape, BF16) for shape in (shapes[0], shapes[1], shapes[3], shapes[4])]
+        + [pltpu.SemaphoreType.DMA((GROUPS, 4))],
         compiler_params=PARAMS,
         cost_estimate=pl.CostEstimate(flops=20 * tokens * STATE * channels, bytes_accessed=14_000_000, transcendentals=0),
         name="finish",
@@ -476,32 +455,19 @@
     return lax.all_to_all(messages.astype(jnp.float16), GROUP, split_axis=0, concat_axis=0, tiled=True)
 
 
-def message_kernel(mine_ref, a_ref, bias_ref, skip_ref, out_ref):
-    row, lane = iota((8, LANES), 0), iota((8, LANES), 1)
-    per_dev = a_ref.shape[0]
-    value = jnp.zeros((8, LANES), F32)
-    for k, ref in enumerate((a_ref, bias_ref, skip_ref)):
-        for i in range(per_dev):
-            value = jnp.where((row == k) & (lane == mine_ref[0] * per_dev + i), ref[i], value)
-    out_ref[...] = jnp.broadcast_to(value[None], out_ref.shape)
-
-
-def gathered(a_log, dt_bias, d_skip, heads):
+def gathered(own, heads):
     parts = lax.axis_size("head")
-    message = pl.pallas_call(
-        message_kernel,
-        in_specs=[pl.BlockSpec(memory_space=pltpu.SMEM)] * 4,
-        out_shape=jax.ShapeDtypeStruct((parts, 8, LANES), F32),
-        compiler_params=PARAMS,
-        name="message",
-    )(lax.axis_index("head").reshape(1), a_log, dt_bias, d_skip)
-    return lax.all_to_all(message, "head", split_axis=0, concat_axis=0, tiled=True).sum(axis=0)[:, :heads]
+    per_dev = own.shape[1]
+    mine = lax.axis_index("head")
+    whole = jnp.where(iota((8, LANES), 1) // per_dev == mine, jnp.tile(own, (1, LANES // per_dev)), 0.0)
+    whole = jnp.broadcast_to(whole[None], (parts, 8, LANES))
+    return lax.all_to_all(whole, "head", split_axis=0, concat_axis=0, tiled=True).sum(axis=0)[:, :heads]
 
 
 def per_device(features, dt_raw, b_proj, c_proj, cotangent, starts, a_log, dt_bias, d_skip):
     parts = lax.axis_size(GROUP)
     tokens, heads = dt_raw.shape
-    params = gathered(a_log, dt_bias, d_skip, heads)
+    params = gathered(jnp.stack([a_log, dt_bias, d_skip] + [d_skip] * 5), heads)
     marks = lax.dynamic_slice(starts, (lax.axis_index("head") * tokens,), (tokens,)).astype(F32)
     marks = jnp.broadcast_to(marks[None], (8, tokens))
     skip = jnp.broadcast_to(jnp.repeat(params[2], HEADDIM)[None], (8, heads * HEADDIM))

time: 303 us -> 299 us (0.987)
  Pallas kernels: 24.2 us -> 20.1 us
    pallas_call x3 -> x2, Pallas kernels: 13 us -> 8.84 us  [the longest x1 6.21 us: finish(): pl.pallas_call(finish_kernel, in_specs=[close] * 17, out_specs=[far, far,...]
    unnamed x55 -> x49, local copies, waits for them, and re-layouts: 16.5 us -> 14.5 us
where the time goes in v7:
time: 299 us; the launch traced here: 298 us
  waiting for transfers between devices  204 us (68%)
  starting transfers between devices  44.7 us (15%)
  Pallas kernels  20.1 us (7%)
  local copies, waits for them, and re-layouts  17.2 us (6%)
  other arithmetic  10.7 us (4%)
    all_to_all x2, waiting for transfers between devices, exchanged(): lax.all_to_all(messages.astype(jnp.float16), GROUP, split_axis=0, concat_...  195 us
    all_to_all x1, starting transfers between devices, gathered(): lax.all_to_all(whole, 'head', split_axis=0, concat_axis=0, tiled=True)  18.2 us
    all_to_all x2, starting transfers between devices, exchanged(): lax.all_to_all(messages.astype(jnp.float16), GROUP, split_axis=0, concat_...  16.3 us
    unnamed x49, local copies, waits for them, and re-layouts  14.5 us
    ppermute x3, starting transfers between devices, per_device(): lax.ppermute(total, 'far', [(p, (p + by) % count) for p in range(count)])  10.2 us
    pallas_call x1, Pallas kernels, inner(): pl.pallas_call(inner_kernel, grid=(GROUPS,), in_specs=[values, values, pr...  8.1 us
    all_to_all x1, waiting for transfers between devices, gathered(): lax.all_to_all(whole, 'head', split_axis=0, concat_axis=0, tiled=True)  7.45 us
    pallas_call x1, Pallas kernels, finish(): pl.pallas_call(finish_kernel, in_specs=[close] * 17, out_specs=[far, far,...  6.21 us
  transfers between devices with their start and end apart: 6, of which 4 were waited for; matrix products, arithmetic and copies ran while one was open for 1% of the time, Pallas kernels for 3%

profile of v7, /device:TPU:8, one launch (start us, length us, event | category | flops | bytes accessed | tf_op | source)
XLA Modules:
  0.0 297.8 jit_solution(6604980115193854711)
XLA Ops:
  0.7 0.9 stack.37
  1.6 0.1 copy.22
  1.7 0.1 fusion
  1.8 0.7 broadcast_in_dim.27
  2.5 18.2 %all-to-all-start = ((f32[16,8,128]{2,1,0:T(8,128)}), f32[16,8,128]{2,1,0:T(8,128)S(1)}, u32[]{:S(2)}, u32[]{:S(2)}) async-start(f32[16,8,128]{2,1,0:T(8,128)} %broadcast_in_dim.27), calls=%async_computation | async-start | bytes 131072 | tf_op jit(solution)/shard_map/all_to_all | solution.py:464
  20.7 0.8 copy.24.dt_ref
  21.5 1.2 copy-done
  22.7 1.2 copy-done.2
  24.0 0.9 copy-done.8
  24.9 0.9 copy-done.10
  25.8 0.2 staged.1
  25.9 0.8 dynamic-slice_convert_fusion
  26.7 7.5 %all-to-all-done = f32[16,8,128]{2,1,0:T(8,128)S(1)} async-done(((f32[16,8,128]{2,1,0:T(8,128)}), f32[16,8,128]{2,1,0:T(8,128)S(1)}, u32[]{:S(2)}, u32[]{:S(2)}) %all-to-all-start) | async-done | bytes 65568 | tf_op jit(solution)/shard_map/all_to_all | solution.py:464
  34.2 0.5 prep.2
  34.7 2.6 states.1
  37.3 1.7 convert_element_type.22
  39.0 8.7 %all-to-all-start.1 = ((f16[128,72,128]{2,1,0:T(8,128)(2,1)}), f16[128,72,128]{2,1,0:T(8,128)(2,1)}, u32[]{:S(2)}, u32[]{:S(2)}) async-start(f16[128,72,128]{2,1,0:T(8,128)(2,1)} %convert_element_type.22), calls=%async_computation.1 | async-start | bytes 4718592 | tf_op jit(solution)/shard_map/all_to_all | solution.py:455
  47.8 111.6 %all-to-all-done.1 = f16[128,72,128]{2,1,0:T(8,128)(2,1)} async-done(((f16[128,72,128]{2,1,0:T(8,128)(2,1)}), f16[128,72,128]{2,1,0:T(8,128)(2,1)}, u32[]{:S(2)}, u32[]{:S(2)}) %all-to-all-start.1) | async-done | bytes 2359328 | tf_op jit(solution)/shard_map/all_to_all | solution.py:455
  159.4 2.0 convert_element_type.23.pay_ref
  161.3 0.9 totals.1.own_ref
  162.3 4.7 %collective-permute-start.2 = (f32[2,40,128]{2,1,0:T(8,128)S(1)}, f32[2,40,128]{2,1,0:T(8,128)S(1)}, u32[]{:S(2)}, u32[]{:S(2)}) collective-permute-start(f32[2,40,128]{2,1,0:T(8,128)S(1)} %totals.1.own_ref), channel_id=1, source_target_pairs={{0,384},{128,0},{256,128},{384,256},{1,385},{129,1},{257,129},{385... | collective-permute-start | bytes 122888 | tf_op jit(solution)/shard_map/ppermute | solution.py:488
  166.9 2.7 collective-permute-start.1
  169.6 2.8 collective-permute-start
  172.6 2.0 convert_element_type.24.pay_ref
  174.6 2.1 collective-permute-done
  176.8 1.2 entering.1
  177.9 1.9 convert_element_type.26
  179.8 7.6 %all-to-all-start.2 = ((f16[128,64,128]{2,1,0:T(8,128)(2,1)}), f16[128,64,128]{2,1,0:T(8,128)(2,1)}, u32[]{:S(2)}, u32[]{:S(2)}) async-start(f16[128,64,128]{2,1,0:T(8,128)(2,1)} %convert_element_type.26), calls=%async_computation.2 | async-start | bytes 4194304 | tf_op jit(solution)/shard_map/all_to_all | solution.py:455
  187.4 0.4 prep.3
  187.9 0.7 copy-done.20
  188.6 0.6 copy-done.22
  189.3 0.1 broadcast_in_dim.30
  189.4 0.9 copy-done.21
  190.3 0.8 copy-done.23
  191.1 8.1 %inner.1 = (f32[128,4096]{1,0:T(8,128)S(1)}, f32[128,4096]{1,0:T(8,128)S(1)}, f32[128,512]{1,0:T(8,128)S(1)}, f32[128,512]{1,0:T(8,128)S(1)}, f32[4,128,16]{2,1,0:T(8,128)S(1)}, /*index=5*/f32[4,128,16]{2,1,0:T(8,128)S(1)}) custom-call(bf16[128,4096]{1,0:T(8,128)(2,1)S(1)} %copy-done.1, bf16[128,4096]{1,0:T(8,128)(2,1)S(1)} %copy-done.3, ...), custom_call_target="tpu_custom_call" | custom-call | flops 20000000000 | bytes 8000000 | tf_op jit(solution)/shard_map/inner/pallas_call | solution.py:326
  199.2 1.4 copy-done.4
  200.6 1.4 copy-done.6
  202.0 0.7 copy-done.12
  202.7 0.7 copy-done.14
  203.4 0.7 copy-done.16
  204.1 0.7 copy-done.18
  204.8 83.0 %all-to-all-done.2 = f16[128,64,128]{2,1,0:T(8,128)(2,1)} async-done(((f16[128,64,128]{2,1,0:T(8,128)(2,1)}), f16[128,64,128]{2,1,0:T(8,128)(2,1)}, u32[]{:S(2)}, u32[]{:S(2)}) %all-to-all-start.2) | async-done | bytes 2097184 | tf_op jit(solution)/shard_map/all_to_all | solution.py:455
  287.8 2.2 convert_element_type.27.pay_ref
  290.1 0.6 copy-done.7
  290.7 0.1 copy-done.17
  290.8 0.1 copy-done.19
  290.9 6.2 %finish.1 = (bf16[128,4096]{1,0:T(8,128)(2,1)}, bf16[128,4096]{1,0:T(8,128)(2,1)}, bf16[128,64]{1,0:T(8,128)(2,1)S(1)}, bf16[128,512]{1,0:T(8,128)(2,1)}, bf16[128,512]{1,0:T(8,128)(2,1)}) custom-call(f32[128,64,128]{2,1,0:T(8,128)S(1)} %convert_element_type.27.pay_ref, f32[8,128]{1,0:T(8,128)S(1)} %get-tuple-element.37.most_ref, ...), custom_call_target="tpu_custom_call" | custom-call | flops 1342177280 | bytes 14000000 | tf_op jit(solution)/shard_map/finish/pallas_call | solution.py:438
  297.1 0.7 copy.26
  (52 shorter events, 0.4 us)
Async XLA Ops:
  2.5 31.7 %all-to-all-start = ((f32[16,8,128]{2,1,0:T(8,128)}), f32[16,8,128]{2,1,0:T(8,128)S(1)}, u32[]{:S(2)}, u32[]{:S(2)}) async-start(f32[16,8,128]{2,1,0:T(8,128)} %broadcast_in_dim.27), calls=%async_computation | async-start | bytes 131072 | tf_op jit(solution)/shard_map/all_to_all | solution.py:464
  21.5 1.2 copy-start
  22.7 1.2 copy-start.2
  24.0 0.9 copy-start.8
  24.9 0.9 copy-start.10
  39.0 120.3 %all-to-all-start.1 = ((f16[128,72,128]{2,1,0:T(8,128)(2,1)}), f16[128,72,128]{2,1,0:T(8,128)(2,1)}, u32[]{:S(2)}, u32[]{:S(2)}) async-start(f16[128,72,128]{2,1,0:T(8,128)(2,1)} %convert_element_type.22), calls=%async_computation.1 | async-start | bytes 4718592 | tf_op jit(solution)/shard_map/all_to_all | solution.py:455
  162.3 12.3 %collective-permute-start.2 = (f32[2,40,128]{2,1,0:T(8,128)S(1)}, f32[2,40,128]{2,1,0:T(8,128)S(1)}, u32[]{:S(2)}, u32[]{:S(2)}) collective-permute-start(f32[2,40,128]{2,1,0:T(8,128)S(1)} %totals.1.own_ref), channel_id=1, source_target_pairs={{0,384},{128,0},{256,128},{384,256},{1,385},{129,1},{257,129},{385... | collective-permute-start | bytes 122888 | tf_op jit(solution)/shard_map/ppermute | solution.py:488
  166.9 7.7 %collective-permute-start.1 = (f32[2,40,128]{2,1,0:T(8,128)S(1)}, f32[2,40,128]{2,1,0:T(8,128)S(1)}, u32[]{:S(2)}, u32[]{:S(2)}) collective-permute-start(f32[2,40,128]{2,1,0:T(8,128)S(1)} %totals.1.own_ref), channel_id=1, source_target_pairs={{0,256},{128,384},{256,0},{384,128},{1,257},{129,385},{257,1},{385... | collective-permute-start | bytes 122888 | tf_op jit(solution)/shard_map/ppermute | solution.py:488
  169.6 7.1 %collective-permute-start = (f32[2,40,128]{2,1,0:T(8,128)S(1)}, f32[2,40,128]{2,1,0:T(8,128)S(1)}, u32[]{:S(2)}, u32[]{:S(2)}) collective-permute-start(f32[2,40,128]{2,1,0:T(8,128)S(1)} %totals.1.own_ref), channel_id=1, source_target_pairs={{0,128},{128,256},{256,384},{384,0},{1,129},{129,257},{257,385},{3... | collective-permute-start | bytes 122888 | tf_op jit(solution)/shard_map/ppermute | solution.py:488
  179.8 9.5 %copy-start.1 = (bf16[128,4096]{1,0:T(8,128)(2,1)S(1)}, bf16[128,4096]{1,0:T(8,128)(2,1)}, u32[]{:S(2)}) copy-start(bf16[128,4096]{1,0:T(8,128)(2,1)} %x_ref.3) | copy-start | bytes 3145732
  179.8 9.6 %copy-start.3 = (bf16[128,4096]{1,0:T(8,128)(2,1)S(1)}, bf16[128,4096]{1,0:T(8,128)(2,1)}, u32[]{:S(2)}) copy-start(bf16[128,4096]{1,0:T(8,128)(2,1)} %w_ref.3) | copy-start | bytes 3145732
  179.8 9.6 %copy-start.9 = (bf16[128,512]{1,0:T(8,128)(2,1)S(1)}, bf16[128,512]{1,0:T(8,128)(2,1)}, u32[]{:S(2)}) copy-start(bf16[128,512]{1,0:T(8,128)(2,1)} %b_ref.3) | copy-start | bytes 393220
  179.8 9.6 %copy-start.11 = (bf16[128,512]{1,0:T(8,128)(2,1)S(1)}, bf16[128,512]{1,0:T(8,128)(2,1)}, u32[]{:S(2)}) copy-start(bf16[128,512]{1,0:T(8,128)(2,1)} %c_ref.3) | copy-start | bytes 393220
  179.8 108.0 %all-to-all-start.2 = ((f16[128,64,128]{2,1,0:T(8,128)(2,1)}), f16[128,64,128]{2,1,0:T(8,128)(2,1)}, u32[]{:S(2)}, u32[]{:S(2)}) async-start(f16[128,64,128]{2,1,0:T(8,128)(2,1)} %convert_element_type.26), calls=%async_computation.2 | async-start | bytes 4194304 | tf_op jit(solution)/shard_map/all_to_all | solution.py:455
  187.9 0.7 copy-start.20
  188.6 0.6 copy-start.22
  189.4 1.0 copy-start.21
  190.3 0.8 copy-start.23
  199.2 1.4 copy-start.4
  200.6 1.4 copy-start.6
  202.0 0.7 copy-start.12
  202.7 0.7 copy-start.14
  203.4 0.7 copy-start.16
  204.1 0.7 copy-start.18
  287.8 2.3 copy-start.5
  287.8 2.9 copy-start.7
  287.8 2.9 copy-start.13
  287.8 2.9 copy-start.15
  287.8 3.0 %copy-start.17 = (f32[4,128,16]{2,1,0:T(8,128)S(1)}, f32[4,128,16]{2,1,0:T(8,128)}, u32[]{:S(2)}) copy-start(f32[4,128,16]{2,1,0:T(8,128)} %copy-done.16) | copy-start | bytes 98308
  287.8 3.1 %copy-start.19 = (f32[4,128,16]{2,1,0:T(8,128)S(1)}, f32[4,128,16]{2,1,0:T(8,128)}, u32[]{:S(2)}) copy-start(f32[4,128,16]{2,1,0:T(8,128)} %copy-done.18) | copy-start | bytes 98308

commit v8 on v7

--- a/solution.py
+++ b/solution.py
@@ -362,7 +362,7 @@
     columns = []
     for first in range(group * per_group, (group + 1) * per_group, fold):
         columns.append(jnp.concatenate([pay_ref[first + k, here] for k in range(fold)], axis=0))
-    return jnp.concatenate(columns, axis=1) * jnp.exp2(power - (TOP + 2.0 - BITS))
+    return jnp.concatenate(columns, axis=1), jnp.exp2(power - (TOP + 2.0 - BITS))
 
 
 def carried_terms(state, values, scale, proj):
@@ -386,12 +386,13 @@
     rows, cols, met, copies = [], [], [], []
     for g in range(GROUPS):
         mine, own = slice(g * wide, (g + 1) * wide), slice(g * STATE, (g + 1) * STATE)
-        enter, leave = state_from(pay_ref, most_ref, g, 0), state_from(pay_ref, most_ref, g, 1)
-        terms, grad, sums = carried_terms(enter, w_ref[:, mine].astype(F32), reach_ref[g], c_ref[:, own])
+        enter, enter_scale = state_from(pay_ref, most_ref, g, 0)
+        leave, leave_scale = state_from(pay_ref, most_ref, g, 1)
+        terms, grad, sums = carried_terms(enter, w_ref[:, mine].astype(F32), reach_ref[g] * enter_scale, c_ref[:, own])
         mixed_ref[:, mine] = (y_ref[:, mine] + terms).astype(BF16)
         gradc_ref[:, own] = (gc_ref[:, own] + grad).astype(BF16)
         rows.append(sums)
-        terms, grad, sums = carried_terms(leave, x_ref[:, mine].astype(F32), tail_ref[g], b_ref[:, own])
+        terms, grad, sums = carried_terms(leave, x_ref[:, mine].astype(F32), tail_ref[g] * leave_scale, b_ref[:, own])
         gradx_ref[:, mine] = (gx_ref[:, mine] + terms).astype(BF16)
         gradb_ref[:, own] = (gb_ref[:, own] + grad).astype(BF16)
         cols.append(sums)
@@ -406,7 +407,7 @@
             copy = pltpu.make_async_copy(source.at[:, here], target.at[:, here], sems.at[g, k])
             copy.start()
             copies.append(copy)
-        both = jnp.sum(enter * leave, axis=0, keepdims=True)
+        both = jnp.sum(enter * leave, axis=0, keepdims=True) * (enter_scale * leave_scale)
         met.append(head_sums(jnp.broadcast_to(both, (8, wide))))
 
     def whole(parts):
@@ -424,7 +425,7 @@
         + keep * whole(met)[0:1]
     )
     grad_size = (whole(col_ref) + late) / whole(size_ref) + decay * grad_rate
-    dt_ref[...] = (grad_size * whole(sig_ref)).astype(BF16)
+    dt_ref[...] = (grad_size * whole(sig_ref)).T.astype(BF16)
     for copy in copies:
         copy.wait()
 
@@ -432,7 +433,7 @@
 def finish(pay, most, x, w, b, c, tail, reach, y, gx, gb, gc, col, diff, size, sig, edge):
     tokens, channels = x.shape
     heads = channels // HEADDIM
-    shapes = [(tokens, channels), (tokens, channels), (tokens, heads), b.shape, b.shape]
+    shapes = [(tokens, channels), (tokens, channels), (heads, tokens), b.shape, b.shape]
     close = pl.BlockSpec(memory_space=pltpu.VMEM)
     far = pl.BlockSpec(memory_space=pl.ANY)
     return pl.pallas_call(
@@ -487,9 +488,10 @@
     came, total = lax.optimization_barrier((came, total))
     far = [lax.ppermute(total, "far", [(p, (p + by) % count) for p in range(count)]) for by in range(1, count)]
     left, most = entering(came.astype(F32), total, jnp.stack(far), mask)
-    return finish(
+    mixed, grad_x, grad_dt, grad_b, grad_c = finish(
         exchanged(left).astype(F32), most, features, cotangent, b_proj, c_proj, tail, reach, y, gx, gb, gc, col, diff, size, sig, edge
     )
+    return mixed, grad_x, grad_dt.T, grad_b, grad_c
 
 
 def solution(mesh):

time: 299 us -> 299 us (level)
  no operation moved by 1% of the time
where the time goes in v8:
time: 299 us; the launch traced here: 298 us
  waiting for transfers between devices  204 us (68%)
  starting transfers between devices  44.7 us (15%)
  Pallas kernels  20.9 us (7%)
  local copies, waits for them, and re-layouts  16.5 us (6%)
  other arithmetic  10.7 us (4%)
    all_to_all x2, waiting for transfers between devices, exchanged(): lax.all_to_all(messages.astype(jnp.float16), GROUP, split_axis=0, concat_...  195 us
    all_to_all x1, starting transfers between devices, gathered(): lax.all_to_all(whole, 'head', split_axis=0, concat_axis=0, tiled=True)  18.2 us
    all_to_all x2, starting transfers between devices, exchanged(): lax.all_to_all(messages.astype(jnp.float16), GROUP, split_axis=0, concat_...  16.3 us
    unnamed x49, local copies, waits for them, and re-layouts  14.5 us
    ppermute x3, starting transfers between devices, per_device(): lax.ppermute(total, 'far', [(p, (p + by) % count) for p in range(count)])  10.2 us
    pallas_call x1, Pallas kernels, inner(): pl.pallas_call(inner_kernel, grid=(GROUPS,), in_specs=[values, values, pr...  8.1 us
    all_to_all x1, waiting for transfers between devices, gathered(): lax.all_to_all(whole, 'head', split_axis=0, concat_axis=0, tiled=True)  7.45 us
    pallas_call x1, Pallas kernels, finish(): pl.pallas_call(finish_kernel, in_specs=[close] * 17, out_specs=[far, far,...  7.01 us
  transfers between devices with their start and end apart: 6, of which 4 were waited for; matrix products, arithmetic and copies ran while one was open for 1% of the time, Pallas kernels for 3%

profile of v8, /device:TPU:8, one launch (start us, length us, event | category | flops | bytes accessed | tf_op | source)
XLA Modules:
  0.0 298.0 jit_solution(1530411104021799427)
XLA Ops:
  0.7 0.9 stack.37
  1.6 0.1 copy.20
  1.7 0.1 fusion
  1.8 0.7 broadcast_in_dim.27
  2.5 18.2 %all-to-all-start = ((f32[16,8,128]{2,1,0:T(8,128)}), f32[16,8,128]{2,1,0:T(8,128)S(1)}, u32[]{:S(2)}, u32[]{:S(2)}) async-start(f32[16,8,128]{2,1,0:T(8,128)} %broadcast_in_dim.27), calls=%async_computation | async-start | bytes 131072 | tf_op jit(solution)/shard_map/all_to_all | solution.py:465
  20.7 0.8 copy.22.dt_ref
  21.5 1.2 copy-done
  22.7 1.2 copy-done.2
  24.0 0.9 copy-done.8
  24.9 0.9 copy-done.10
  25.8 0.2 staged.1
  25.9 0.8 dynamic-slice_convert_fusion
  26.7 7.5 %all-to-all-done = f32[16,8,128]{2,1,0:T(8,128)S(1)} async-done(((f32[16,8,128]{2,1,0:T(8,128)}), f32[16,8,128]{2,1,0:T(8,128)S(1)}, u32[]{:S(2)}, u32[]{:S(2)}) %all-to-all-start) | async-done | bytes 65568 | tf_op jit(solution)/shard_map/all_to_all | solution.py:465
  34.2 0.5 prep.2
  34.7 2.6 states.1
  37.3 1.7 convert_element_type.22
  39.0 8.7 %all-to-all-start.1 = ((f16[128,72,128]{2,1,0:T(8,128)(2,1)}), f16[128,72,128]{2,1,0:T(8,128)(2,1)}, u32[]{:S(2)}, u32[]{:S(2)}) async-start(f16[128,72,128]{2,1,0:T(8,128)(2,1)} %convert_element_type.22), calls=%async_computation.1 | async-start | bytes 4718592 | tf_op jit(solution)/shard_map/all_to_all | solution.py:456
  47.8 111.6 %all-to-all-done.1 = f16[128,72,128]{2,1,0:T(8,128)(2,1)} async-done(((f16[128,72,128]{2,1,0:T(8,128)(2,1)}), f16[128,72,128]{2,1,0:T(8,128)(2,1)}, u32[]{:S(2)}, u32[]{:S(2)}) %all-to-all-start.1) | async-done | bytes 2359328 | tf_op jit(solution)/shard_map/all_to_all | solution.py:456
  159.4 2.0 convert_element_type.23.pay_ref
  161.3 0.9 totals.1.own_ref
  162.3 4.7 %collective-permute-start.2 = (f32[2,40,128]{2,1,0:T(8,128)S(1)}, f32[2,40,128]{2,1,0:T(8,128)S(1)}, u32[]{:S(2)}, u32[]{:S(2)}) collective-permute-start(f32[2,40,128]{2,1,0:T(8,128)S(1)} %totals.1.own_ref), channel_id=1, source_target_pairs={{0,384},{128,0},{256,128},{384,256},{1,385},{129,1},{257,129},{385... | collective-permute-start | bytes 122888 | tf_op jit(solution)/shard_map/ppermute | solution.py:489
  166.9 2.7 collective-permute-start.1
  169.6 2.8 collective-permute-start
  172.6 2.0 convert_element_type.24.pay_ref
  174.6 2.1 collective-permute-done
  176.8 1.2 entering.1
  177.9 1.9 convert_element_type.26
  179.8 7.6 %all-to-all-start.2 = ((f16[128,64,128]{2,1,0:T(8,128)(2,1)}), f16[128,64,128]{2,1,0:T(8,128)(2,1)}, u32[]{:S(2)}, u32[]{:S(2)}) async-start(f16[128,64,128]{2,1,0:T(8,128)(2,1)} %convert_element_type.26), calls=%async_computation.2 | async-start | bytes 4194304 | tf_op jit(solution)/shard_map/all_to_all | solution.py:456
  187.4 0.4 prep.3
  187.9 0.7 copy-done.20
  188.6 0.6 copy-done.22
  189.2 0.1 broadcast_in_dim.29
  189.3 0.1 broadcast_in_dim.30
  189.4 0.9 copy-done.21
  190.3 0.8 copy-done.23
  191.1 8.1 %inner.1 = (f32[128,4096]{1,0:T(8,128)S(1)}, f32[128,4096]{1,0:T(8,128)S(1)}, f32[128,512]{1,0:T(8,128)S(1)}, f32[128,512]{1,0:T(8,128)S(1)}, f32[4,128,16]{2,1,0:T(8,128)S(1)}, /*index=5*/f32[4,128,16]{2,1,0:T(8,128)S(1)}) custom-call(bf16[128,4096]{1,0:T(8,128)(2,1)S(1)} %copy-done.1, bf16[128,4096]{1,0:T(8,128)(2,1)S(1)} %copy-done.3, ...), custom_call_target="tpu_custom_call" | custom-call | flops 20000000000 | bytes 8000000 | tf_op jit(solution)/shard_map/inner/pallas_call | solution.py:326
  199.2 1.4 copy-done.4
  200.6 1.4 copy-done.6
  202.0 0.7 copy-done.12
  202.7 0.7 copy-done.14
  203.4 0.7 copy-done.16
  204.1 0.7 copy-done.18
  204.8 83.0 %all-to-all-done.2 = f16[128,64,128]{2,1,0:T(8,128)(2,1)} async-done(((f16[128,64,128]{2,1,0:T(8,128)(2,1)}), f16[128,64,128]{2,1,0:T(8,128)(2,1)}, u32[]{:S(2)}, u32[]{:S(2)}) %all-to-all-start.2) | async-done | bytes 2097184 | tf_op jit(solution)/shard_map/all_to_all | solution.py:456
  287.8 2.2 convert_element_type.27.pay_ref
  290.1 0.6 copy-done.7
  290.7 0.1 copy-done.17
  290.8 0.1 copy-done.19
  290.9 7.0 %finish.1 = (bf16[128,4096]{1,0:T(8,128)(2,1)}, bf16[128,4096]{1,0:T(8,128)(2,1)}, bf16[64,128]{1,0:T(8,128)(2,1)}, bf16[128,512]{1,0:T(8,128)(2,1)}, bf16[128,512]{1,0:T(8,128)(2,1)}) custom-call(f32[128,64,128]{2,1,0:T(8,128)S(1)} %convert_element_type.27.pay_ref, f32[8,128]{1,0:T(8,128)S(1)} %get-tuple-element.42.most_ref, ...), custom_call_target="tpu_custom_call" | custom-call | flops 1342177280 | bytes 14000000 | tf_op jit(solution)/shard_map/finish/pallas_call | solution.py:439
  (51 shorter events, 0.4 us)
Async XLA Ops:
  2.5 31.7 %all-to-all-start = ((f32[16,8,128]{2,1,0:T(8,128)}), f32[16,8,128]{2,1,0:T(8,128)S(1)}, u32[]{:S(2)}, u32[]{:S(2)}) async-start(f32[16,8,128]{2,1,0:T(8,128)} %broadcast_in_dim.27), calls=%async_computation | async-start | bytes 131072 | tf_op jit(solution)/shard_map/all_to_all | solution.py:465
  21.5 1.2 copy-start
  22.7 1.2 copy-start.2
  24.0 0.9 copy-start.8
  24.9 0.9 copy-start.10
  39.0 120.3 %all-to-all-start.1 = ((f16[128,72,128]{2,1,0:T(8,128)(2,1)}), f16[128,72,128]{2,1,0:T(8,128)(2,1)}, u32[]{:S(2)}, u32[]{:S(2)}) async-start(f16[128,72,128]{2,1,0:T(8,128)(2,1)} %convert_element_type.22), calls=%async_computation.1 | async-start | bytes 4718592 | tf_op jit(solution)/shard_map/all_to_all | solution.py:456
  162.3 12.3 %collective-permute-start.2 = (f32[2,40,128]{2,1,0:T(8,128)S(1)}, f32[2,40,128]{2,1,0:T(8,128)S(1)}, u32[]{:S(2)}, u32[]{:S(2)}) collective-permute-start(f32[2,40,128]{2,1,0:T(8,128)S(1)} %totals.1.own_ref), channel_id=1, source_target_pairs={{0,384},{128,0},{256,128},{384,256},{1,385},{129,1},{257,129},{385... | collective-permute-start | bytes 122888 | tf_op jit(solution)/shard_map/ppermute | solution.py:489
  166.9 7.7 %collective-permute-start.1 = (f32[2,40,128]{2,1,0:T(8,128)S(1)}, f32[2,40,128]{2,1,0:T(8,128)S(1)}, u32[]{:S(2)}, u32[]{:S(2)}) collective-permute-start(f32[2,40,128]{2,1,0:T(8,128)S(1)} %totals.1.own_ref), channel_id=1, source_target_pairs={{0,256},{128,384},{256,0},{384,128},{1,257},{129,385},{257,1},{385... | collective-permute-start | bytes 122888 | tf_op jit(solution)/shard_map/ppermute | solution.py:489
  169.6 7.1 %collective-permute-start = (f32[2,40,128]{2,1,0:T(8,128)S(1)}, f32[2,40,128]{2,1,0:T(8,128)S(1)}, u32[]{:S(2)}, u32[]{:S(2)}) collective-permute-start(f32[2,40,128]{2,1,0:T(8,128)S(1)} %totals.1.own_ref), channel_id=1, source_target_pairs={{0,128},{128,256},{256,384},{384,0},{1,129},{129,257},{257,385},{3... | collective-permute-start | bytes 122888 | tf_op jit(solution)/shard_map/ppermute | solution.py:489
  179.8 9.5 %copy-start.1 = (bf16[128,4096]{1,0:T(8,128)(2,1)S(1)}, bf16[128,4096]{1,0:T(8,128)(2,1)}, u32[]{:S(2)}) copy-start(bf16[128,4096]{1,0:T(8,128)(2,1)} %x_ref.3) | copy-start | bytes 3145732
  179.8 9.6 %copy-start.3 = (bf16[128,4096]{1,0:T(8,128)(2,1)S(1)}, bf16[128,4096]{1,0:T(8,128)(2,1)}, u32[]{:S(2)}) copy-start(bf16[128,4096]{1,0:T(8,128)(2,1)} %w_ref.3) | copy-start | bytes 3145732
  179.8 9.6 %copy-start.9 = (bf16[128,512]{1,0:T(8,128)(2,1)S(1)}, bf16[128,512]{1,0:T(8,128)(2,1)}, u32[]{:S(2)}) copy-start(bf16[128,512]{1,0:T(8,128)(2,1)} %b_ref.3) | copy-start | bytes 393220
  179.8 9.6 %copy-start.11 = (bf16[128,512]{1,0:T(8,128)(2,1)S(1)}, bf16[128,512]{1,0:T(8,128)(2,1)}, u32[]{:S(2)}) copy-start(bf16[128,512]{1,0:T(8,128)(2,1)} %c_ref.3) | copy-start | bytes 393220
  179.8 108.0 %all-to-all-start.2 = ((f16[128,64,128]{2,1,0:T(8,128)(2,1)}), f16[128,64,128]{2,1,0:T(8,128)(2,1)}, u32[]{:S(2)}, u32[]{:S(2)}) async-start(f16[128,64,128]{2,1,0:T(8,128)(2,1)} %convert_element_type.26), calls=%async_computation.2 | async-start | bytes 4194304 | tf_op jit(solution)/shard_map/all_to_all | solution.py:456
  187.9 0.7 copy-start.20
  188.6 0.6 copy-start.22
  189.4 1.0 copy-start.21
  190.3 0.8 copy-start.23
  199.2 1.4 copy-start.4
  200.6 1.4 copy-start.6
  202.0 0.7 copy-start.12
  202.7 0.7 copy-start.14
  203.4 0.7 copy-start.16
  204.1 0.7 copy-start.18
  287.8 2.3 copy-start.5
  287.8 2.9 copy-start.7
  287.8 2.9 copy-start.13
  287.8 2.9 copy-start.15
  287.8 3.0 %copy-start.17 = (f32[4,128,16]{2,1,0:T(8,128)S(1)}, f32[4,128,16]{2,1,0:T(8,128)}, u32[]{:S(2)}) copy-start(f32[4,128,16]{2,1,0:T(8,128)} %copy-done.16) | copy-start | bytes 98308
  287.8 3.1 %copy-start.19 = (f32[4,128,16]{2,1,0:T(8,128)S(1)}, f32[4,128,16]{2,1,0:T(8,128)}, u32[]{:S(2)}) copy-start(f32[4,128,16]{2,1,0:T(8,128)} %copy-done.18) | copy-start | bytes 98308

commit v9 on v8

--- a/solution.py
+++ b/solution.py
@@ -158,6 +158,7 @@
             state = state_of(val_ref[:, mine], proj_ref[:, own], scale_ref[g])
             power = exponent_of(state)
             spread = jnp.where(row == 4 + which, power, spread)
+            spread = jnp.where((row == 6 + which) & (lane == which * GROUPS + g), 1.0, spread)
             all_powers = jnp.where(lane == which * GROUPS + g, power, all_powers)
             state = state * jnp.exp2(TOP - power)
             for k in range(per_group):
@@ -189,9 +190,8 @@
     return jnp.exp((side[0:1] + side[1:2] + side[2:3]) * (1.0 / 128.0))
 
 
-def lane_of(row, mask_ref, which):
-    mine = mask_ref[mask_ref.shape[0] - 2 + which : mask_ref.shape[0] - 1 + which]
-    return jnp.sum(row * mine, axis=1, keepdims=True)
+def lane_of(row, pay_ref, part, which):
+    return jnp.sum(row * pay_ref[0, 2 * part :][6 + which : 7 + which], axis=1, keepdims=True)
 
 
 def block_of(pay_ref, i, part, which):
@@ -249,7 +249,7 @@
             valid = mask_ref[which * others + by - 1 : which * others + by] > 0.0
             state = jnp.where(valid, far[0:part] + far[part : part + 1] * state, state)
         starts.append(state)
-        scales.append(jnp.exp2(TOP + 2.0 - BITS - lane_of(most[1:2], mask_ref, which)))
+        scales.append(jnp.exp2(TOP + 2.0 - BITS - lane_of(most[1:2], pay_ref, part, which)))
 
     def step(k, carry):
         forth, back = carry
@@ -478,11 +478,8 @@
     came = exchanged(states(*near, tail, reach, edge, parts))
     y, gx, gb, gc, col, diff = inner(features, cotangent, b_proj, c_proj, run, runt, bias, skip)
     count, here = lax.axis_size("far"), lax.axis_index("far")
-    group = lax.axis_index(GROUP) * GROUPS // parts
-    lane = jnp.arange(LANES)
     mask = [jnp.full((LANES,), here - by >= 0) for by in range(1, count)]
     mask += [jnp.full((LANES,), here + by < count) for by in range(1, count)]
-    mask += [lane == group, lane == GROUPS + group]
     mask = jnp.stack(mask).astype(F32)
     total = totals(came.astype(F32))
     came, total = lax.optimization_barrier((came, total))

time: 299 us -> 295 us (0.987)
  blocking collectives: 0 us -> 120 us
  waiting for transfers between devices: 204 us -> 92.6 us
  starting transfers between devices: 44.7 us -> 35.9 us
  other arithmetic: 10.7 us -> 7.62 us
    all_to_all x0 -> x1, blocking collectives: none -> 120 us  [exchanged(): lax.all_to_all(messages.astype(jnp.float16), GROUP, split_axis=0, concat_...]
    all_to_all x2 -> x1, waiting for transfers between devices: 195 us -> 82.9 us  [exchanged(): lax.all_to_all(messages.astype(jnp.float16), GROUP, split_axis=0, concat_...]
    all_to_all x2 -> x1, starting transfers between devices: 16.3 us -> 7.59 us  [exchanged(): lax.all_to_all(messages.astype(jnp.float16), GROUP, split_axis=0, concat_...]
    unnamed x49 -> x51, local copies, waits for them, and re-layouts: 14.5 us -> 14.6 us
  transfers between devices with their start and end apart: 6 -> 5, of which waited for: 4 -> 3; matrix products, arithmetic and copies ran while one was open for 1% -> 1% of each run, Pallas kernels for 3% -> 3%
where the time goes in v9:
time: 295 us
  blocking collectives  120 us (41%)
  waiting for transfers between devices  92.6 us (31%)
  starting transfers between devices  35.9 us (12%)
  Pallas kernels  20.9 us (7%)
  local copies, waits for them, and re-layouts  16.5 us (6%)
  other arithmetic  7.62 us (3%)
    all_to_all x1, blocking collectives, exchanged(): lax.all_to_all(messages.astype(jnp.float16), GROUP, split_axis=0, concat_...  120 us
    all_to_all x1, waiting for transfers between devices, exchanged(): lax.all_to_all(messages.astype(jnp.float16), GROUP, split_axis=0, concat_...  82.9 us
    all_to_all x1, starting transfers between devices, gathered(): lax.all_to_all(whole, 'head', split_axis=0, concat_axis=0, tiled=True)  18.2 us
    unnamed x51, local copies, waits for them, and re-layouts  14.6 us
    ppermute x3, starting transfers between devices, per_device(): lax.ppermute(total, 'far', [(p, (p + by) % count) for p in range(count)])  10.2 us
    pallas_call x1, Pallas kernels, inner(): pl.pallas_call(inner_kernel, grid=(GROUPS,), in_specs=[values, values, pr...  8.11 us
    all_to_all x1, starting transfers between devices, exchanged(): lax.all_to_all(messages.astype(jnp.float16), GROUP, split_axis=0, concat_...  7.59 us
    all_to_all x1, waiting for transfers between devices, gathered(): lax.all_to_all(whole, 'head', split_axis=0, concat_axis=0, tiled=True)  7.45 us
  transfers between devices with their start and end apart: 5, of which 3 were waited for; matrix products, arithmetic and copies ran while one was open for 1% of the time, Pallas kernels for 3%

profile of v9, /device:TPU:8, one launch (start us, length us, event | category | flops | bytes accessed | tf_op | source)
XLA Modules:
  0.0 294.6 jit_solution(15706554574129100309)
XLA Ops:
  0.7 0.9 stack.35
  1.6 0.1 copy.20
  1.7 0.1 fusion
  1.8 0.7 broadcast_in_dim.27
  2.5 18.2 %all-to-all-start = ((f32[16,8,128]{2,1,0:T(8,128)}), f32[16,8,128]{2,1,0:T(8,128)S(1)}, u32[]{:S(2)}, u32[]{:S(2)}) async-start(f32[16,8,128]{2,1,0:T(8,128)} %broadcast_in_dim.27), calls=%async_computation | async-start | bytes 131072 | tf_op jit(solution)/shard_map/all_to_all | solution.py:465
  20.7 0.8 copy.22.dt_ref
  21.5 1.2 copy-done
  22.7 1.2 copy-done.2
  24.0 0.9 copy-done.8
  24.9 0.9 copy-done.10
  25.8 0.2 staged.1
  25.9 0.8 dynamic-slice_convert_fusion
  26.7 7.5 %all-to-all-done = f32[16,8,128]{2,1,0:T(8,128)S(1)} async-done(((f32[16,8,128]{2,1,0:T(8,128)}), f32[16,8,128]{2,1,0:T(8,128)S(1)}, u32[]{:S(2)}, u32[]{:S(2)}) %all-to-all-start) | async-done | bytes 65568 | tf_op jit(solution)/shard_map/all_to_all | solution.py:465
  34.2 0.5 prep.2
  34.7 2.6 states.1
  37.3 0.3 convert_element_type.22
  37.6 120.0 %all_to_all.15 = f16[128,72,128]{2,1,0:T(8,128)(2,1)S(1)} all-to-all(f16[128,72,128]{2,1,0:T(8,128)(2,1)S(1)} %convert_element_type.22), channel_id=1, replica_groups=mesh['far'=4,'near'=8,'head'=16] {'near','head'}, dimensions={0} | all-to-all | bytes 4718592 | tf_op jit(solution)/shard_map/all_to_all | solution.py:456
  157.6 0.3 convert_element_type.23.pay_ref
  157.9 0.9 totals.1.own_ref
  158.8 4.7 %collective-permute-start.2 = (f32[2,40,128]{2,1,0:T(8,128)S(1)}, f32[2,40,128]{2,1,0:T(8,128)S(1)}, u32[]{:S(2)}, u32[]{:S(2)}) collective-permute-start(f32[2,40,128]{2,1,0:T(8,128)S(1)} %totals.1.own_ref), channel_id=1, source_target_pairs={{0,384},{128,0},{256,128},{384,256},{1,385},{129,1},{257,129},{385... | collective-permute-start | bytes 122888 | tf_op jit(solution)/shard_map/ppermute | solution.py:486
  163.5 2.7 collective-permute-start.1
  166.2 2.8 collective-permute-start
  169.2 2.0 convert_element_type.24.pay_ref
  171.2 2.2 collective-permute-done
  173.4 1.2 entering.1
  174.5 1.9 convert_element_type.26
  176.4 7.6 %all-to-all-start.2 = ((f16[128,64,128]{2,1,0:T(8,128)(2,1)}), f16[128,64,128]{2,1,0:T(8,128)(2,1)}, u32[]{:S(2)}, u32[]{:S(2)}) async-start(f16[128,64,128]{2,1,0:T(8,128)(2,1)} %convert_element_type.26), calls=%async_computation.2 | async-start | bytes 4194304 | tf_op jit(solution)/shard_map/all_to_all | solution.py:456
  184.0 0.4 prep.3
  184.5 0.7 copy-done.20
  185.2 0.6 copy-done.22
  185.8 0.1 broadcast_in_dim.29
  185.9 0.1 broadcast_in_dim.30
  186.0 0.9 copy-done.21
  186.9 0.8 copy-done.23
  187.7 8.1 %inner.1 = (f32[128,4096]{1,0:T(8,128)S(1)}, f32[128,4096]{1,0:T(8,128)S(1)}, f32[128,512]{1,0:T(8,128)S(1)}, f32[128,512]{1,0:T(8,128)S(1)}, f32[4,128,16]{2,1,0:T(8,128)S(1)}, /*index=5*/f32[4,128,16]{2,1,0:T(8,128)S(1)}) custom-call(bf16[128,4096]{1,0:T(8,128)(2,1)S(1)} %copy-done.1, bf16[128,4096]{1,0:T(8,128)(2,1)S(1)} %copy-done.3, ...), custom_call_target="tpu_custom_call" | custom-call | flops 20000000000 | bytes 8000000 | tf_op jit(solution)/shard_map/inner/pallas_call | solution.py:326
  195.8 1.4 copy-done.4
  197.2 1.4 copy-done.6
  198.6 0.7 copy-done.12
  199.3 0.7 copy-done.14
  200.0 0.7 copy-done.16
  200.7 0.7 copy-done.18
  201.5 82.9 %all-to-all-done.2 = f16[128,64,128]{2,1,0:T(8,128)(2,1)} async-done(((f16[128,64,128]{2,1,0:T(8,128)(2,1)}), f16[128,64,128]{2,1,0:T(8,128)(2,1)}, u32[]{:S(2)}, u32[]{:S(2)}) %all-to-all-start.2) | async-done | bytes 2097184 | tf_op jit(solution)/shard_map/all_to_all | solution.py:456
  284.4 2.2 convert_element_type.27.pay_ref
  286.7 0.6 copy-done.7
  287.3 0.1 copy-done.15
  287.3 0.1 copy-done.17
  287.4 0.1 copy-done.19
  287.5 7.0 %finish.1 = (bf16[128,4096]{1,0:T(8,128)(2,1)}, bf16[128,4096]{1,0:T(8,128)(2,1)}, bf16[64,128]{1,0:T(8,128)(2,1)}, bf16[128,512]{1,0:T(8,128)(2,1)}, bf16[128,512]{1,0:T(8,128)(2,1)}) custom-call(f32[128,64,128]{2,1,0:T(8,128)S(1)} %convert_element_type.27.pay_ref, f32[8,128]{1,0:T(8,128)S(1)} %get-tuple-element.42.most_ref, ...), custom_call_target="tpu_custom_call" | custom-call | flops 1342177280 | bytes 14000000 | tf_op jit(solution)/shard_map/finish/pallas_call | solution.py:439
  (51 shorter events, 0.3 us)
Async XLA Ops:
  2.5 31.7 %all-to-all-start = ((f32[16,8,128]{2,1,0:T(8,128)}), f32[16,8,128]{2,1,0:T(8,128)S(1)}, u32[]{:S(2)}, u32[]{:S(2)}) async-start(f32[16,8,128]{2,1,0:T(8,128)} %broadcast_in_dim.27), calls=%async_computation | async-start | bytes 131072 | tf_op jit(solution)/shard_map/all_to_all | solution.py:465
  21.5 1.2 copy-start
  22.7 1.2 copy-start.2
  24.0 0.9 copy-start.8
  24.9 0.9 copy-start.10
  157.6 5.9 %copy-start.24 = (f16[128,72,128]{2,1,0:T(8,128)(2,1)}, f16[128,72,128]{2,1,0:T(8,128)(2,1)S(1)}, u32[]{:S(2)}) copy-start(f16[128,72,128]{2,1,0:T(8,128)(2,1)S(1)} %all_to_all.15) | copy-start | bytes 7077892
  158.8 12.3 %collective-permute-start.2 = (f32[2,40,128]{2,1,0:T(8,128)S(1)}, f32[2,40,128]{2,1,0:T(8,128)S(1)}, u32[]{:S(2)}, u32[]{:S(2)}) collective-permute-start(f32[2,40,128]{2,1,0:T(8,128)S(1)} %totals.1.own_ref), channel_id=1, source_target_pairs={{0,384},{128,0},{256,128},{384,256},{1,385},{129,1},{257,129},{385... | collective-permute-start | bytes 122888 | tf_op jit(solution)/shard_map/ppermute | solution.py:486
  163.5 7.7 %collective-permute-start.1 = (f32[2,40,128]{2,1,0:T(8,128)S(1)}, f32[2,40,128]{2,1,0:T(8,128)S(1)}, u32[]{:S(2)}, u32[]{:S(2)}) collective-permute-start(f32[2,40,128]{2,1,0:T(8,128)S(1)} %totals.1.own_ref), channel_id=1, source_target_pairs={{0,256},{128,384},{256,0},{384,128},{1,257},{129,385},{257,1},{385... | collective-permute-start | bytes 122888 | tf_op jit(solution)/shard_map/ppermute | solution.py:486
  166.2 7.1 %collective-permute-start = (f32[2,40,128]{2,1,0:T(8,128)S(1)}, f32[2,40,128]{2,1,0:T(8,128)S(1)}, u32[]{:S(2)}, u32[]{:S(2)}) collective-permute-start(f32[2,40,128]{2,1,0:T(8,128)S(1)} %totals.1.own_ref), channel_id=1, source_target_pairs={{0,128},{128,256},{256,384},{384,0},{1,129},{129,257},{257,385},{3... | collective-permute-start | bytes 122888 | tf_op jit(solution)/shard_map/ppermute | solution.py:486
  176.4 9.5 %copy-start.1 = (bf16[128,4096]{1,0:T(8,128)(2,1)S(1)}, bf16[128,4096]{1,0:T(8,128)(2,1)}, u32[]{:S(2)}) copy-start(bf16[128,4096]{1,0:T(8,128)(2,1)} %x_ref.3) | copy-start | bytes 3145732
  176.4 9.6 %copy-start.3 = (bf16[128,4096]{1,0:T(8,128)(2,1)S(1)}, bf16[128,4096]{1,0:T(8,128)(2,1)}, u32[]{:S(2)}) copy-start(bf16[128,4096]{1,0:T(8,128)(2,1)} %w_ref.3) | copy-start | bytes 3145732
  176.4 9.6 %copy-start.9 = (bf16[128,512]{1,0:T(8,128)(2,1)S(1)}, bf16[128,512]{1,0:T(8,128)(2,1)}, u32[]{:S(2)}) copy-start(bf16[128,512]{1,0:T(8,128)(2,1)} %b_ref.3) | copy-start | bytes 393220
  176.4 9.6 %copy-start.11 = (bf16[128,512]{1,0:T(8,128)(2,1)S(1)}, bf16[128,512]{1,0:T(8,128)(2,1)}, u32[]{:S(2)}) copy-start(bf16[128,512]{1,0:T(8,128)(2,1)} %c_ref.3) | copy-start | bytes 393220
  176.4 108.0 %all-to-all-start.2 = ((f16[128,64,128]{2,1,0:T(8,128)(2,1)}), f16[128,64,128]{2,1,0:T(8,128)(2,1)}, u32[]{:S(2)}, u32[]{:S(2)}) async-start(f16[128,64,128]{2,1,0:T(8,128)(2,1)} %convert_element_type.26), calls=%async_computation.2 | async-start | bytes 4194304 | tf_op jit(solution)/shard_map/all_to_all | solution.py:456
  184.5 0.7 copy-start.20
  185.2 0.6 copy-start.22
  186.0 1.0 copy-start.21
  186.9 0.8 copy-start.23
  195.8 1.4 copy-start.4
  197.2 1.4 copy-start.6
  198.6 0.7 copy-start.12
  199.3 0.7 copy-start.14
  200.0 0.7 copy-start.16
  200.7 0.7 copy-start.18
  284.4 2.3 copy-start.5
  284.4 2.9 copy-start.7
  284.4 2.9 copy-start.13
  284.4 2.9 copy-start.15
  284.4 3.0 %copy-start.17 = (f32[4,128,16]{2,1,0:T(8,128)S(1)}, f32[4,128,16]{2,1,0:T(8,128)}, u32[]{:S(2)}) copy-start(f32[4,128,16]{2,1,0:T(8,128)} %copy-done.16) | copy-start | bytes 98308
  284.4 3.1 %copy-start.19 = (f32[4,128,16]{2,1,0:T(8,128)S(1)}, f32[4,128,16]{2,1,0:T(8,128)}, u32[]{:S(2)}) copy-start(f32[4,128,16]{2,1,0:T(8,128)} %copy-done.18) | copy-start | bytes 98308
